TPU v7x, 256 devices: a whole 4x4x8 slice. The times are simulated.
256 devices in a mesh: rep: 32 (over x, z), shard: 8 (over y, core).
Axes of the slice: x: 4, y: 4, z: 8, core: 2. Of those that a mesh axis runs over, the one named last changes fastest.
Arguments:
- gradient: bfloat16 [32, 2, 3072, 3072], P('rep', None, 'shard')
- error_buffer: bfloat16 [32, 2, 3072, 3072], P('rep', None, 'shard'), may hold values from -4 to 4
- previous_q: float32 [2, 3072, 32], replicated, may hold values from -0.109375 to 0.109375
- run_starts: int32 [32], replicated, may hold values from 0 to 2952, as said below
- run_owners: int32 [32], replicated, may hold values from 0 to 7, as said below
Outputs:
- left_factor: float32 [2, 3072, 32], P(None, 'shard')
- right_factor: float32 [2, 3072, 32], replicated
Inputs may be any that keep to these rules, and one draw needn't show every extreme that they name: `run_starts`: Rising; the runs of device i's flat shard of rows are entries 4 * i to 4 * i + 3, the first starting at row i * 384; every run is a positive multiple of 24 rows long, and every shard is cut into the same four run lengths in some order, one of them 120 rows; the last run is 120 rows long. `run_owners`: the four runs of one shard go to four different owners; every owner receives 384 rows in all and at most 120 rows from one shard.
All inputs are finite; a program needn't handle non-finite values.
Results may differ from a plain program's by a relative error of at most 0.0045.
Values sent between devices are 32-bit elements; how exact they have to be, the bound alone decides.
No kernel may reach another device: no remote copies, remote signals or barrier semaphores. Data moves between devices by JAX's collectives and lax.ppermute only.
A program may use at most 64 MiB of HBM per device.

v0:
```python
import math

import jax
import jax.numpy as jnp
from jax import lax
from jax.sharding import PartitionSpec as P


def orthonormal(factor, gram_matrix):
    cholesky_factor = jnp.linalg.cholesky(gram_matrix)

    def solve_one(triangle, right_side):
        return jax.scipy.linalg.solve_triangular(triangle, right_side, lower=True)

    solved = jax.vmap(solve_one)(cholesky_factor, jnp.swapaxes(factor, 1, 2))
    return jnp.swapaxes(solved, 1, 2)


def send_to_owners(scaled, run_starts, run_owners, total_rows):
    shard_count = lax.axis_size("shard")
    owner_index = lax.axis_index("shard")
    layer_count, row_count, rank_width = scaled.shape
    capacity = 5 * (row_count // 16)
    packed = jnp.moveaxis(scaled, 0, 1).reshape(row_count, layer_count * rank_width)
    packed_width = packed.shape[1]
    padded = jnp.concatenate([packed, jnp.zeros((capacity, packed_width), jnp.float32)], 0)
    run_ends = jnp.concatenate([run_starts[1:], jnp.full((1,), total_rows, jnp.int32)])
    run_lengths = run_ends - run_starts
    first_run = owner_index * 4
    local_starts = lax.dynamic_slice_in_dim(run_starts, first_run, 4) - owner_index * row_count
    local_lengths = lax.dynamic_slice_in_dim(run_lengths, first_run, 4)
    local_owners = lax.dynamic_slice_in_dim(run_owners, first_run, 4)
    offsets = jnp.arange(capacity, dtype=jnp.int32)
    pieces = []
    for run_index in range(4):
        run_piece = lax.dynamic_slice_in_dim(padded, local_starts[run_index], capacity, 0)
        pieces.append(jnp.where((offsets < local_lengths[run_index])[:, None], run_piece, 0.0))
    stacked = jnp.stack(pieces)
    targets = (local_owners[None, :] == jnp.arange(shard_count, dtype=jnp.int32)[:, None]).astype(
        jnp.float32
    )
    outgoing = jnp.einsum("dj,jcw->dcw", targets, stacked, precision=lax.Precision.HIGHEST)
    incoming = lax.all_to_all(outgoing, "shard", split_axis=0, concat_axis=0, tiled=True)
    counts = jnp.sum(
        jnp.where(
            run_owners.reshape(shard_count, 4) == owner_index,
            run_lengths.reshape(shard_count, 4),
            0,
        ),
        axis=1,
    )
    block_starts = jnp.cumsum(counts) - counts

    def place_rows(source, gathered):
        arrived = lax.dynamic_index_in_dim(incoming, source, 0, keepdims=False)
        return lax.dynamic_update_slice_in_dim(gathered, arrived, block_starts[source], 0)

    gathered = lax.fori_loop(
        0, shard_count, place_rows, jnp.zeros((row_count + capacity, packed_width), jnp.float32)
    )
    return jnp.moveaxis(gathered[:row_count].reshape(row_count, layer_count, rank_width), 1, 0)


def compress(matrices, q_low, run_starts, run_owners, total_rows):
    factor_local = jnp.einsum("lrc,lck->lrk", matrices, q_low, preferred_element_type=jnp.float32)
    factor_sum = lax.psum(factor_local, "rep")
    gram_local = jnp.einsum("lrk,lrj->lkj", factor_sum, factor_sum, precision=lax.Precision.HIGHEST)
    gram_matrix = lax.psum(gram_local, "shard")
    own_basis = orthonormal(factor_sum, gram_matrix)
    left_part = send_to_owners(
        own_basis * math.sqrt(total_rows), run_starts, run_owners, total_rows
    )
    right_local = jnp.einsum(
        "lrc,lrk->lck", matrices, own_basis.astype(jnp.bfloat16), preferred_element_type=jnp.float32
    )
    right_part = lax.psum(right_local, ("rep", "shard"))
    return (left_part, right_part)


def shards(gradient, error_buffer, previous_q, run_starts, run_owners):
    matrices = (gradient[0].astype(jnp.float32) + error_buffer[0].astype(jnp.float32)).astype(
        jnp.bfloat16
    )
    q_low = previous_q.astype(jnp.bfloat16)
    total_rows = matrices.shape[1] * lax.axis_size("shard")
    left_parts = []
    right_parts = []
    for layer_index in range(matrices.shape[0]):
        left_part, right_part = compress(
            matrices[layer_index : layer_index + 1],
            q_low[layer_index : layer_index + 1],
            run_starts,
            run_owners,
            total_rows,
        )
        left_parts.append(left_part)
        right_parts.append(right_part)
    return (jnp.concatenate(left_parts, 0), jnp.concatenate(right_parts, 0))


def solution(mesh):
    return jax.shard_map(
        shards,
        mesh=mesh,
        in_specs=(P("rep", None, "shard", None), P("rep", None, "shard", None), P(), P(), P()),
        out_specs=(P(None, "shard", None), P()),
        check_vma=False,
    )
```

profile of v0, /device:TPU:1, one launch (start us, length us, event | category | flops | bytes accessed | tf_op | source)
XLA Modules:
  0.0 481.6 jit_solution(1498098431245569897)
XLA Ops:
  7.2 1.2 convert_element_type.32
  8.4 5.7 %add_convert_fusion = bf16[1,2,384,3072]{3,2,1,0:T(8,128)(2,1)S(1)} fusion(bf16[1,2,384,3072]{3,2,1,0:T(8,128)(2,1)} %param.13, bf16[1,2,384,3072]{3,2,1,0:T(8,128)(2,1)} %param.12), kind=kLoop, calls=%fused_computation.2 | loop fusion | flops 9437184 | bytes 14155776 | tf_op jit(solution)/shard_map/convert_element_type | solution.py:81
  14.1 1.9 fusion.2
  16.2 1.4 fusion.3
  17.8 0.7 fusion.44
  23.8 0.7 fusion.43
  27.4 1.2 iota_compare_fusion.3
  28.6 1.4 iota_compare_fusion.5
  30.0 128.3 %all-reduce.10.cloned.1.call-done = (f32[1,384,32]{1,2,0:T(8,128)}, f32[1,384,32]{1,2,0:T(8,128)}) async-done(((f32[1,384,32]{1,2,0:T(8,128)}, f32[1,384,32]{1,2,0:T(8,128)}), (f32[1,384,32]{1,2,0:T(8,128)}, f32[1,384,32]{1,2,0:T(8,128)})) %all-reduce.10.cloned.1.call-update) | async-done | bytes 98320 | tf_op jit(solution)/shard_map/psum | solution.py:66
  158.2 1.1 convolution_bitcast_fusion.4
  159.3 1.1 convolution_bitcast_fusion.5
  160.4 25.2 %all-reduce.4 = (f32[1,32,32]{1,2,0:T(8,128)S(1)}, f32[1,32,32]{1,2,0:T(8,128)S(1)}) all-reduce(f32[1,32,32]{1,2,0:T(8,128)S(1)} %convolution_bitcast_fusion.4, f32[1,32,32]{1,2,0:T(8,128)S(1)} %convolution_bitcast_fusion.5), channel_id=1, replica_groups=mesh['rep'=32,'shard'=8] {'shard'}, use_global_device_ids=true, to_apply=%region_9.12 | all-reduce | flops 2048 | bytes 16384 | tf_op jit(solution)/shard_map/psum | solution.py:68
  185.7 2.9 custom-call.8
  188.7 0.6 compare_reduce_fusion.1
  189.3 0.7 fusion.16
  190.0 2.4 custom-call.9
  192.4 1.1 convolution_bitcast_fusion.3
  193.5 2.9 convolution_bitcast_fusion.1
  196.5 2.9 custom-call.10
  199.4 0.6 compare_reduce_fusion
  200.1 0.7 fusion.17
  200.7 2.4 custom-call.11
  203.1 1.1 convolution_bitcast_fusion.2
  204.2 2.9 convolution_bitcast_fusion
  207.6 0.7 copy.30
  208.3 6.8 %all-to-all-start = ((f32[8,120,32]{1,2,0:T(8,128)}), f32[8,120,32]{1,2,0:T(8,128)S(1)}, u32[]{:S(2)}, u32[]{:S(2)}) async-start(f32[8,120,32]{1,2,0:T(8,128)} %copy.30), calls=%async_computation | async-start | bytes 262144 | tf_op jit(solution)/shard_map/all_to_all | solution.py:43
  215.5 0.7 copy.36
  216.2 4.2 all-to-all-done
  220.4 4.1 all-to-all-start.1
  224.6 23.9 %while.26 = (s32[]{:T(128)}, f32[504,32]{0,1:T(8,128)S(1)}, f32[8,120,32]{1,2,0:T(8,128)S(1)}, s32[8]{0:T(128)S(1)}, s32[]{:T(128)}, /*index=5*/s32[]{:T(128)}, s32[]{:T(128)}) while((s32[]{:T(128)}, f32[504,32]{0,1:T(8,128)S(1)}, f32[8,120,32]{1,2,0:T(8,128)S(1)}, s32[8]{0:T(128)S(1)}, s32[]{:T(128)}, /*index=5*/s32[]{:T(128)}, ...), condition=%wide.region_7.10_spmd, body=%wide.region_6.9_spmd.sunk | while | flops 5 | bytes 61571 | solution.py:58
  224.6 0.6 dynamic_slice.124
  227.5 0.6 dynamic_slice.124
  230.4 0.6 dynamic_slice.124
  233.3 0.6 dynamic_slice.124
  236.3 0.6 dynamic_slice.124
  239.4 0.6 dynamic_slice.124
  242.4 0.6 dynamic_slice.124
  245.4 0.6 dynamic_slice.124
  248.5 23.9 %while.27 = (s32[]{:T(128)}, f32[504,32]{0,1:T(8,128)S(1)}, f32[8,120,32]{1,2,0:T(8,128)S(1)}, s32[8]{0:T(128)S(1)}, s32[]{:T(128)}, /*index=5*/s32[]{:T(128)}, s32[]{:T(128)}) while((s32[]{:T(128)}, f32[504,32]{0,1:T(8,128)S(1)}, f32[8,120,32]{1,2,0:T(8,128)S(1)}, s32[8]{0:T(128)S(1)}, s32[]{:T(128)}, /*index=5*/s32[]{:T(128)}, ...), condition=%wide.region_11.14_spmd, body=%wide.region_10.13_spmd.sunk | while | flops 5 | bytes 61571 | solution.py:58
  248.5 0.6 dynamic_slice.126
  251.4 0.6 dynamic_slice.126
  257.2 0.6 dynamic_slice.126
  260.2 0.6 dynamic_slice.126
  263.3 0.6 dynamic_slice.126
  269.3 0.6 dynamic_slice.126
  272.3 0.6 pad_maximum_fusion.1
  273.0 199.7 %all-reduce.8.cloned.1.call-done = (f32[1,3072,32]{1,2,0:T(8,128)}, f32[1,3072,32]{1,2,0:T(8,128)}) async-done(((f32[1,3072,32]{1,2,0:T(8,128)}, f32[1,3072,32]{1,2,0:T(8,128)}), (f32[1,3072,32]{1,2,0:T(8,128)}, f32[1,3072,32]{1,2,0:T(8,128)})) %all-reduce.8.cloned.1.call-update) | async-done | bytes 786448 | tf_op jit(solution)/shard_map/psum | solution.py:76
  472.7 2.0 pad_maximum_fusion
  (70 shorter events, 10.0 us)
Async XLA Ops:
  7.2 151.1 %all-reduce.10.cloned.1.call-start = ((), (), s32[]{:S(2)}) async-start(), calls=%async_computation.3 | async-start | bytes 196608 | tf_op jit(solution)/shard_map/psum | solution.py:66
  14.1 2.1 copy-start
  14.1 3.6 copy-start.1
  14.1 9.4 %copy-start.2 = (s32[32]{0:T(128)S(1)}, s32[32]{0:T(128)}, u32[]{:S(2)}) copy-start(s32[32]{0:T(128)} %param.16) | copy-start | bytes 388
  208.3 12.1 %all-to-all-start = ((f32[8,120,32]{1,2,0:T(8,128)}), f32[8,120,32]{1,2,0:T(8,128)S(1)}, u32[]{:S(2)}, u32[]{:S(2)}) async-start(f32[8,120,32]{1,2,0:T(8,128)} %copy.30), calls=%async_computation | async-start | bytes 262144 | tf_op jit(solution)/shard_map/all_to_all | solution.py:43
  215.1 257.6 %all-reduce.8.cloned.1.call-start = ((), (), s32[]{:S(2)}) async-start(), calls=%async_computation.2 | async-start | bytes 1572864 | tf_op jit(solution)/shard_map/psum | solution.py:76
  220.4 28.0 %all-to-all-start.1 = ((f32[8,120,32]{1,2,0:T(8,128)}), f32[8,120,32]{1,2,0:T(8,128)S(1)}, u32[]{:S(2)}, u32[]{:S(2)}) async-start(f32[8,120,32]{1,2,0:T(8,128)} %copy.36), calls=%async_computation.1 | async-start | bytes 262144 | tf_op jit(solution)/shard_map/all_to_all | solution.py:43
Sparse Core Ops, SparseCore 0:
  17.8 140.3 all-reduce.9
  222.2 250.4 all-reduce.7
where the time goes:
time: 484 us; the launch traced here: 482 us
  waiting for transfers between devices  332 us (69%)
  loops' own time  31.6 us (7%)
  other arithmetic  26.1 us (5%)
  blocking collectives  25.2 us (5%)
  between operations  21.8 us (5%)
  local copies, waits for them, and re-layouts  19.5 us (4%)
  matrix products  14.1 us (3%)
  starting transfers between devices  11 us (2%)
    psum x1, waiting for transfers between devices, compress(): right_part = lax.psum(right_local, ('rep', 'shard'))  200 us
    psum x1, waiting for transfers between devices, compress(): factor_sum = lax.psum(factor_local, 'rep')  128 us
    another operation x2, loops' own time, send_to_owners(): lax.fori_loop(0, shard_count, place_rows, jnp.zeros((row_count + capacity...  31.6 us
    psum x1, blocking collectives, compress(): gram_matrix = lax.psum(gram_local, 'shard')  25.2 us
    all_to_all x2, starting transfers between devices, send_to_owners(): lax.all_to_all(outgoing, 'shard', split_axis=0, concat_axis=0, tiled=True)  10.9 us
  transfers between devices with their start and end apart: 4, of which 3 were waited for; matrix products, arithmetic and copies ran while one was open for 5% of the time, Pallas kernels for 0%

commit v1 on v0

v1 whole, which is shorter than its diff:
```python
import functools
import math

import jax
import jax.numpy as jnp
from jax import lax
from jax.experimental import pallas as pl
from jax.experimental.pallas import tpu as pltpu
from jax.sharding import PartitionSpec as P

LAYERS = 2
RANK = 32
ROWS = 384
COLS = 3072
HALF = COLS // 2
REP = 32
YS = 4
BLOCKS = ROWS // 128
ROW_TILES = LAYERS * RANK // 8
TILES = ROW_TILES * BLOCKS
LEFT, GRAM, SCALE, SLOTS = TILES, TILES + 1, TILES + 3, TILES + 4
VMEM_LIMIT = 40 * 1024 * 1024
F32 = jnp.float32
BF16 = jnp.bfloat16


def whole(memory_space=pltpu.VMEM):
    return pl.BlockSpec(memory_space=memory_space)


def params(**more):
    return pltpu.CompilerParams(vmem_limit_bytes=VMEM_LIMIT, **more)


def split3(value):
    high = value.astype(BF16)
    rest = value - high.astype(F32)
    middle = rest.astype(BF16)
    low = (rest - middle.astype(F32)).astype(BF16)
    return high, middle, low


def dot_rows(left, right):
    return lax.dot_general(left, right, (((1,), (1,)), ((), ())), preferred_element_type=F32)


def merge_kernel(gradient, error, q, merged, partial):
    layer, block = pl.program_id(0), pl.program_id(1)
    total = (gradient[0, 0].astype(F32) + error[0, 0].astype(F32)).astype(BF16)
    merged[0] = total
    terms = dot_rows(q[0].astype(BF16), total)
    for part in range(RANK // 8):
        partial[(layer * (RANK // 8) + part) * BLOCKS + block] = terms[part * 8 : part * 8 + 8]

    @pl.when((layer == 0) & (block == 0))
    def _():
        partial[TILES:] = jnp.zeros((REP - TILES, 8, 128), F32)


def merge(gradient, error, q):
    block = pl.BlockSpec((1, 1, 128, COLS), lambda l, b: (0, l, b, 0))
    return pl.pallas_call(
        merge_kernel,
        grid=(LAYERS, BLOCKS),
        in_specs=[block, block, pl.BlockSpec((1, RANK, COLS), lambda l, b: (l, 0, 0))],
        out_specs=[
            pl.BlockSpec((1, 128, COLS), lambda l, b: (l, b, 0)),
            pl.BlockSpec((REP, 8, 128), lambda l, b: (0, 0, 0)),
        ],
        out_shape=[
            jax.ShapeDtypeStruct((LAYERS, ROWS, COLS), BF16),
            jax.ShapeDtypeStruct((REP, 8, 128), F32),
        ],
        compiler_params=params(),
        name="merge_project",
    )(gradient, error, q)


def rows_of(tiles):
    return jnp.concatenate(
        [
            jnp.concatenate([tiles[row * BLOCKS + block] for block in range(BLOCKS)], axis=1)
            for row in range(ROW_TILES)
        ],
        axis=0,
    )


def product_kernel(with_extras, place, dest, tiles, merged, out):
    rep, half = place[0], place[3]
    factor = rows_of(tiles)
    biggest = [
        jnp.max(jnp.abs(factor[l * RANK : l * RANK + RANK]), keepdims=True) for l in range(LAYERS)
    ]
    scales = [jnp.where(b > 0, b * 64.0, 1.0) for b in biggest]
    for layer in range(LAYERS):
        scaled = factor[layer * RANK : layer * RANK + RANK] * (1.0 / scales[layer])
        parts = jnp.concatenate(split3(scaled), axis=0)
        for y in range(YS):
            first = pl.multiple_of(half * HALF + y * ROWS, 128)
            product = jnp.dot(
                parts, merged[layer, :, pl.ds(first, ROWS)], preferred_element_type=F32
            )
            product = product[:RANK] + product[RANK : 2 * RANK] + product[2 * RANK :]
            for part in range(RANK // 8):
                for block in range(BLOCKS):
                    out[y, (layer * (RANK // 8) + part) * BLOCKS + block] = product[
                        part * 8 : part * 8 + 8, block * 128 : block * 128 + 128
                    ]
    tile = jnp.minimum(rep, TILES - 1)
    row_tile = tile // BLOCKS
    column = (tile - row_tile * BLOCKS) * 128
    rows = jnp.concatenate([tiles[row_tile * BLOCKS + block] for block in range(BLOCKS)], axis=1)
    rows = jnp.concatenate(split3(rows), axis=0)
    wanted = jnp.broadcast_to(dest[0:1], (128, ROWS)) - lax.broadcasted_iota(
        jnp.int32, (128, ROWS), 0
    )
    for y in range(YS):
        base = (y * 2 + half) * ROWS + column
        chosen = jnp.where(wanted == base, 1.0, 0.0).astype(BF16)
        found = dot_rows(rows, chosen)
        out[y, LEFT] = found[:8] + found[8:16] + found[16:]
    high, middle, low = split3(factor)
    left = jnp.concatenate([high, middle, low], axis=0)
    right = jnp.concatenate([high, high, middle, middle, low, low], axis=0)
    gram = dot_rows(left, right)
    gram = gram[:64] + gram[64:128] + gram[128:]
    gram = gram[:, :128] + gram[:, 128:256] + gram[:, 256:]
    lane = lax.broadcasted_iota(jnp.int32, (RANK, 128), 1)
    gram = jnp.where(lax.rem(lane, 64) < 32, gram[:RANK], gram[RANK:])
    gram = jnp.where(lane[:16] < 64, gram[:16], gram[16:])
    scale = jnp.concatenate([jnp.broadcast_to(s, (4, 128)) for s in scales], axis=0)
    for y in range(YS):
        out[y, GRAM] = gram[:8]
        out[y, GRAM + 1] = gram[8:]
        out[y, SCALE] = scale


def product(place, dest, tiles, merged, name):
    return pl.pallas_call(
        functools.partial(product_kernel, True),
        in_specs=[whole(pltpu.SMEM), whole(), whole(), whole()],
        out_specs=whole(),
        out_shape=jax.ShapeDtypeStruct((YS, SLOTS, 8, 128), F32),
        compiler_params=params(),
        name=name,
    )(place, dest, tiles, merged)


def add_scaled(pieces):
    largest = functools.reduce(jnp.maximum, [p[SCALE] for p in pieces])
    ratios = [p[SCALE] / largest for p in pieces]
    out = []
    for slot in range(SLOTS):
        if slot == SCALE:
            out.append(largest)
        elif slot < TILES:
            row = 0 if slot < TILES // 2 else 4
            out.append(
                functools.reduce(
                    jnp.add, [p[slot] * r[row : row + 1] for p, r in zip(pieces, ratios)]
                )
            )
        else:
            out.append(functools.reduce(jnp.add, [p[slot] for p in pieces]))
    return out


def pair_kernel(mine, other, out):
    for y in range(YS):
        summed = add_scaled([[ref[y, s] for s in range(SLOTS)] for ref in (mine, other)])
        for slot in range(SLOTS):
            out[y, slot] = summed[slot]


def pair(mine, other):
    return pl.pallas_call(
        pair_kernel,
        in_specs=[whole(), whole()],
        out_specs=whole(),
        out_shape=jax.ShapeDtypeStruct((YS, SLOTS, 8, 128), F32),
        compiler_params=params(),
        name="add_cores",
    )(mine, other)


def line_kernel(pieces, product_out, rest_out):
    summed = add_scaled([[pieces[y, s] for s in range(SLOTS)] for y in range(YS)])
    for slot in range(TILES):
        product_out[slot] = summed[slot]
    product_out[TILES:] = jnp.zeros((REP - TILES, 8, 128), F32)
    for slot in range(TILES, SLOTS):
        rest_out[slot - TILES] = summed[slot]


def line(pieces):
    return pl.pallas_call(
        line_kernel,
        in_specs=[whole()],
        out_specs=[whole(), whole()],
        out_shape=[
            jax.ShapeDtypeStruct((REP, 8, 128), F32),
            jax.ShapeDtypeStruct((SLOTS - TILES, 8, 128), F32),
        ],
        compiler_params=params(),
        name="add_line",
    )(pieces)


def invert_kernel(rest, out):
    packed = jnp.concatenate([rest[GRAM - LEFT], rest[GRAM + 1 - LEFT]], axis=0)
    turned = pltpu.roll(packed, 64, 1)
    row = lax.broadcasted_iota(jnp.int32, (RANK, 128), 0)
    lane = lax.broadcasted_iota(jnp.int32, (RANK, 128), 1)
    gram = jnp.concatenate([packed, turned], axis=0)
    unit = jnp.where(row == lax.rem(lane, RANK), 1.0, 0.0)
    work = jnp.where(lane < 64, gram, unit)
    first = lax.rem(lane, 64) < RANK
    for step in range(RANK - 1):
        column = jnp.where(
            first,
            jnp.broadcast_to(work[:, step : step + 1], (RANK, 128)),
            jnp.broadcast_to(work[:, RANK + step : RANK + step + 1], (RANK, 128)),
        )
        pivot = work[step : step + 1] / column[step : step + 1]
        work = work - jnp.where(row > step, column, 0.0) * pivot
    diagonal = [
        jnp.sum(jnp.where(lane == row + l * RANK, work, 0.0), axis=1, keepdims=True)
        for l in range(LAYERS)
    ]
    root = jnp.where(
        first,
        jnp.broadcast_to(diagonal[0], (RANK, 128)),
        jnp.broadcast_to(diagonal[1], (RANK, 128)),
    )
    inverse = pltpu.roll(work / jnp.sqrt(root), 64, 1)
    left = jnp.concatenate(
        [jnp.where(lane < RANK, inverse, 0.0), jnp.where((lane >= RANK) & (lane < 64), inverse, 0.0)],
        axis=0,
    )
    scale = rest[SCALE - LEFT]
    out[0] = left * math.sqrt(COLS)
    out[1] = jnp.concatenate(
        [left[:RANK] * scale[0:1], left[RANK:] * scale[4:5]], axis=0
    )


def invert(rest):
    return pl.pallas_call(
        invert_kernel,
        in_specs=[whole()],
        out_specs=whole(),
        out_shape=jax.ShapeDtypeStruct((2, 64, 128), F32),
        compiler_params=params(),
        cost_estimate=pl.CostEstimate(flops=2_000_000, bytes_accessed=20_000_000, transcendentals=0),
        name="invert_triangle",
    )(rest)


def finish_kernel(tiles, inverse, left_out, right_out):
    for which, out in ((1, None), (0, left_out)):
        rows = rows_of([tiles[t, 1 - which] for t in range(TILES)])
        done = jnp.dot(
            inverse[which][:, :64],
            rows,
            precision=lax.Precision.HIGHEST,
            preferred_element_type=F32,
        )
        if out is not None:
            out[0] = done[:RANK]
            out[1] = done[RANK:]
        else:
            for t in range(TILES):
                row, block = divmod(t, BLOCKS)
                tile = done[row * 8 : row * 8 + 8, block * 128 : block * 128 + 128]
                for y in range(YS):
                    right_out[y, t] = tile


def finish(tiles, inverse):
    return pl.pallas_call(
        finish_kernel,
        in_specs=[whole(), whole()],
        out_specs=[whole(), whole()],
        out_shape=[
            jax.ShapeDtypeStruct((LAYERS, RANK, ROWS), F32),
            jax.ShapeDtypeStruct((YS, TILES, 8, 128), F32),
        ],
        compiler_params=params(),
        name="apply_triangle",
    )(tiles, inverse)


def assemble_kernel(place, mine, other, out):
    for ref, half in ((mine, place[2]), (other, 1 - place[2])):
        for y in range(YS):
            for t in range(TILES):
                row, block = divmod(t, BLOCKS)
                layer, row = divmod(row, RANK // 8)
                first = pl.multiple_of(half * HALF + y * ROWS + block * 128, 128)
                out[layer, row * 8 : row * 8 + 8, pl.ds(first, 128)] = ref[y, t]


def assemble(place, mine, other):
    return pl.pallas_call(
        assemble_kernel,
        in_specs=[whole(pltpu.SMEM), whole(), whole()],
        out_specs=whole(),
        out_shape=jax.ShapeDtypeStruct((LAYERS, RANK, COLS), F32),
        compiler_params=params(),
        name="assemble_right",
    )(place, mine, other)


def sum_kernel(pieces, *refs):
    out = refs[-1]
    total = functools.reduce(jnp.add, [pieces[r] for r in range(REP)])
    if len(refs) == 1:
        for r in range(REP):
            out[r] = total
    else:
        rest = refs[0]
        for r in range(REP):
            out[r, 0] = total
            out[r, 1] = rest[0]


def sum_and_copy(pieces, rest=None):
    shape = (REP, 8, 128) if rest is None else (REP, 2, 8, 128)
    operands = (pieces,) if rest is None else (pieces, rest)
    return pl.pallas_call(
        sum_kernel,
        in_specs=[whole()] * len(operands),
        out_specs=whole(),
        out_shape=jax.ShapeDtypeStruct(shape, F32),
        compiler_params=params(),
        name="add_replicas",
    )(*operands)


def destinations(run_starts, run_owners, shard):
    ends = jnp.concatenate([run_starts[1:], jnp.full((1,), COLS, jnp.int32)])
    lengths = ends - run_starts
    index = jnp.arange(REP, dtype=jnp.int32)
    before = (index[None, :] < index[:, None]) & (run_owners[None, :] == run_owners[:, None])
    offset = jnp.sum(jnp.where(before, lengths[None, :], 0), axis=1)
    shift = run_owners * ROWS + offset - run_starts
    position = shard * ROWS + jnp.arange(ROWS, dtype=jnp.int32)
    inside = (run_starts[:, None] <= position[None, :]) & (position[None, :] < ends[:, None])
    row = position + jnp.sum(jnp.where(inside, shift[:, None], 0), axis=0)
    return jnp.broadcast_to(row[None, :], (8, ROWS))


def exchange(value, axis):
    return lax.all_to_all(value, axis, split_axis=0, concat_axis=0, tiled=True)


def swap(value):
    return lax.ppermute(value, "core", [(0, 1), (1, 0)])


def shards(gradient, error_buffer, previous_q, run_starts, run_owners):
    rep = lax.axis_index("x") * 8 + lax.axis_index("z")
    line_at, core = lax.axis_index("y"), lax.axis_index("core")
    dest = destinations(run_starts, run_owners, line_at * 2 + core)
    merged, partial = merge(gradient, error_buffer, jnp.swapaxes(previous_q, 1, 2))
    partial = exchange(partial, ("x", "z"))
    tiles = exchange(sum_and_copy(partial), ("x", "z"))
    theirs = jnp.stack([rep, line_at, core, 1 - core]).astype(jnp.int32)
    ours = jnp.stack([rep, line_at, core, core]).astype(jnp.int32)
    sent = swap(product(theirs, dest, tiles, merged, "product_other_half"))
    kept = product(ours, dest, tiles, merged, "product_own_half")
    pieces = exchange(pair(kept, sent), "y")
    terms, rest = line(pieces)
    inverse = invert(rest)
    summed = sum_and_copy(exchange(terms, ("x", "z")), rest)
    left, right = finish(exchange(summed, ("x", "z")), inverse)
    right = exchange(right, "y")
    right = assemble(ours, right, swap(right))
    return (jnp.swapaxes(left, 1, 2), jnp.swapaxes(right, 1, 2))


def solution(mesh):
    grid = jax.sharding.Mesh(mesh.devices.reshape(4, 8, YS, 2), ("x", "z", "y", "core"))
    rep, shard = ("x", "z"), ("y", "core")
    return jax.shard_map(
        shards,
        mesh=grid,
        in_specs=(P(rep, None, shard, None), P(rep, None, shard, None), P(), P(), P()),
        out_specs=(P(None, shard, None), P()),
        check_vma=False,
    )
```

time: 484 us -> 113 us (0.23)
  waiting for transfers between devices: 332 us -> 26 us
  loops' own time: 31.6 us -> 0 us
  other arithmetic: 26.1 us -> 0.52 us
  between operations: 21.8 us -> 0.75 us
  starting transfers between devices: 11 us -> 28.5 us
  Pallas kernels: 0 us -> 15.5 us
  matrix products: 14.1 us -> 0 us
  local copies, waits for them, and re-layouts: 19.5 us -> 8.01 us
  blocking collectives: 25.2 us -> 33.1 us
    psum x2 -> x0, waiting for transfers between devices: 328 us -> none  [the longest x1 200 us: compress(): right_part = lax.psum(right_local, ('rep', 'shard'))]
    all_to_all x0 -> x3, blocking collectives: none -> 33.1 us  [exchange(): return lax.all_to_all(value, axis, split_axis=0, concat_axis=0, tiled=True)]
    another operation x2 -> x0, loops' own time: 31.6 us -> none  [send_to_owners(): lax.fori_loop(0, shard_count, place_rows, jnp.zeros((row_count + capacity...]
    psum x1 -> x0, blocking collectives: 25.2 us -> none  [compress(): gram_matrix = lax.psum(gram_local, 'shard')]
    all_to_all x2 -> x3, waiting for transfers between devices: 4.25 us -> 24.7 us  [exchange(): return lax.all_to_all(value, axis, split_axis=0, concat_axis=0, tiled=True)]
    pallas_call x0 -> x10, Pallas kernels: none -> 15.5 us  [the longest x1 5.69 us: merge(): pl.pallas_call(merge_kernel, grid=(LAYERS, BLOCKS), in_specs=[block, bloc...]
    another operation x16 -> x2, other arithmetic: 13.7 us -> 0.16 us  [the longest x1 0.08 us: shards(): theirs = jnp.stack([rep, line_at, core, 1 - core]).astype(jnp.int32)]
    dot_general x8 -> x0, matrix products: 11.9 us -> none  [the longest x2 5.88 us: compress(): jnp.einsum('lrc,lrk->lck', matrices, own_basis.astype(jnp.bfloat16), pref...]
  transfers between devices with their start and end apart: 4 -> 5, of which waited for: 3 -> 4; matrix products, arithmetic and copies ran while one was open for 5% -> 1% of each run, Pallas kernels for 0% -> 4%
where the time goes in v1:
time: 113 us; the launch traced here: 112 us
  blocking collectives  33.1 us (29%)
  starting transfers between devices  28.5 us (25%)
  waiting for transfers between devices  26 us (23%)
  Pallas kernels  15.5 us (14%)
  local copies, waits for them, and re-layouts  8.01 us (7%)
    all_to_all x3, blocking collectives, exchange(): return lax.all_to_all(value, axis, split_axis=0, concat_axis=0, tiled=True)  33.1 us
    all_to_all x3, waiting for transfers between devices, exchange(): return lax.all_to_all(value, axis, split_axis=0, concat_axis=0, tiled=True)  24.7 us
    all_to_all x3, starting transfers between devices, exchange(): return lax.all_to_all(value, axis, split_axis=0, concat_axis=0, tiled=True)  19.6 us
    ppermute x2, starting transfers between devices, swap(): return lax.ppermute(value, 'core', [(0, 1), (1, 0)])  8.86 us
    unnamed x12, local copies, waits for them, and re-layouts  7.93 us
    pallas_call x1, Pallas kernels, merge(): pl.pallas_call(merge_kernel, grid=(LAYERS, BLOCKS), in_specs=[block, bloc...  5.69 us
    pallas_call x2, Pallas kernels, product(): pl.pallas_call(functools.partial(product_kernel, True), in_specs=[whole(p...  3.06 us
    pallas_call x1, Pallas kernels, invert(): pl.pallas_call(invert_kernel, in_specs=[whole()], out_specs=whole(), out_...  2.76 us
  transfers between devices with their start and end apart: 5, of which 4 were waited for; matrix products, arithmetic and copies ran while one was open for 1% of the time, Pallas kernels for 4%

profile of v1, /device:TPU:1, one launch (start us, length us, event | category | flops | bytes accessed | tf_op | source)
XLA Modules:
  0.0 112.4 jit_solution(5709927646959924756)
XLA Ops:
  0.6 0.0 copy-start.2
  0.6 2.3 %copy-done.2 = bf16[1,2,384,3072]{3,2,1,0:T(8,128)(2,1)S(1)} copy-done((bf16[1,2,384,3072]{3,2,1,0:T(8,128)(2,1)S(1)}, bf16[1,2,384,3072]{3,2,1,0:T(8,128)(2,1)}, u32[]{:S(2)}) %copy-start.2) | copy-done | bytes 4718616
  3.0 0.0 copy-start.3
  3.0 1.1 %copy-done.3 = f32[2,3072,32]{1,2,0:T(8,128)S(1)} copy-done((f32[2,3072,32]{1,2,0:T(8,128)S(1)}, f32[2,3072,32]{1,2,0:T(8,128)}, u32[]{:S(2)}) %copy-start.3) | copy-done | bytes 786456
  4.1 0.0 copy-start.5
  4.1 0.0 copy-start.4
  4.1 5.7 %merge_project.1 = (bf16[2,384,3072]{2,1,0:T(8,128)(2,1)S(1)}, f32[32,8,128]{2,1,0:T(8,128)}) custom-call(bf16[1,2,384,3072]{3,2,1,0:T(8,128)(2,1)S(1)} %copy-done.2, bf16[1,2,384,3072]{3,2,1,0:T(8,128)(2,1)} %error.1, f32[2,32,3072]{2,1,0:T(8,128)S(1)} %bitcast.7), custom_call_target="tpu_custom_call" | custom-call | tf_op jit(solution)/shard_map/merge_project/pallas_call | solution.py:62
  9.8 0.0 copy-start
  9.8 2.1 %copy-done = bf16[2,384,3072]{2,1,0:T(8,128)(2,1)} copy-done((bf16[2,384,3072]{2,1,0:T(8,128)(2,1)}, bf16[2,384,3072]{2,1,0:T(8,128)(2,1)S(1)}, u32[]{:S(2)}) %copy-start) | copy-done | bytes 4718616
  11.9 11.9 %all-to-all-start = ((f32[32,8,128]{2,1,0:T(8,128)}), f32[32,8,128]{2,1,0:T(8,128)S(1)}, u32[]{:S(2)}, u32[]{:S(2)}) async-start(f32[32,8,128]{2,1,0:T(8,128)} %get-tuple-element.8), calls=%async_computation | async-start | bytes 262144 | tf_op jit(solution)/shard_map/all_to_all | solution.py:355
  23.8 0.0 copy-done.5
  23.8 0.1 slice.3
  23.9 0.1 pad_add_fusion.2
  24.0 0.0 copy-done.4
  24.0 0.2 select_reduce_fusion.1
  24.2 0.1 select_reduce_fusion
  24.3 8.7 %all-to-all-done.pieces = f32[32,8,128]{2,1,0:T(8,128)S(1)} async-done(((f32[32,8,128]{2,1,0:T(8,128)}), f32[32,8,128]{2,1,0:T(8,128)S(1)}, u32[]{:S(2)}, u32[]{:S(2)}) %all-to-all-start) | async-done | bytes 131104 | tf_op jit(solution)/shard_map/all_to_all | solution.py:355
  33.0 0.7 add_replicas.2
  33.7 3.9 %all-to-all-start.1 = ((f32[32,8,128]{2,1,0:T(8,128)}), f32[32,8,128]{2,1,0:T(8,128)S(1)}, u32[]{:S(2)}, u32[]{:S(2)}) async-start(f32[32,8,128]{2,1,0:T(8,128)} %add_replicas.2), calls=%async_computation.1 | async-start | bytes 262144 | tf_op jit(solution)/shard_map/all_to_all | solution.py:355
  37.5 0.1 pad_add_fusion.3
  37.6 9.1 %all-to-all-done.1.tiles = f32[32,8,128]{2,1,0:T(8,128)S(1)} async-done(((f32[32,8,128]{2,1,0:T(8,128)}), f32[32,8,128]{2,1,0:T(8,128)S(1)}, u32[]{:S(2)}, u32[]{:S(2)}) %all-to-all-start.1) | async-done | bytes 131104 | tf_op jit(solution)/shard_map/all_to_all | solution.py:355
  46.7 0.0 copy-start.1
  46.7 2.3 %copy-done.1 = bf16[2,384,3072]{2,1,0:T(8,128)(2,1)S(1)} copy-done((bf16[2,384,3072]{2,1,0:T(8,128)(2,1)S(1)}, bf16[2,384,3072]{2,1,0:T(8,128)(2,1)}, u32[]{:S(2)}) %copy-start.1) | copy-done | bytes 4718616
  49.0 1.5 %product_other_half.1 = f32[4,28,8,128]{3,2,1,0:T(8,128)S(1)} custom-call(s32[4]{0:T(128)S(1)} %get-tuple-element.14.place, s32[8,384]{1,0:T(8,128)S(1)} %broadcast_in_dim.44.dest, f32[32,8,128]{2,1,0:T(8,128)S(1)} %all-to-all-done.1.tiles, bf16[2,384,3072]{2,1,0:T(8,128)(2,1)S(1)} %copy-done.1), custom_call_target="tpu_custom_call" | custom-call | tf_op jit(solution)/shard_map/product_other_half/pallas_call | solution.py:140
  50.5 3.4 %collective-permute-start = (f32[4,28,8,128]{3,2,1,0:T(8,128)S(1)}, f32[4,28,8,128]{3,2,1,0:T(8,128)S(1)}, u32[]{:S(2)}, u32[]{:S(2)}) collective-permute-start(f32[4,28,8,128]{3,2,1,0:T(8,128)S(1)} %product_other_half.1), channel_id=1, source_target_pairs={{0,1},{1,0},{2,3},{3,2},{4,5},{5,4},{6,7},{7,6},{8,9},{9,8},{10,11... | collective-permute-start | bytes 1376264 | tf_op jit(solution)/shard_map/ppermute | solution.py:359
  53.9 0.1 pad_add_fusion.place
  54.0 1.5 %product_own_half.1.mine = f32[4,28,8,128]{3,2,1,0:T(8,128)S(1)} custom-call(s32[4]{0:T(128)S(1)} %pad_add_fusion.place, s32[8,384]{1,0:T(8,128)S(1)} %broadcast_in_dim.44.dest, f32[32,8,128]{2,1,0:T(8,128)S(1)} %all-to-all-done.1.tiles, bf16[2,384,3072]{2,1,0:T(8,128)(2,1)S(1)} %copy-done.1), custom_call_target="tpu_custom_call" | custom-call | tf_op jit(solution)/shard_map/product_own_half/pallas_call | solution.py:140
  55.5 0.0 collective-permute-done.other
  55.5 0.1 add_cores.1
  55.6 12.1 %all_to_all.30.pieces = f32[4,28,8,128]{3,2,1,0:T(8,128)S(1)} all-to-all(f32[4,28,8,128]{3,2,1,0:T(8,128)S(1)} %add_cores.1), channel_id=1, replica_groups=mesh['x'=4,'z'=8,'y'=4,'core'=2] {'y'}, dimensions={0} | all-to-all | bytes 917504 | tf_op jit(solution)/shard_map/all_to_all | solution.py:355
  67.8 12.3 %all_to_all.31.pieces = f32[32,8,128]{2,1,0:T(8,128)S(1)} all-to-all(f32[32,8,128]{2,1,0:T(8,128)S(1)} %get-tuple-element.10), channel_id=1, replica_groups=mesh['x'=4,'z'=8,'y'=4,'core'=2] {'x','z'}, dimensions={0} | all-to-all | bytes 262144 | tf_op jit(solution)/shard_map/all_to_all | solution.py:355
  80.1 0.7 add_replicas.3
  80.9 3.9 %all-to-all-start.4 = ((f32[32,2,8,128]{3,2,1,0:T(8,128)}), f32[32,2,8,128]{3,2,1,0:T(8,128)S(1)}, u32[]{:S(2)}, u32[]{:S(2)}) async-start(f32[32,2,8,128]{3,2,1,0:T(8,128)} %add_replicas.3), calls=%async_computation.4 | async-start | bytes 524288 | tf_op jit(solution)/shard_map/all_to_all | solution.py:355
  84.8 2.8 %invert_triangle.1.inverse = f32[2,64,128]{2,1,0:T(8,128)S(1)} custom-call(f32[4,8,128]{2,1,0:T(8,128)S(1)} %get-tuple-element.11.refs_0_.rest), custom_call_target="tpu_custom_call" | custom-call | flops 2000000 | bytes 20000000 | tf_op jit(solution)/shard_map/invert_triangle/pallas_call | solution.py:249
  87.5 6.9 %all-to-all-done.4.tiles = f32[32,2,8,128]{3,2,1,0:T(8,128)S(1)} async-done(((f32[32,2,8,128]{3,2,1,0:T(8,128)}), f32[32,2,8,128]{3,2,1,0:T(8,128)S(1)}, u32[]{:S(2)}, u32[]{:S(2)}) %all-to-all-start.4) | async-done | bytes 262176 | tf_op jit(solution)/shard_map/all_to_all | solution.py:355
  94.5 0.9 apply_triangle.1
  95.4 8.6 %all_to_all.32.mine = f32[4,24,8,128]{3,2,1,0:T(8,128)S(1)} all-to-all(f32[4,24,8,128]{3,2,1,0:T(8,128)S(1)} %get-tuple-element.13), channel_id=1, replica_groups=mesh['x'=4,'z'=8,'y'=4,'core'=2] {'y'}, dimensions={0} | all-to-all | bytes 786432 | tf_op jit(solution)/shard_map/all_to_all | solution.py:355
  104.0 5.5 %collective-permute-start.1 = (f32[4,24,8,128]{3,2,1,0:T(8,128)S(1)}, f32[4,24,8,128]{3,2,1,0:T(8,128)S(1)}, u32[]{:S(2)}, u32[]{:S(2)}) collective-permute-start(f32[4,24,8,128]{3,2,1,0:T(8,128)S(1)} %all_to_all.32.mine), channel_id=1, source_target_pairs={{0,1},{1,0},{2,3},{3,2},{4,5},{5,4},{6,7},{7,6},{8,9},{9,8},{10,11... | collective-permute-start | bytes 1179656 | tf_op jit(solution)/shard_map/ppermute | solution.py:359
  109.5 1.3 %collective-permute-done.1.other = f32[4,24,8,128]{3,2,1,0:T(8,128)S(1)} collective-permute-done((f32[4,24,8,128]{3,2,1,0:T(8,128)S(1)}, f32[4,24,8,128]{3,2,1,0:T(8,128)S(1)}, u32[]{:S(2)}, u32[]{:S(2)}) %collective-permute-start.1) | collective-permute-done | bytes 393248 | tf_op jit(solution)/shard_map/ppermute | solution.py:359
  110.9 1.5 %assemble_right.1 = f32[2,32,3072]{2,1,0:T(8,128)} custom-call(s32[4]{0:T(128)S(1)} %pad_add_fusion.place, f32[4,24,8,128]{3,2,1,0:T(8,128)S(1)} %all_to_all.32.mine, f32[4,24,8,128]{3,2,1,0:T(8,128)S(1)} %collective-permute-done.1.other), custom_call_target="tpu_custom_call" | custom-call | tf_op jit(solution)/shard_map/assemble_right/pallas_call | solution.py:305
  (5 shorter events, 0.1 us)
Async XLA Ops:
  0.6 2.3 %copy-start.2 = (bf16[1,2,384,3072]{3,2,1,0:T(8,128)(2,1)S(1)}, bf16[1,2,384,3072]{3,2,1,0:T(8,128)(2,1)}, u32[]{:S(2)}) copy-start(bf16[1,2,384,3072]{3,2,1,0:T(8,128)(2,1)} %gradient.1) | copy-start | bytes 14155780
  3.0 1.1 %copy-start.3 = (f32[2,3072,32]{1,2,0:T(8,128)S(1)}, f32[2,3072,32]{1,2,0:T(8,128)}, u32[]{:S(2)}) copy-start(f32[2,3072,32]{1,2,0:T(8,128)} %param.7) | copy-start | bytes 2359300
  4.1 19.7 %copy-start.5 = (s32[32]{0:T(128)S(1)}, s32[32]{0:T(128)}, u32[]{:S(2)}) copy-start(s32[32]{0:T(128)} %param.8) | copy-start | bytes 388
  4.1 19.9 %copy-start.4 = (s32[32]{0:T(128)S(1)}, s32[32]{0:T(128)}, u32[]{:S(2)}) copy-start(s32[32]{0:T(128)} %param.9) | copy-start | bytes 388
  9.8 2.1 %copy-start = (bf16[2,384,3072]{2,1,0:T(8,128)(2,1)}, bf16[2,384,3072]{2,1,0:T(8,128)(2,1)S(1)}, u32[]{:S(2)}) copy-start(bf16[2,384,3072]{2,1,0:T(8,128)(2,1)S(1)} %get-tuple-element.9.merged) | copy-start | bytes 14155780
  11.9 21.0 %all-to-all-start = ((f32[32,8,128]{2,1,0:T(8,128)}), f32[32,8,128]{2,1,0:T(8,128)S(1)}, u32[]{:S(2)}, u32[]{:S(2)}) async-start(f32[32,8,128]{2,1,0:T(8,128)} %get-tuple-element.8), calls=%async_computation | async-start | bytes 262144 | tf_op jit(solution)/shard_map/all_to_all | solution.py:355
  33.7 13.0 %all-to-all-start.1 = ((f32[32,8,128]{2,1,0:T(8,128)}), f32[32,8,128]{2,1,0:T(8,128)S(1)}, u32[]{:S(2)}, u32[]{:S(2)}) async-start(f32[32,8,128]{2,1,0:T(8,128)} %add_replicas.2), calls=%async_computation.1 | async-start | bytes 262144 | tf_op jit(solution)/shard_map/all_to_all | solution.py:355
  46.7 2.3 %copy-start.1 = (bf16[2,384,3072]{2,1,0:T(8,128)(2,1)S(1)}, bf16[2,384,3072]{2,1,0:T(8,128)(2,1)}, u32[]{:S(2)}) copy-start(bf16[2,384,3072]{2,1,0:T(8,128)(2,1)} %copy-done) | copy-start | bytes 14155780
  50.5 5.0 %collective-permute-start = (f32[4,28,8,128]{3,2,1,0:T(8,128)S(1)}, f32[4,28,8,128]{3,2,1,0:T(8,128)S(1)}, u32[]{:S(2)}, u32[]{:S(2)}) collective-permute-start(f32[4,28,8,128]{3,2,1,0:T(8,128)S(1)} %product_other_half.1), channel_id=1, source_target_pairs={{0,1},{1,0},{2,3},{3,2},{4,5},{5,4},{6,7},{7,6},{8,9},{9,8},{10,11... | collective-permute-start | bytes 1376264 | tf_op jit(solution)/shard_map/ppermute | solution.py:359
  80.9 13.6 %all-to-all-start.4 = ((f32[32,2,8,128]{3,2,1,0:T(8,128)}), f32[32,2,8,128]{3,2,1,0:T(8,128)S(1)}, u32[]{:S(2)}, u32[]{:S(2)}) async-start(f32[32,2,8,128]{3,2,1,0:T(8,128)} %add_replicas.3), calls=%async_computation.4 | async-start | bytes 524288 | tf_op jit(solution)/shard_map/all_to_all | solution.py:355
  104.0 6.8 %collective-permute-start.1 = (f32[4,24,8,128]{3,2,1,0:T(8,128)S(1)}, f32[4,24,8,128]{3,2,1,0:T(8,128)S(1)}, u32[]{:S(2)}, u32[]{:S(2)}) collective-permute-start(f32[4,24,8,128]{3,2,1,0:T(8,128)S(1)} %all_to_all.32.mine), channel_id=1, source_target_pairs={{0,1},{1,0},{2,3},{3,2},{4,5},{5,4},{6,7},{7,6},{8,9},{9,8},{10,11... | collective-permute-start | bytes 1179656 | tf_op jit(solution)/shard_map/ppermute | solution.py:359

commit v2 on v1

--- a/solution.py
+++ b/solution.py
@@ -19,7 +19,10 @@
 ROW_TILES = LAYERS * RANK // 8
 TILES = ROW_TILES * BLOCKS
 LEFT, GRAM, SCALE, SLOTS = TILES, TILES + 1, TILES + 3, TILES + 4
-VMEM_LIMIT = 40 * 1024 * 1024
+CHUNK = 512
+CHUNKS = COLS // CHUNK
+RUNS = 4
+VMEM_LIMIT = 24 * 1024 * 1024
 F32 = jnp.float32
 BF16 = jnp.bfloat16
 
@@ -44,36 +47,100 @@
     return lax.dot_general(left, right, (((1,), (1,)), ((), ())), preferred_element_type=F32)
 
 
-def merge_kernel(gradient, error, q, merged, partial):
-    layer, block = pl.program_id(0), pl.program_id(1)
-    total = (gradient[0, 0].astype(F32) + error[0, 0].astype(F32)).astype(BF16)
-    merged[0] = total
-    terms = dot_rows(q[0].astype(BF16), total)
-    for part in range(RANK // 8):
-        partial[(layer * (RANK // 8) + part) * BLOCKS + block] = terms[part * 8 : part * 8 + 8]
-
-    @pl.when((layer == 0) & (block == 0))
-    def _():
-        partial[TILES:] = jnp.zeros((REP - TILES, 8, 128), F32)
-
-
-def merge(gradient, error, q):
-    block = pl.BlockSpec((1, 1, 128, COLS), lambda l, b: (0, l, b, 0))
+def merge_kernel(
+    gradient, error, q, starts, owners, merged, partial, dest, g, e, q_in, table, sems, table_sems
+):
+    tables = [
+        pltpu.make_async_copy(source, table.at[i], table_sems.at[i])
+        for i, source in enumerate((starts, owners))
+    ]
+    for copy in tables:
+        copy.start()
+    copies = []
+    for layer in range(LAYERS):
+        copies.append([pltpu.make_async_copy(q.at[layer], q_in.at[layer], sems.at[layer, CHUNKS, 0])])
+        for chunk in range(CHUNKS):
+            columns = pl.ds(chunk * CHUNK, CHUNK)
+            copies.append(
+                [
+                    pltpu.make_async_copy(
+                        source.at[0, layer, :, columns],
+                        into.at[layer, chunk],
+                        sems.at[layer, chunk, i],
+                    )
+                    for i, (source, into) in enumerate(((gradient, g), (error, e)))
+                ]
+            )
+    for group in copies:
+        for copy in group:
+            copy.start()
+    partial[TILES:] = jnp.zeros((REP - TILES, 8, 128), F32)
+    for copy in tables:
+        copy.wait()
+    dest[...] = destinations(table)
+    arrived = iter(copies)
+    for layer in range(LAYERS):
+        for copy in next(arrived):
+            copy.wait()
+        terms = jnp.zeros((RANK, ROWS), F32)
+        for chunk in range(CHUNKS):
+            for copy in next(arrived):
+                copy.wait()
+            total = (g[layer, chunk].astype(F32) + e[layer, chunk].astype(F32)).astype(BF16)
+            columns = slice(chunk * CHUNK, chunk * CHUNK + CHUNK)
+            merged[layer, :, columns] = total
+            terms = terms + dot_rows(q_in[layer, :, columns].astype(BF16), total)
+        for part in range(RANK // 8):
+            for block in range(BLOCKS):
+                partial[(layer * (RANK // 8) + part) * BLOCKS + block] = terms[
+                    part * 8 : part * 8 + 8, block * 128 : block * 128 + 128
+                ]
+
+
+def destinations(table):
+    shard = lax.axis_index("y") * 2 + lax.axis_index("core")
+    first = shard * RUNS
+    mine = [table[1, first + t] for t in range(RUNS)]
+
+    def count(run, before):
+        length = table[0, run + 1] - table[0, run]
+        return tuple(b + jnp.where(table[1, run] == o, length, 0) for b, o in zip(before, mine))
+
+    before = lax.fori_loop(0, first, count, (jnp.int32(0),) * RUNS)
+    position = shard * ROWS + lax.broadcasted_iota(jnp.int32, (8, ROWS), 1)
+    place = position
+    for t in range(RUNS):
+        start = table[0, first + t]
+        moved = position + (mine[t] * ROWS + before[t] - start)
+        place = jnp.where(position >= start, moved, place)
+    return place
+
+
+def merge(gradient, error, q, run_starts, run_owners):
+    operands = [
+        pltpu.with_memory_space_constraint(value, pltpu.HBM)
+        for value in (gradient, error, q, run_starts, run_owners)
+    ]
     return pl.pallas_call(
         merge_kernel,
-        grid=(LAYERS, BLOCKS),
-        in_specs=[block, block, pl.BlockSpec((1, RANK, COLS), lambda l, b: (l, 0, 0))],
-        out_specs=[
-            pl.BlockSpec((1, 128, COLS), lambda l, b: (l, b, 0)),
-            pl.BlockSpec((REP, 8, 128), lambda l, b: (0, 0, 0)),
+        in_specs=[whole(pltpu.HBM)] * 5,
+        out_specs=[whole()] * 3,
+        out_shape=[
+            pltpu.VMEM((LAYERS, ROWS, COLS), BF16),
+            jax.ShapeDtypeStruct((REP, 8, 128), F32),
+            jax.ShapeDtypeStruct((8, ROWS), jnp.int32),
         ],
-        out_shape=[
-            jax.ShapeDtypeStruct((LAYERS, ROWS, COLS), BF16),
-            jax.ShapeDtypeStruct((REP, 8, 128), F32),
+        scratch_shapes=[
+            pltpu.VMEM((LAYERS, CHUNKS, ROWS, CHUNK), BF16),
+            pltpu.VMEM((LAYERS, CHUNKS, ROWS, CHUNK), BF16),
+            pltpu.VMEM((LAYERS, RANK, COLS), F32),
+            pltpu.SMEM((2, REP), jnp.int32),
+            pltpu.SemaphoreType.DMA((LAYERS, CHUNKS + 1, 2)),
+            pltpu.SemaphoreType.DMA((2,)),
         ],
         compiler_params=params(),
         name="merge_project",
-    )(gradient, error, q)
+    )(*operands)
 
 
 def rows_of(tiles):
@@ -86,26 +153,26 @@
     )
 
 
-def product_kernel(with_extras, place, dest, tiles, merged, out):
-    rep, half = place[0], place[3]
+def product_kernel(own, dest, tiles, merged, out):
+    rep = lax.axis_index("x") * 8 + lax.axis_index("z")
+    half = lax.axis_index("core") if own else 1 - lax.axis_index("core")
     factor = rows_of(tiles)
     biggest = [
         jnp.max(jnp.abs(factor[l * RANK : l * RANK + RANK]), keepdims=True) for l in range(LAYERS)
     ]
     scales = [jnp.where(b > 0, b * 64.0, 1.0) for b in biggest]
+    columns = pl.ds(pl.multiple_of(half * HALF, 128), HALF)
     for layer in range(LAYERS):
         scaled = factor[layer * RANK : layer * RANK + RANK] * (1.0 / scales[layer])
         parts = jnp.concatenate(split3(scaled), axis=0)
+        product = jnp.dot(parts, merged[layer, :, columns], preferred_element_type=F32)
+        product = product[:RANK] + product[RANK : 2 * RANK] + product[2 * RANK :]
         for y in range(YS):
-            first = pl.multiple_of(half * HALF + y * ROWS, 128)
-            product = jnp.dot(
-                parts, merged[layer, :, pl.ds(first, ROWS)], preferred_element_type=F32
-            )
-            product = product[:RANK] + product[RANK : 2 * RANK] + product[2 * RANK :]
             for part in range(RANK // 8):
                 for block in range(BLOCKS):
+                    first = y * ROWS + block * 128
                     out[y, (layer * (RANK // 8) + part) * BLOCKS + block] = product[
-                        part * 8 : part * 8 + 8, block * 128 : block * 128 + 128
+                        part * 8 : part * 8 + 8, first : first + 128
                     ]
     tile = jnp.minimum(rep, TILES - 1)
     row_tile = tile // BLOCKS
@@ -136,15 +203,15 @@
         out[y, SCALE] = scale
 
 
-def product(place, dest, tiles, merged, name):
-    return pl.pallas_call(
-        functools.partial(product_kernel, True),
-        in_specs=[whole(pltpu.SMEM), whole(), whole(), whole()],
+def product(own, dest, tiles, merged):
+    return pl.pallas_call(
+        functools.partial(product_kernel, own),
+        in_specs=[whole()] * 3,
         out_specs=whole(),
         out_shape=jax.ShapeDtypeStruct((YS, SLOTS, 8, 128), F32),
         compiler_params=params(),
-        name=name,
-    )(place, dest, tiles, merged)
+        name="product_own_half" if own else "product_other_half",
+    )(dest, tiles, pltpu.with_memory_space_constraint(merged, pltpu.VMEM))
 
 
 def add_scaled(pieces):
@@ -239,10 +306,8 @@
         axis=0,
     )
     scale = rest[SCALE - LEFT]
-    out[0] = left * math.sqrt(COLS)
-    out[1] = jnp.concatenate(
-        [left[:RANK] * scale[0:1], left[RANK:] * scale[4:5]], axis=0
-    )
+    out[0] = jnp.concatenate([left[:RANK] * scale[0:1], left[RANK:] * scale[4:5]], axis=0)
+    out[1] = left * math.sqrt(COLS)
 
 
 def invert(rest):
@@ -257,59 +322,49 @@
     )(rest)
 
 
-def finish_kernel(tiles, inverse, left_out, right_out):
-    for which, out in ((1, None), (0, left_out)):
-        rows = rows_of([tiles[t, 1 - which] for t in range(TILES)])
-        done = jnp.dot(
-            inverse[which][:, :64],
-            rows,
-            precision=lax.Precision.HIGHEST,
-            preferred_element_type=F32,
-        )
-        if out is not None:
-            out[0] = done[:RANK]
-            out[1] = done[RANK:]
-        else:
-            for t in range(TILES):
-                row, block = divmod(t, BLOCKS)
-                tile = done[row * 8 : row * 8 + 8, block * 128 : block * 128 + 128]
-                for y in range(YS):
-                    right_out[y, t] = tile
-
-
-def finish(tiles, inverse):
-    return pl.pallas_call(
-        finish_kernel,
+def apply_kernel(which, tiles, inverse, out):
+    rows = rows_of([tiles[t, which] for t in range(TILES)])
+    done = jnp.dot(
+        inverse[which][:, :64], rows, precision=lax.Precision.HIGHEST, preferred_element_type=F32
+    )
+    for copy in range(out.shape[0]):
+        out[copy] = done
+
+
+def apply(which, copies, tiles, inverse):
+    return pl.pallas_call(
+        functools.partial(apply_kernel, which),
         in_specs=[whole(), whole()],
-        out_specs=[whole(), whole()],
-        out_shape=[
-            jax.ShapeDtypeStruct((LAYERS, RANK, ROWS), F32),
-            jax.ShapeDtypeStruct((YS, TILES, 8, 128), F32),
-        ],
-        compiler_params=params(),
-        name="apply_triangle",
+        out_specs=whole(),
+        out_shape=jax.ShapeDtypeStruct((copies, LAYERS * RANK, ROWS), F32),
+        compiler_params=params(),
+        name="apply_left" if which else "apply_right",
     )(tiles, inverse)
 
 
-def assemble_kernel(place, mine, other, out):
-    for ref, half in ((mine, place[2]), (other, 1 - place[2])):
+def assemble_kernel(mine, other, out, sems):
+    core = lax.axis_index("core")
+    copies = []
+    for i, (piece, half) in enumerate(((mine, core), (other, 1 - core))):
         for y in range(YS):
-            for t in range(TILES):
-                row, block = divmod(t, BLOCKS)
-                layer, row = divmod(row, RANK // 8)
-                first = pl.multiple_of(half * HALF + y * ROWS + block * 128, 128)
-                out[layer, row * 8 : row * 8 + 8, pl.ds(first, 128)] = ref[y, t]
-
-
-def assemble(place, mine, other):
+            columns = pl.ds(pl.multiple_of(half * HALF + y * ROWS, 128), ROWS)
+            copies.append(pltpu.make_async_copy(piece.at[y], out.at[:, columns], sems.at[i, y]))
+    for copy in copies:
+        copy.start()
+    for copy in copies:
+        copy.wait()
+
+
+def assemble(mine, other):
     return pl.pallas_call(
         assemble_kernel,
-        in_specs=[whole(pltpu.SMEM), whole(), whole()],
-        out_specs=whole(),
-        out_shape=jax.ShapeDtypeStruct((LAYERS, RANK, COLS), F32),
+        in_specs=[whole(), whole()],
+        out_specs=whole(pltpu.HBM),
+        out_shape=jax.ShapeDtypeStruct((LAYERS * RANK, COLS), F32),
+        scratch_shapes=[pltpu.SemaphoreType.DMA((2, YS))],
         compiler_params=params(),
         name="assemble_right",
-    )(place, mine, other)
+    )(mine, other)
 
 
 def sum_kernel(pieces, *refs):
@@ -338,19 +393,6 @@
     )(*operands)
 
 
-def destinations(run_starts, run_owners, shard):
-    ends = jnp.concatenate([run_starts[1:], jnp.full((1,), COLS, jnp.int32)])
-    lengths = ends - run_starts
-    index = jnp.arange(REP, dtype=jnp.int32)
-    before = (index[None, :] < index[:, None]) & (run_owners[None, :] == run_owners[:, None])
-    offset = jnp.sum(jnp.where(before, lengths[None, :], 0), axis=1)
-    shift = run_owners * ROWS + offset - run_starts
-    position = shard * ROWS + jnp.arange(ROWS, dtype=jnp.int32)
-    inside = (run_starts[:, None] <= position[None, :]) & (position[None, :] < ends[:, None])
-    row = position + jnp.sum(jnp.where(inside, shift[:, None], 0), axis=0)
-    return jnp.broadcast_to(row[None, :], (8, ROWS))
-
-
 def exchange(value, axis):
     return lax.all_to_all(value, axis, split_axis=0, concat_axis=0, tiled=True)
 
@@ -360,24 +402,20 @@
 
 
 def shards(gradient, error_buffer, previous_q, run_starts, run_owners):
-    rep = lax.axis_index("x") * 8 + lax.axis_index("z")
-    line_at, core = lax.axis_index("y"), lax.axis_index("core")
-    dest = destinations(run_starts, run_owners, line_at * 2 + core)
-    merged, partial = merge(gradient, error_buffer, jnp.swapaxes(previous_q, 1, 2))
-    partial = exchange(partial, ("x", "z"))
-    tiles = exchange(sum_and_copy(partial), ("x", "z"))
-    theirs = jnp.stack([rep, line_at, core, 1 - core]).astype(jnp.int32)
-    ours = jnp.stack([rep, line_at, core, core]).astype(jnp.int32)
-    sent = swap(product(theirs, dest, tiles, merged, "product_other_half"))
-    kept = product(ours, dest, tiles, merged, "product_own_half")
-    pieces = exchange(pair(kept, sent), "y")
+    rep = ("x", "z")
+    q = jnp.swapaxes(previous_q, 1, 2)
+    merged, partial, dest = merge(gradient, error_buffer, q, run_starts, run_owners)
+    tiles = exchange(sum_and_copy(exchange(partial, rep)), rep)
+    sent = swap(product(False, dest, tiles, merged))
+    pieces = exchange(pair(product(True, dest, tiles, merged), sent), "y")
     terms, rest = line(pieces)
     inverse = invert(rest)
-    summed = sum_and_copy(exchange(terms, ("x", "z")), rest)
-    left, right = finish(exchange(summed, ("x", "z")), inverse)
-    right = exchange(right, "y")
-    right = assemble(ours, right, swap(right))
-    return (jnp.swapaxes(left, 1, 2), jnp.swapaxes(right, 1, 2))
+    tiles = exchange(sum_and_copy(exchange(terms, rep), rest), rep)
+    right = exchange(apply(0, YS, tiles, inverse), "y")
+    left = apply(1, 1, tiles, inverse)
+    right = assemble(right, swap(right))
+    shape = (LAYERS, RANK, -1)
+    return tuple(jnp.swapaxes(value.reshape(shape), 1, 2) for value in (left, right))
 
 
 def solution(mesh):

time: 113 us -> 101 us (0.89)
  blocking collectives: 33.1 us -> 66.8 us
  waiting for transfers between devices: 26 us -> 7.85 us
  starting transfers between devices: 28.5 us -> 12.8 us
  local copies, waits for them, and re-layouts: 8.01 us -> 0 us
  Pallas kernels: 15.5 us -> 12.2 us
    all_to_all x3 -> x5, blocking collectives: 33.1 us -> 66.8 us  [exchange(): return lax.all_to_all(value, axis, split_axis=0, concat_axis=0, tiled=True)]
    all_to_all x3 -> x1, waiting for transfers between devices: 24.7 us -> 6.88 us  [exchange(): return lax.all_to_all(value, axis, split_axis=0, concat_axis=0, tiled=True)]
    all_to_all x3 -> x1, starting transfers between devices: 19.6 us -> 3.87 us  [exchange(): return lax.all_to_all(value, axis, split_axis=0, concat_axis=0, tiled=True)]
    unnamed x12 -> x0, local copies, waits for them, and re-layouts: 7.93 us -> none
    pallas_call x5 -> x6, Pallas kernels: 11.2 us -> 8.56 us  [the longest x1 4.62 us: merge(): pl.pallas_call(merge_kernel, in_specs=[whole(pltpu.HBM)] * 5, out_specs=[...]
  transfers between devices with their start and end apart: 5 -> 3, of which waited for: 4 -> 3; matrix products, arithmetic and copies ran while one was open for 1% -> 0% of each run, Pallas kernels for 4% -> 5%
where the time goes in v2:
time: 101 us; the launch traced here: 100 us
  blocking collectives  66.8 us (66%)
  starting transfers between devices  12.8 us (13%)
  Pallas kernels  12.2 us (12%)
  waiting for transfers between devices  7.85 us (8%)
    all_to_all x5, blocking collectives, exchange(): return lax.all_to_all(value, axis, split_axis=0, concat_axis=0, tiled=True)  66.8 us
    ppermute x2, starting transfers between devices, swap(): return lax.ppermute(value, 'core', [(0, 1), (1, 0)])  8.89 us
    all_to_all x1, waiting for transfers between devices, exchange(): return lax.all_to_all(value, axis, split_axis=0, concat_axis=0, tiled=True)  6.88 us
    pallas_call x1, Pallas kernels, merge(): pl.pallas_call(merge_kernel, in_specs=[whole(pltpu.HBM)] * 5, out_specs=[...  4.62 us
    all_to_all x1, starting transfers between devices, exchange(): return lax.all_to_all(value, axis, split_axis=0, concat_axis=0, tiled=True)  3.87 us
    pallas_call x1, Pallas kernels, invert(): pl.pallas_call(invert_kernel, in_specs=[whole()], out_specs=whole(), out_...  2.76 us
  transfers between devices with their start and end apart: 3, of which 3 were waited for; matrix products, arithmetic and copies ran while one was open for 0% of the time, Pallas kernels for 5%

profile of v2, /device:TPU:1, one launch (start us, length us, event | category | flops | bytes accessed | tf_op | source)
XLA Modules:
  0.0 100.3 jit_solution(375687625718517373)
XLA Ops:
  0.6 4.6 %merge_project.1 = (bf16[2,384,3072]{2,1,0:T(8,128)(2,1)S(1)}, f32[32,8,128]{2,1,0:T(8,128)S(1)}, s32[8,384]{1,0:T(8,128)S(1)}) custom-call(bf16[1,2,384,3072]{3,2,1,0:T(8,128)(2,1)} %gradient.1, bf16[1,2,384,3072]{3,2,1,0:T(8,128)(2,1)} %error.1, f32[2,32,3072]{2,1,0:T(8,128)} %bitcast.8, s32[32]{0:T(128)} %starts.1, s32[32]{0:T(128)} %owners.1), custom_call_target="tpu_custom_call" | custom-call | tf_op jit(solution)/shard_map/merge_project/pallas_call | solution.py:124
  5.3 20.8 %all_to_all.30.pieces = f32[32,8,128]{2,1,0:T(8,128)S(1)} all-to-all(f32[32,8,128]{2,1,0:T(8,128)S(1)} %get-tuple-element.8), channel_id=1, replica_groups=mesh['x'=4,'z'=8,'y'=4,'core'=2] {'x','z'}, dimensions={0} | all-to-all | bytes 262144 | tf_op jit(solution)/shard_map/all_to_all | solution.py:397
  26.1 12.7 %all_to_all.31.tiles = f32[32,8,128]{2,1,0:T(8,128)S(1)} all-to-all(f32[32,8,128]{2,1,0:T(8,128)S(1)} %add_replicas.2), channel_id=1, replica_groups=mesh['x'=4,'z'=8,'y'=4,'core'=2] {'x','z'}, dimensions={0} | all-to-all | bytes 262144 | tf_op jit(solution)/shard_map/all_to_all | solution.py:397
  38.8 1.0 product_other_half.1
  39.8 3.4 %collective-permute-start = (f32[4,28,8,128]{3,2,1,0:T(8,128)S(1)}, f32[4,28,8,128]{3,2,1,0:T(8,128)S(1)}, u32[]{:S(2)}, u32[]{:S(2)}) collective-permute-start(f32[4,28,8,128]{3,2,1,0:T(8,128)S(1)} %product_other_half.1), channel_id=1, source_target_pairs={{0,1},{1,0},{2,3},{3,2},{4,5},{5,4},{6,7},{7,6},{8,9},{9,8},{10,11... | collective-permute-start | bytes 1376264 | tf_op jit(solution)/shard_map/ppermute | solution.py:401
  43.2 0.9 product_own_half.1.mine
  44.1 0.5 collective-permute-done.other
  44.6 0.1 add_cores.1
  44.7 12.2 %all_to_all.32.pieces = f32[4,28,8,128]{3,2,1,0:T(8,128)S(1)} all-to-all(f32[4,28,8,128]{3,2,1,0:T(8,128)S(1)} %add_cores.1), channel_id=1, replica_groups=mesh['x'=4,'z'=8,'y'=4,'core'=2] {'y'}, dimensions={0} | all-to-all | bytes 917504 | tf_op jit(solution)/shard_map/all_to_all | solution.py:397
  56.9 12.5 %all_to_all.33.pieces = f32[32,8,128]{2,1,0:T(8,128)S(1)} all-to-all(f32[32,8,128]{2,1,0:T(8,128)S(1)} %get-tuple-element.10), channel_id=1, replica_groups=mesh['x'=4,'z'=8,'y'=4,'core'=2] {'x','z'}, dimensions={0} | all-to-all | bytes 262144 | tf_op jit(solution)/shard_map/all_to_all | solution.py:397
  69.4 0.7 add_replicas.3
  70.2 3.9 %all-to-all-start.4 = ((f32[32,2,8,128]{3,2,1,0:T(8,128)}), f32[32,2,8,128]{3,2,1,0:T(8,128)S(1)}, u32[]{:S(2)}, u32[]{:S(2)}) async-start(f32[32,2,8,128]{3,2,1,0:T(8,128)} %add_replicas.3), calls=%async_computation.4 | async-start | bytes 524288 | tf_op jit(solution)/shard_map/all_to_all | solution.py:397
  74.0 2.8 %invert_triangle.1.inverse = f32[2,64,128]{2,1,0:T(8,128)S(1)} custom-call(f32[4,8,128]{2,1,0:T(8,128)S(1)} %get-tuple-element.11.refs_0_.rest), custom_call_target="tpu_custom_call" | custom-call | flops 2000000 | bytes 20000000 | tf_op jit(solution)/shard_map/invert_triangle/pallas_call | solution.py:314
  76.8 6.9 %all-to-all-done.4.tiles = f32[32,2,8,128]{3,2,1,0:T(8,128)S(1)} async-done(((f32[32,2,8,128]{3,2,1,0:T(8,128)}), f32[32,2,8,128]{3,2,1,0:T(8,128)S(1)}, u32[]{:S(2)}, u32[]{:S(2)}) %all-to-all-start.4) | async-done | bytes 262176 | tf_op jit(solution)/shard_map/all_to_all | solution.py:397
  83.7 0.2 apply_right.1
  83.9 8.6 %all_to_all.34.mine = f32[4,64,384]{2,1,0:T(8,128)S(1)} all-to-all(f32[4,64,384]{2,1,0:T(8,128)S(1)} %apply_right.1), channel_id=1, replica_groups=mesh['x'=4,'z'=8,'y'=4,'core'=2] {'y'}, dimensions={0} | all-to-all | bytes 786432 | tf_op jit(solution)/shard_map/all_to_all | solution.py:397
  92.5 5.5 %collective-permute-start.1 = (f32[4,64,384]{2,1,0:T(8,128)S(1)}, f32[4,64,384]{2,1,0:T(8,128)S(1)}, u32[]{:S(2)}, u32[]{:S(2)}) collective-permute-start(f32[4,64,384]{2,1,0:T(8,128)S(1)} %all_to_all.34.mine), channel_id=1, source_target_pairs={{0,1},{1,0},{2,3},{3,2},{4,5},{5,4},{6,7},{7,6},{8,9},{9,8},{10,11... | collective-permute-start | bytes 1179656 | tf_op jit(solution)/shard_map/ppermute | solution.py:401
  98.0 0.9 apply_left.1
  98.9 0.5 collective-permute-done.1.other
  99.4 0.9 assemble_right.1
  (2 shorter events, 0.1 us)
Async XLA Ops:
  39.8 4.9 %collective-permute-start = (f32[4,28,8,128]{3,2,1,0:T(8,128)S(1)}, f32[4,28,8,128]{3,2,1,0:T(8,128)S(1)}, u32[]{:S(2)}, u32[]{:S(2)}) collective-permute-start(f32[4,28,8,128]{3,2,1,0:T(8,128)S(1)} %product_other_half.1), channel_id=1, source_target_pairs={{0,1},{1,0},{2,3},{3,2},{4,5},{5,4},{6,7},{7,6},{8,9},{9,8},{10,11... | collective-permute-start | bytes 1376264 | tf_op jit(solution)/shard_map/ppermute | solution.py:401
  70.2 13.5 %all-to-all-start.4 = ((f32[32,2,8,128]{3,2,1,0:T(8,128)}), f32[32,2,8,128]{3,2,1,0:T(8,128)S(1)}, u32[]{:S(2)}, u32[]{:S(2)}) async-start(f32[32,2,8,128]{3,2,1,0:T(8,128)} %add_replicas.3), calls=%async_computation.4 | async-start | bytes 524288 | tf_op jit(solution)/shard_map/all_to_all | solution.py:397
  92.5 6.8 %collective-permute-start.1 = (f32[4,64,384]{2,1,0:T(8,128)S(1)}, f32[4,64,384]{2,1,0:T(8,128)S(1)}, u32[]{:S(2)}, u32[]{:S(2)}) collective-permute-start(f32[4,64,384]{2,1,0:T(8,128)S(1)} %all_to_all.34.mine), channel_id=1, source_target_pairs={{0,1},{1,0},{2,3},{3,2},{4,5},{5,4},{6,7},{7,6},{8,9},{9,8},{10,11... | collective-permute-start | bytes 1179656 | tf_op jit(solution)/shard_map/ppermute | solution.py:401

commit v3 on v2

v3 whole, which is shorter than its diff:
```python
import functools
import math

import jax
import jax.numpy as jnp
from jax import lax
from jax.experimental import pallas as pl
from jax.experimental.pallas import tpu as pltpu
from jax.sharding import PartitionSpec as P

LAYERS = 2
RANK = 32
RANKS = LAYERS * RANK
ROWS = 384
COLS = 3072
HALF = COLS // 2
XS, ZS, YS = 4, 8, 4
PART = RANKS // XS
LEFT, REST = RANKS, RANKS + PART
SENT = REST + 8
CHUNK = 512
CHUNKS = COLS // CHUNK
RUNS = 4
VMEM_LIMIT = 24 * 1024 * 1024
F32 = jnp.float32
BF16 = jnp.bfloat16


def whole(memory_space=pltpu.VMEM):
    return pl.BlockSpec(memory_space=memory_space)


def params(**more):
    return pltpu.CompilerParams(vmem_limit_bytes=VMEM_LIMIT, **more)


def split3(value):
    high = value.astype(BF16)
    rest = value - high.astype(F32)
    middle = rest.astype(BF16)
    low = (rest - middle.astype(F32)).astype(BF16)
    return high, middle, low


def dot_rows(left, right):
    return lax.dot_general(left, right, (((1,), (1,)), ((), ())), preferred_element_type=F32)


def merge_kernel(
    gradient, error, q, starts, owners, merged, partial, dest, g, e, q_in, table, sems, table_sems
):
    tables = [
        pltpu.make_async_copy(source, table.at[i], table_sems.at[i])
        for i, source in enumerate((starts, owners))
    ]
    for copy in tables:
        copy.start()
    copies = []
    for layer in range(LAYERS):
        copies.append([pltpu.make_async_copy(q.at[layer], q_in.at[layer], sems.at[layer, CHUNKS, 0])])
        for chunk in range(CHUNKS):
            columns = pl.ds(chunk * CHUNK, CHUNK)
            copies.append(
                [
                    pltpu.make_async_copy(
                        source.at[0, layer, :, columns],
                        into.at[layer, chunk],
                        sems.at[layer, chunk, i],
                    )
                    for i, (source, into) in enumerate(((gradient, g), (error, e)))
                ]
            )
    for group in copies:
        for copy in group:
            copy.start()
    for copy in tables:
        copy.wait()
    dest[...] = destinations(table)
    arrived = iter(copies)
    for layer in range(LAYERS):
        for copy in next(arrived):
            copy.wait()
        terms = jnp.zeros((RANK, ROWS), F32)
        for chunk in range(CHUNKS):
            for copy in next(arrived):
                copy.wait()
            total = (g[layer, chunk].astype(F32) + e[layer, chunk].astype(F32)).astype(BF16)
            columns = slice(chunk * CHUNK, chunk * CHUNK + CHUNK)
            merged[layer, :, columns] = total
            terms = terms + dot_rows(q_in[layer, :, columns].astype(BF16), total)
        partial[layer * RANK : layer * RANK + RANK] = terms


def destinations(table):
    shard = lax.axis_index("y") * 2 + lax.axis_index("core")
    first = shard * RUNS
    mine = [table[1, first + t] for t in range(RUNS)]

    def count(run, before):
        length = table[0, run + 1] - table[0, run]
        return tuple(b + jnp.where(table[1, run] == o, length, 0) for b, o in zip(before, mine))

    before = lax.fori_loop(0, first, count, (jnp.int32(0),) * RUNS)
    position = shard * ROWS + lax.broadcasted_iota(jnp.int32, (8, ROWS), 1)
    place = position
    for t in range(RUNS):
        start = table[0, first + t]
        moved = position + (mine[t] * ROWS + before[t] - start)
        place = jnp.where(position >= start, moved, place)
    return place


def merge(gradient, error, q, run_starts, run_owners):
    operands = [
        pltpu.with_memory_space_constraint(value, pltpu.HBM)
        for value in (gradient, error, q, run_starts, run_owners)
    ]
    return pl.pallas_call(
        merge_kernel,
        in_specs=[whole(pltpu.HBM)] * 5,
        out_specs=[whole()] * 3,
        out_shape=[
            pltpu.VMEM((LAYERS, ROWS, COLS), BF16),
            jax.ShapeDtypeStruct((RANKS, ROWS), F32),
            jax.ShapeDtypeStruct((8, ROWS), jnp.int32),
        ],
        scratch_shapes=[
            pltpu.VMEM((LAYERS, CHUNKS, ROWS, CHUNK), BF16),
            pltpu.VMEM((LAYERS, CHUNKS, ROWS, CHUNK), BF16),
            pltpu.VMEM((LAYERS, RANK, COLS), F32),
            pltpu.SMEM((2, 2 * YS * RUNS), jnp.int32),
            pltpu.SemaphoreType.DMA((LAYERS, CHUNKS + 1, 2)),
            pltpu.SemaphoreType.DMA((2,)),
        ],
        compiler_params=params(),
        name="merge_project",
    )(*operands)


def product_kernel(own, dest, factor_in, merged, out):
    at = lax.axis_index("y")
    half = lax.axis_index("core") if own else 1 - lax.axis_index("core")
    factor = factor_in[...]
    biggest = [
        jnp.max(jnp.abs(factor[l * RANK : l * RANK + RANK]), keepdims=True) for l in range(LAYERS)
    ]
    scales = [jnp.where(b > 0, b * 64.0, 1.0) for b in biggest]
    columns = pl.ds(pl.multiple_of(half * HALF, 128), HALF)
    step = [lax.rem(y - at + YS, YS) for y in range(YS)]
    for layer in range(LAYERS):
        ranks = slice(layer * RANK, layer * RANK + RANK)
        parts = jnp.concatenate(split3(factor[ranks] * (1.0 / scales[layer])), axis=0)
        product = jnp.dot(parts, merged[layer, :, columns], preferred_element_type=F32)
        product = product[:RANK] + product[RANK : 2 * RANK] + product[2 * RANK :]
        for y in range(YS):
            out[step[y], ranks] = product[:, y * ROWS : y * ROWS + ROWS]
    first = pl.multiple_of(lax.axis_index("x") * PART, PART)
    rows = jnp.concatenate(split3(factor_in[pl.ds(first, PART)]), axis=0)
    wanted = jnp.broadcast_to(dest[0:1], (ROWS, ROWS)) - lax.broadcasted_iota(
        jnp.int32, (ROWS, ROWS), 0
    )
    for y in range(YS):
        chosen = jnp.where(wanted == (y * 2 + half) * ROWS, 1.0, 0.0).astype(BF16)
        found = dot_rows(rows, chosen)
        out[step[y], LEFT:REST] = found[:PART] + found[PART : 2 * PART] + found[2 * PART :]
    high, middle, low = split3(factor)
    left = jnp.concatenate([high, middle, low], axis=0)
    right = jnp.concatenate([high, high, middle, middle, low, low], axis=0)
    gram = dot_rows(left, right)
    gram = gram[:64] + gram[64:128] + gram[128:]
    gram = gram[:, :128] + gram[:, 128:256] + gram[:, 256:]
    lane = lax.broadcasted_iota(jnp.int32, (RANK, 128), 1)
    gram = jnp.where(lax.rem(lane, 64) < 32, gram[:RANK], gram[RANK:])
    gram = jnp.where(lane[:16] < 64, gram[:16], gram[16:])
    scale = jnp.concatenate([jnp.broadcast_to(s, (4, 128)) for s in scales], axis=0)
    rest = jnp.concatenate([gram[:8], gram[8:], scale], axis=1)
    for k in range(YS):
        out[k, REST:] = rest


def product(own, dest, factor, merged):
    return pl.pallas_call(
        functools.partial(product_kernel, own),
        in_specs=[whole()] * 3,
        out_specs=whole(),
        out_shape=jax.ShapeDtypeStruct((YS, SENT, ROWS), F32),
        compiler_params=params(),
        name="product_own_half" if own else "product_other_half",
    )(dest, factor, pltpu.with_memory_space_constraint(merged, pltpu.VMEM))


def add_scaled(pieces):
    scales = [p[REST:, 256:] for p in pieces]
    largest = functools.reduce(jnp.maximum, scales)
    ratios = [scale / largest for scale in scales]
    products = []
    for layer in range(LAYERS):
        ranks = slice(layer * RANK, layer * RANK + RANK)
        terms = []
        for piece, ratio in zip(pieces, ratios):
            row = jnp.broadcast_to(ratio[4 * layer : 4 * layer + 1], (RANK, 128))
            terms.append(piece[ranks] * jnp.concatenate([row] * (ROWS // 128), axis=1))
        products.append(functools.reduce(jnp.add, terms))
    left = functools.reduce(jnp.add, [p[LEFT:REST] for p in pieces])
    gram = functools.reduce(jnp.add, [p[REST:, :256] for p in pieces])
    return products, left, jnp.concatenate([gram, largest], axis=1)


def store_scaled(pieces, out, rest):
    products, left, last = add_scaled(pieces)
    for layer in range(LAYERS):
        out[layer * RANK : layer * RANK + RANK] = products[layer]
    out[LEFT:REST] = left
    rest[...] = last


def pair_kernel(mine, other, *outs):
    for k, out in enumerate(outs):
        store_scaled([mine.at[k], other.at[k]], out, out.at[REST:])


def pair(mine, other):
    return pl.pallas_call(
        pair_kernel,
        in_specs=[whole(), whole()],
        out_specs=[whole()] * YS,
        out_shape=[jax.ShapeDtypeStruct((SENT, ROWS), F32)] * YS,
        compiler_params=params(),
        name="add_cores",
    )(mine, other)


def line_kernel(a, b, c, d, out, rest):
    store_scaled([a, b, c, d], out, rest)


def line(pieces):
    return pl.pallas_call(
        line_kernel,
        in_specs=[whole()] * YS,
        out_specs=[whole(), whole()],
        out_shape=[
            jax.ShapeDtypeStruct((REST, ROWS), F32),
            jax.ShapeDtypeStruct((SENT - REST, ROWS), F32),
        ],
        compiler_params=params(),
        name="add_line",
    )(*pieces)


def cross_kernel(own, *refs):
    *others, out, left = refs
    pieces = [own, *others]
    out[...] = (own[:LEFT] + others[1][:LEFT]) + (others[0][:LEFT] + others[2][:LEFT])
    for k, piece in enumerate(pieces):
        part = lax.rem(lax.axis_index("x") - k + XS, XS)
        left[pl.ds(pl.multiple_of(part * PART, PART), PART)] = piece[LEFT:REST]


def cross(pieces):
    return pl.pallas_call(
        cross_kernel,
        in_specs=[whole()] * XS,
        out_specs=[whole(), whole()],
        out_shape=[jax.ShapeDtypeStruct((RANKS, ROWS), F32)] * 2,
        compiler_params=params(),
        name="add_cross",
    )(*pieces)


def add_kernel(*refs):
    *pieces, out = refs
    while len(pieces) > 1:
        pieces = [a[...] + b[...] for a, b in zip(pieces[::2], pieces[1::2])]
    out[...] = pieces[0]


def add(*pieces):
    return pl.pallas_call(
        add_kernel,
        in_specs=[whole()] * len(pieces),
        out_specs=whole(),
        out_shape=jax.ShapeDtypeStruct((RANKS, ROWS), F32),
        compiler_params=params(),
        name="add_pieces",
    )(*pieces)


def invert_kernel(rest, out):
    packed = jnp.concatenate([rest[:, :128], rest[:, 128:256]], axis=0)
    turned = pltpu.roll(packed, 64, 1)
    row = lax.broadcasted_iota(jnp.int32, (RANK, 128), 0)
    lane = lax.broadcasted_iota(jnp.int32, (RANK, 128), 1)
    gram = jnp.concatenate([packed, turned], axis=0)
    unit = jnp.where(row == lax.rem(lane, RANK), 1.0, 0.0)
    work = jnp.where(lane < 64, gram, unit)
    first = lax.rem(lane, 64) < RANK
    for step in range(RANK - 1):
        column = jnp.where(
            first,
            jnp.broadcast_to(work[:, step : step + 1], (RANK, 128)),
            jnp.broadcast_to(work[:, RANK + step : RANK + step + 1], (RANK, 128)),
        )
        pivot = work[step : step + 1] / column[step : step + 1]
        work = work - jnp.where(row > step, column, 0.0) * pivot
    diagonal = [
        jnp.sum(jnp.where(lane == row + l * RANK, work, 0.0), axis=1, keepdims=True)
        for l in range(LAYERS)
    ]
    root = jnp.where(
        first,
        jnp.broadcast_to(diagonal[0], (RANK, 128)),
        jnp.broadcast_to(diagonal[1], (RANK, 128)),
    )
    inverse = pltpu.roll(work / jnp.sqrt(root), 64, 1)
    left = jnp.concatenate(
        [jnp.where(lane < RANK, inverse, 0.0), jnp.where((lane >= RANK) & (lane < 64), inverse, 0.0)],
        axis=0,
    )
    scale = rest[:, 256:]
    out[0] = jnp.concatenate([left[:RANK] * scale[0:1], left[RANK:] * scale[4:5]], axis=0)
    out[1] = left * math.sqrt(COLS)


def invert(rest):
    return pl.pallas_call(
        invert_kernel,
        in_specs=[whole()],
        out_specs=whole(),
        out_shape=jax.ShapeDtypeStruct((2, 64, 128), F32),
        compiler_params=params(),
        cost_estimate=pl.CostEstimate(flops=2_000_000, bytes_accessed=20_000_000, transcendentals=0),
        name="invert_triangle",
    )(rest)


def apply_kernel(which, rows, inverse, out):
    out[...] = jnp.dot(
        inverse[which][:, :RANKS],
        rows[...],
        precision=lax.Precision.HIGHEST,
        preferred_element_type=F32,
    )


def apply(which, rows, inverse):
    return pl.pallas_call(
        functools.partial(apply_kernel, which),
        in_specs=[whole(), whole()],
        out_specs=whole(),
        out_shape=jax.ShapeDtypeStruct((RANKS, ROWS), F32),
        compiler_params=params(),
        name="apply_left" if which else "apply_right",
    )(rows, inverse)


def assemble_kernel(*refs):
    *pieces, out, sems = refs
    core, at = lax.axis_index("core"), lax.axis_index("y")
    copies = []
    for i, piece in enumerate(pieces):
        half = core if i < YS else 1 - core
        block = lax.rem(at - i % YS + YS, YS)
        columns = pl.ds(pl.multiple_of(half * HALF + block * ROWS, 128), ROWS)
        copies.append(pltpu.make_async_copy(piece, out.at[:, columns], sems.at[i]))
    for copy in copies:
        copy.start()
    for copy in copies:
        copy.wait()


def assemble(pieces):
    return pl.pallas_call(
        assemble_kernel,
        in_specs=[whole()] * (2 * YS),
        out_specs=whole(pltpu.HBM),
        out_shape=jax.ShapeDtypeStruct((RANKS, COLS), F32),
        scratch_shapes=[pltpu.SemaphoreType.DMA((2 * YS,))],
        compiler_params=params(),
        name="assemble_right",
    )(*pieces)


def swap(value):
    return lax.ppermute(value, "core", [(0, 1), (1, 0)])


def rotate(value, axis, step):
    size = lax.axis_size(axis)
    return lax.ppermute(value, axis, [(i, (i + step) % size) for i in range(size)])


def along_z(value, even, odd):
    sources = [(z + (odd if z % 2 else even)) % ZS for z in range(ZS)]
    return lax.ppermute(value, "z", [(source, z) for z, source in enumerate(sources)])


def sum_z(value):
    value = add(value, along_z(value, 1, -1))
    return add(value, along_z(value, -3, 3), along_z(value, -1, 1), along_z(value, 2, -2))


def shards(gradient, error_buffer, previous_q, run_starts, run_owners):
    q = jnp.swapaxes(previous_q, 1, 2)
    merged, partial, dest = merge(gradient, error_buffer, q, run_starts, run_owners)
    far, near, back = [rotate(partial, "x", step) for step in (2, 1, 3)]
    factor = sum_z(add(partial, far, near, back))
    sent = swap(product(False, dest, factor, merged))
    pieces = pair(product(True, dest, factor, merged), sent)
    pieces = [pieces[0]] + [rotate(pieces[k], "y", k) for k in range(1, YS)]
    terms, rest = line(pieces)
    inverse = invert(rest)
    terms, rows = cross([terms] + [rotate(terms, "x", k) for k in range(1, XS)])
    right = apply(0, sum_z(terms), inverse)
    left = apply(1, rows, inverse)
    right = [right] + [rotate(right, "y", k) for k in range(1, YS)]
    right = assemble(right + [swap(value) for value in right])
    shape = (LAYERS, RANK, -1)
    return tuple(jnp.swapaxes(value.reshape(shape), 1, 2) for value in (left, right))


def solution(mesh):
    grid = jax.sharding.Mesh(mesh.devices.reshape(XS, ZS, YS, 2), ("x", "z", "y", "core"))
    rep, shard = ("x", "z"), ("y", "core")
    return jax.shard_map(
        shards,
        mesh=grid,
        in_specs=(P(rep, None, shard, None), P(rep, None, shard, None), P(), P(), P()),
        out_specs=(P(None, shard, None), P()),
        check_vma=False,
    )
```

time: 101 us -> 90.3 us (0.89)
  blocking collectives: 66.8 us -> 0 us
  starting transfers between devices: 12.8 us -> 48.3 us
  waiting for transfers between devices: 7.85 us -> 29 us
    all_to_all x5 -> x0, blocking collectives: 66.8 us -> none  [exchange(): return lax.all_to_all(value, axis, split_axis=0, concat_axis=0, tiled=True)]
    ppermute x0 -> x20, starting transfers between devices: none -> 33.6 us  [the longest x8 18.1 us: along_z(): lax.ppermute(value, 'z', [(source, z) for z, source in enumerate(sources)])]
    ppermute x0 -> x20, waiting for transfers between devices: none -> 28.6 us  [the longest x12 17.3 us: rotate(): lax.ppermute(value, axis, [(i, (i + step) % size) for i in range(size)])]
    all_to_all x1 -> x0, waiting for transfers between devices: 6.88 us -> none  [exchange(): return lax.all_to_all(value, axis, split_axis=0, concat_axis=0, tiled=True)]
    ppermute x2 -> x5, starting transfers between devices: 8.89 us -> 14.7 us  [swap(): return lax.ppermute(value, 'core', [(0, 1), (1, 0)])]
    all_to_all x1 -> x0, starting transfers between devices: 3.87 us -> none  [exchange(): return lax.all_to_all(value, axis, split_axis=0, concat_axis=0, tiled=True)]
  transfers between devices with their start and end apart: 3 -> 25, of which waited for: 3 -> 13; matrix products, arithmetic and copies ran while one was open for 0% -> 0% of each run, Pallas kernels for 5% -> 5%
where the time goes in v3:
time: 90.3 us; the launch traced here: 90.2 us
  starting transfers between devices  48.3 us (53%)
  waiting for transfers between devices  29 us (32%)
  Pallas kernels  12 us (13%)
    ppermute x8, starting transfers between devices, along_z(): lax.ppermute(value, 'z', [(source, z) for z, source in enumerate(sources)])  18.1 us
    ppermute x12, waiting for transfers between devices, rotate(): lax.ppermute(value, axis, [(i, (i + step) % size) for i in range(size)])  17.3 us
    ppermute x12, starting transfers between devices, rotate(): lax.ppermute(value, axis, [(i, (i + step) % size) for i in range(size)])  15.4 us
    ppermute x5, starting transfers between devices, swap(): return lax.ppermute(value, 'core', [(0, 1), (1, 0)])  14.7 us
    ppermute x8, waiting for transfers between devices, along_z(): lax.ppermute(value, 'z', [(source, z) for z, source in enumerate(sources)])  11.2 us
    pallas_call x1, Pallas kernels, merge(): pl.pallas_call(merge_kernel, in_specs=[whole(pltpu.HBM)] * 5, out_specs=[...  4.62 us
    pallas_call x1, Pallas kernels, invert(): pl.pallas_call(invert_kernel, in_specs=[whole()], out_specs=whole(), out_...  2.76 us
    pallas_call x2, Pallas kernels, product(): pl.pallas_call(functools.partial(product_kernel, own), in_specs=[whole()]...  2.29 us
  transfers between devices with their start and end apart: 25, of which 13 were waited for; matrix products, arithmetic and copies ran while one was open for 0% of the time, Pallas kernels for 5%

profile of v3, /device:TPU:1, one launch (start us, length us, event | category | flops | bytes accessed | tf_op | source)
XLA Modules:
  0.0 90.2 jit_solution(17361329628242947496)
XLA Ops:
  0.6 4.6 %merge_project.1 = (bf16[2,384,3072]{2,1,0:T(8,128)(2,1)S(1)}, f32[64,384]{1,0:T(8,128)S(1)}, s32[8,384]{1,0:T(8,128)S(1)}) custom-call(bf16[1,2,384,3072]{3,2,1,0:T(8,128)(2,1)} %gradient.1, bf16[1,2,384,3072]{3,2,1,0:T(8,128)(2,1)} %error.1, f32[2,32,3072]{2,1,0:T(8,128)} %bitcast.8, s32[32]{0:T(128)} %starts.1, s32[32]{0:T(128)} %owners.1), custom_call_target="tpu_custom_call" | custom-call | tf_op jit(solution)/shard_map/merge_project/pallas_call | solution.py:118
  5.3 3.4 %collective-permute-start.2 = (f32[64,384]{1,0:T(8,128)S(1)}, f32[64,384]{1,0:T(8,128)S(1)}, u32[]{:S(2)}, u32[]{:S(2)}) collective-permute-start(f32[64,384]{1,0:T(8,128)S(1)} %get-tuple-element.14.refs_0_), channel_id=1, source_target_pairs={{0,192},{64,0},{128,64},{192,128},{1,193},{65,1},{129,65},{193,129... | collective-permute-start | bytes 294920 | tf_op jit(solution)/shard_map/ppermute | solution.py:390
  8.6 0.0 collective-permute-start.1
  8.7 1.7 %collective-permute-start = (f32[64,384]{1,0:T(8,128)S(1)}, f32[64,384]{1,0:T(8,128)S(1)}, u32[]{:S(2)}, u32[]{:S(2)}) collective-permute-start(f32[64,384]{1,0:T(8,128)S(1)} %get-tuple-element.14.refs_0_), channel_id=1, source_target_pairs={{0,128},{64,192},{128,0},{192,64},{1,129},{65,193},{129,1},{193,65... | collective-permute-start | bytes 294920 | tf_op jit(solution)/shard_map/ppermute | solution.py:390
  10.4 4.5 %collective-permute-done.1.refs_2_ = f32[64,384]{1,0:T(8,128)S(1)} collective-permute-done((f32[64,384]{1,0:T(8,128)S(1)}, f32[64,384]{1,0:T(8,128)S(1)}, u32[]{:S(2)}, u32[]{:S(2)}) %collective-permute-start.1) | collective-permute-done | bytes 98336 | tf_op jit(solution)/shard_map/ppermute | solution.py:390
  14.9 0.0 collective-permute-done.refs_1_
  14.9 1.7 %collective-permute-start.3 = (f32[64,384]{1,0:T(8,128)S(1)}, f32[64,384]{1,0:T(8,128)S(1)}, u32[]{:S(2)}, u32[]{:S(2)}) collective-permute-start(f32[64,384]{1,0:T(8,128)S(1)} %add_pieces.5.refs_0_), channel_id=1, source_target_pairs={{8,0},{0,8},{24,16},{16,24},{40,32},{32,40},{56,48},{48,56},{9,1},... | collective-permute-start | bytes 294920 | tf_op jit(solution)/shard_map/ppermute | solution.py:395
  16.7 2.0 %collective-permute-done.3.refs_1_ = f32[64,384]{1,0:T(8,128)S(1)} collective-permute-done((f32[64,384]{1,0:T(8,128)S(1)}, f32[64,384]{1,0:T(8,128)S(1)}, u32[]{:S(2)}, u32[]{:S(2)}) %collective-permute-start.3) | collective-permute-done | bytes 98336 | tf_op jit(solution)/shard_map/ppermute | solution.py:395
  18.7 5.9 %collective-permute-start.6 = (f32[64,384]{1,0:T(8,128)S(1)}, f32[64,384]{1,0:T(8,128)S(1)}, u32[]{:S(2)}, u32[]{:S(2)}) collective-permute-start(f32[64,384]{1,0:T(8,128)S(1)} %add_pieces.6.refs_0_), channel_id=1, source_target_pairs={{16,0},{56,8},{32,16},{8,24},{48,32},{24,40},{0,48},{40,56},{17,1}... | collective-permute-start | bytes 294920 | tf_op jit(solution)/shard_map/ppermute | solution.py:395
  24.6 2.4 %collective-permute-start.4 = (f32[64,384]{1,0:T(8,128)S(1)}, f32[64,384]{1,0:T(8,128)S(1)}, u32[]{:S(2)}, u32[]{:S(2)}) collective-permute-start(f32[64,384]{1,0:T(8,128)S(1)} %add_pieces.6.refs_0_), channel_id=1, source_target_pairs={{40,0},{32,8},{56,16},{48,24},{8,32},{0,40},{24,48},{16,56},{41,1}... | collective-permute-start | bytes 294920 | tf_op jit(solution)/shard_map/ppermute | solution.py:395
  27.0 2.9 %collective-permute-done.5.refs_2_ = f32[64,384]{1,0:T(8,128)S(1)} collective-permute-done((f32[64,384]{1,0:T(8,128)S(1)}, f32[64,384]{1,0:T(8,128)S(1)}, u32[]{:S(2)}, u32[]{:S(2)}) %collective-permute-start.5) | collective-permute-done | bytes 98336 | tf_op jit(solution)/shard_map/ppermute | solution.py:395
  29.9 1.3 %collective-permute-done.4.refs_1_ = f32[64,384]{1,0:T(8,128)S(1)} collective-permute-done((f32[64,384]{1,0:T(8,128)S(1)}, f32[64,384]{1,0:T(8,128)S(1)}, u32[]{:S(2)}, u32[]{:S(2)}) %collective-permute-start.4) | collective-permute-done | bytes 98336 | tf_op jit(solution)/shard_map/ppermute | solution.py:395
  31.2 1.1 %product_other_half.1 = f32[4,88,384]{2,1,0:T(8,128)S(1)} custom-call(s32[8,384]{1,0:T(8,128)S(1)} %get-tuple-element.13.dest, f32[64,384]{1,0:T(8,128)S(1)} %add_pieces.7.factor_in, bf16[2,384,3072]{2,1,0:T(8,128)(2,1)S(1)} %get-tuple-element.15.merged), custom_call_target="tpu_custom_call" | custom-call | tf_op jit(solution)/shard_map/product_other_half/pallas_call | solution.py:182
  32.4 5.0 %collective-permute-start.7 = (f32[4,88,384]{2,1,0:T(8,128)S(1)}, f32[4,88,384]{2,1,0:T(8,128)S(1)}, u32[]{:S(2)}, u32[]{:S(2)}) collective-permute-start(f32[4,88,384]{2,1,0:T(8,128)S(1)} %product_other_half.1), channel_id=1, source_target_pairs={{0,1},{1,0},{2,3},{3,2},{4,5},{5,4},{6,7},{7,6},{8,9},{9,8},{10,11... | collective-permute-start | bytes 1622024 | tf_op jit(solution)/shard_map/ppermute | solution.py:385
  37.3 1.1 %product_own_half.1.mine = f32[4,88,384]{2,1,0:T(8,128)S(1)} custom-call(s32[8,384]{1,0:T(8,128)S(1)} %get-tuple-element.13.dest, f32[64,384]{1,0:T(8,128)S(1)} %add_pieces.7.factor_in, bf16[2,384,3072]{2,1,0:T(8,128)(2,1)S(1)} %get-tuple-element.15.merged), custom_call_target="tpu_custom_call" | custom-call | tf_op jit(solution)/shard_map/product_own_half/pallas_call | solution.py:182
  38.5 0.4 collective-permute-done.7.other
  38.9 0.1 add_cores.1
  39.0 1.4 %collective-permute-start.8 = (f32[88,384]{1,0:T(8,128)S(1)}, f32[88,384]{1,0:T(8,128)S(1)}, u32[]{:S(2)}, u32[]{:S(2)}) collective-permute-start(f32[88,384]{1,0:T(8,128)S(1)} %get-tuple-element.17), channel_id=1, source_target_pairs={{0,2},{2,4},{4,6},{6,0},{1,3},{3,5},{5,7},{7,1},{8,10},{10,12},{12... | collective-permute-start | bytes 405512 | tf_op jit(solution)/shard_map/ppermute | solution.py:390
  40.4 2.6 %collective-permute-start.9 = (f32[88,384]{1,0:T(8,128)S(1)}, f32[88,384]{1,0:T(8,128)S(1)}, u32[]{:S(2)}, u32[]{:S(2)}) collective-permute-start(f32[88,384]{1,0:T(8,128)S(1)} %get-tuple-element.18), channel_id=1, source_target_pairs={{0,4},{2,6},{4,0},{6,2},{1,5},{3,7},{5,1},{7,3},{8,12},{10,14},{12... | collective-permute-start | bytes 405512 | tf_op jit(solution)/shard_map/ppermute | solution.py:390
  43.0 1.1 %collective-permute-start.10 = (f32[88,384]{1,0:T(8,128)S(1)}, f32[88,384]{1,0:T(8,128)S(1)}, u32[]{:S(2)}, u32[]{:S(2)}) collective-permute-start(f32[88,384]{1,0:T(8,128)S(1)} %get-tuple-element.19), channel_id=1, source_target_pairs={{0,6},{2,0},{4,2},{6,4},{1,7},{3,1},{5,3},{7,5},{8,14},{10,8},{12,... | collective-permute-start | bytes 405512 | tf_op jit(solution)/shard_map/ppermute | solution.py:390
  44.0 1.2 %collective-permute-done.8.b = f32[88,384]{1,0:T(8,128)S(1)} collective-permute-done((f32[88,384]{1,0:T(8,128)S(1)}, f32[88,384]{1,0:T(8,128)S(1)}, u32[]{:S(2)}, u32[]{:S(2)}) %collective-permute-start.8) | collective-permute-done | bytes 135200 | tf_op jit(solution)/shard_map/ppermute | solution.py:390
  45.2 4.0 %collective-permute-done.9.c = f32[88,384]{1,0:T(8,128)S(1)} collective-permute-done((f32[88,384]{1,0:T(8,128)S(1)}, f32[88,384]{1,0:T(8,128)S(1)}, u32[]{:S(2)}, u32[]{:S(2)}) %collective-permute-start.9) | collective-permute-done | bytes 135200 | tf_op jit(solution)/shard_map/ppermute | solution.py:390
  49.2 0.1 add_line.1
  49.3 1.6 %collective-permute-start.13 = (f32[80,384]{1,0:T(8,128)S(1)}, f32[80,384]{1,0:T(8,128)S(1)}, u32[]{:S(2)}, u32[]{:S(2)}) collective-permute-start(f32[80,384]{1,0:T(8,128)S(1)} %get-tuple-element.20.own), channel_id=1, source_target_pairs={{0,192},{64,0},{128,64},{192,128},{1,193},{65,1},{129,65},{193,129... | collective-permute-start | bytes 368648 | tf_op jit(solution)/shard_map/ppermute | solution.py:390
  50.8 0.0 collective-permute-start.12
  50.8 0.9 collective-permute-start.11
  51.7 1.4 %collective-permute-done.13.refs_2_ = f32[80,384]{1,0:T(8,128)S(1)} collective-permute-done((f32[80,384]{1,0:T(8,128)S(1)}, f32[80,384]{1,0:T(8,128)S(1)}, u32[]{:S(2)}, u32[]{:S(2)}) %collective-permute-start.13) | collective-permute-done | bytes 122912 | tf_op jit(solution)/shard_map/ppermute | solution.py:390
  53.1 3.1 %collective-permute-done.12.refs_1_ = f32[80,384]{1,0:T(8,128)S(1)} collective-permute-done((f32[80,384]{1,0:T(8,128)S(1)}, f32[80,384]{1,0:T(8,128)S(1)}, u32[]{:S(2)}, u32[]{:S(2)}) %collective-permute-start.12) | collective-permute-done | bytes 122912 | tf_op jit(solution)/shard_map/ppermute | solution.py:390
  56.2 3.2 %collective-permute-done.11.refs_0_ = f32[80,384]{1,0:T(8,128)S(1)} collective-permute-done((f32[80,384]{1,0:T(8,128)S(1)}, f32[80,384]{1,0:T(8,128)S(1)}, u32[]{:S(2)}, u32[]{:S(2)}) %collective-permute-start.11) | collective-permute-done | bytes 122912 | tf_op jit(solution)/shard_map/ppermute | solution.py:390
  59.4 1.9 %collective-permute-start.14 = (f32[64,384]{1,0:T(8,128)S(1)}, f32[64,384]{1,0:T(8,128)S(1)}, u32[]{:S(2)}, u32[]{:S(2)}) collective-permute-start(f32[64,384]{1,0:T(8,128)S(1)} %get-tuple-element.23.refs_0_), channel_id=1, source_target_pairs={{8,0},{0,8},{24,16},{16,24},{40,32},{32,40},{56,48},{48,56},{9,1},... | collective-permute-start | bytes 294920 | tf_op jit(solution)/shard_map/ppermute | solution.py:395
  61.2 2.0 %collective-permute-done.14.refs_1_ = f32[64,384]{1,0:T(8,128)S(1)} collective-permute-done((f32[64,384]{1,0:T(8,128)S(1)}, f32[64,384]{1,0:T(8,128)S(1)}, u32[]{:S(2)}, u32[]{:S(2)}) %collective-permute-start.14) | collective-permute-done | bytes 98336 | tf_op jit(solution)/shard_map/ppermute | solution.py:395
  63.3 3.2 %collective-permute-start.17 = (f32[64,384]{1,0:T(8,128)S(1)}, f32[64,384]{1,0:T(8,128)S(1)}, u32[]{:S(2)}, u32[]{:S(2)}) collective-permute-start(f32[64,384]{1,0:T(8,128)S(1)} %add_pieces.8.refs_0_), channel_id=1, source_target_pairs={{16,0},{56,8},{32,16},{8,24},{48,32},{24,40},{0,48},{40,56},{17,1}... | collective-permute-start | bytes 294920 | tf_op jit(solution)/shard_map/ppermute | solution.py:395
  66.4 0.8 collective-permute-start.16
  67.2 2.3 %collective-permute-start.15 = (f32[64,384]{1,0:T(8,128)S(1)}, f32[64,384]{1,0:T(8,128)S(1)}, u32[]{:S(2)}, u32[]{:S(2)}) collective-permute-start(f32[64,384]{1,0:T(8,128)S(1)} %add_pieces.8.refs_0_), channel_id=1, source_target_pairs={{40,0},{32,8},{56,16},{48,24},{8,32},{0,40},{24,48},{16,56},{41,1}... | collective-permute-start | bytes 294920 | tf_op jit(solution)/shard_map/ppermute | solution.py:395
  69.5 2.8 %invert_triangle.1.inverse = f32[2,64,128]{2,1,0:T(8,128)S(1)} custom-call(f32[8,384]{1,0:T(8,128)S(1)} %get-tuple-element.22.rest), custom_call_target="tpu_custom_call" | custom-call | flops 2000000 | bytes 20000000 | tf_op jit(solution)/shard_map/invert_triangle/pallas_call | solution.py:326
  72.3 0.0 collective-permute-done.17.refs_3_
  72.3 3.0 %collective-permute-done.15.refs_1_ = f32[64,384]{1,0:T(8,128)S(1)} collective-permute-done((f32[64,384]{1,0:T(8,128)S(1)}, f32[64,384]{1,0:T(8,128)S(1)}, u32[]{:S(2)}, u32[]{:S(2)}) %collective-permute-start.15) | collective-permute-done | bytes 98336 | tf_op jit(solution)/shard_map/ppermute | solution.py:395
  75.3 0.2 apply_right.1.refs_0_
  75.6 2.2 %collective-permute-start.20 = (f32[64,384]{1,0:T(8,128)S(1)}, f32[64,384]{1,0:T(8,128)S(1)}, u32[]{:S(2)}, u32[]{:S(2)}) collective-permute-start(f32[64,384]{1,0:T(8,128)S(1)} %apply_right.1.refs_0_), channel_id=1, source_target_pairs={{0,6},{2,0},{4,2},{6,4},{1,7},{3,1},{5,3},{7,5},{8,14},{10,8},{12,... | collective-permute-start | bytes 294920 | tf_op jit(solution)/shard_map/ppermute | solution.py:390
  77.7 0.6 collective-permute-start.19
  78.4 0.0 collective-permute-start.18
  78.4 3.6 %collective-permute-start.21 = (f32[64,384]{1,0:T(8,128)S(1)}, f32[64,384]{1,0:T(8,128)S(1)}, u32[]{:S(2)}, u32[]{:S(2)}) collective-permute-start(f32[64,384]{1,0:T(8,128)S(1)} %apply_right.1.refs_0_), channel_id=1, source_target_pairs={{0,1},{1,0},{2,3},{3,2},{4,5},{5,4},{6,7},{7,6},{8,9},{9,8},{10,11... | collective-permute-start | bytes 294920 | tf_op jit(solution)/shard_map/ppermute | solution.py:385
  82.0 2.2 %collective-permute-start.24 = (f32[64,384]{1,0:T(8,128)S(1)}, f32[64,384]{1,0:T(8,128)S(1)}, u32[]{:S(2)}, u32[]{:S(2)}) collective-permute-start(f32[64,384]{1,0:T(8,128)S(1)} %collective-permute-done.20.refs_3_), channel_id=1, source_target_pairs={{0,1},{1,0},{2,3},{3,2},{4,5},{5,4},{6,7},{7,6},{8,9},{9,8},{10,11... | collective-permute-start | bytes 294920 | tf_op jit(solution)/shard_map/ppermute | solution.py:385
  84.2 2.9 %collective-permute-start.23 = (f32[64,384]{1,0:T(8,128)S(1)}, f32[64,384]{1,0:T(8,128)S(1)}, u32[]{:S(2)}, u32[]{:S(2)}) collective-permute-start(f32[64,384]{1,0:T(8,128)S(1)} %collective-permute-done.19.refs_2_), channel_id=1, source_target_pairs={{0,1},{1,0},{2,3},{3,2},{4,5},{5,4},{6,7},{7,6},{8,9},{9,8},{10,11... | collective-permute-start | bytes 294920 | tf_op jit(solution)/shard_map/ppermute | solution.py:385
  87.2 1.0 %collective-permute-start.22 = (f32[64,384]{1,0:T(8,128)S(1)}, f32[64,384]{1,0:T(8,128)S(1)}, u32[]{:S(2)}, u32[]{:S(2)}) collective-permute-start(f32[64,384]{1,0:T(8,128)S(1)} %collective-permute-done.18.refs_1_), channel_id=1, source_target_pairs={{0,1},{1,0},{2,3},{3,2},{4,5},{5,4},{6,7},{7,6},{8,9},{9,8},{10,11... | collective-permute-start | bytes 294920 | tf_op jit(solution)/shard_map/ppermute | solution.py:385
  88.2 0.9 apply_left.1
  89.1 0.1 collective-permute-done.22.refs_5_
  89.1 0.9 %assemble_right.1 = f32[64,3072]{1,0:T(8,128)} custom-call(f32[64,384]{1,0:T(8,128)S(1)} %apply_right.1.refs_0_, f32[64,384]{1,0:T(8,128)S(1)} %collective-permute-done.18.refs_1_, f32[64,384]{1,0:T(8,128)S(1)} %collective-permute-done.19.refs_2_, f32[64,384]{1,0:T(8,128)S(1)} %collective-permute-done.20.refs_3_, ...), custom_call_target="tpu_custom_call" | custom-call | tf_op jit(solution)/shard_map/assemble_right/pallas_call | solution.py:373
  (17 shorter events, 0.1 us)
Async XLA Ops:
  5.3 5.1 %collective-permute-start.2 = (f32[64,384]{1,0:T(8,128)S(1)}, f32[64,384]{1,0:T(8,128)S(1)}, u32[]{:S(2)}, u32[]{:S(2)}) collective-permute-start(f32[64,384]{1,0:T(8,128)S(1)} %get-tuple-element.14.refs_0_), channel_id=1, source_target_pairs={{0,192},{64,0},{128,64},{192,128},{1,193},{65,1},{129,65},{193,129... | collective-permute-start | bytes 294920 | tf_op jit(solution)/shard_map/ppermute | solution.py:390
  8.6 6.3 %collective-permute-start.1 = (f32[64,384]{1,0:T(8,128)S(1)}, f32[64,384]{1,0:T(8,128)S(1)}, u32[]{:S(2)}, u32[]{:S(2)}) collective-permute-start(f32[64,384]{1,0:T(8,128)S(1)} %get-tuple-element.14.refs_0_), channel_id=1, source_target_pairs={{0,64},{64,128},{128,192},{192,0},{1,65},{65,129},{129,193},{193,1... | collective-permute-start | bytes 294920 | tf_op jit(solution)/shard_map/ppermute | solution.py:390
  8.7 6.3 %collective-permute-start = (f32[64,384]{1,0:T(8,128)S(1)}, f32[64,384]{1,0:T(8,128)S(1)}, u32[]{:S(2)}, u32[]{:S(2)}) collective-permute-start(f32[64,384]{1,0:T(8,128)S(1)} %get-tuple-element.14.refs_0_), channel_id=1, source_target_pairs={{0,128},{64,192},{128,0},{192,64},{1,129},{65,193},{129,1},{193,65... | collective-permute-start | bytes 294920 | tf_op jit(solution)/shard_map/ppermute | solution.py:390
  14.9 3.7 %collective-permute-start.3 = (f32[64,384]{1,0:T(8,128)S(1)}, f32[64,384]{1,0:T(8,128)S(1)}, u32[]{:S(2)}, u32[]{:S(2)}) collective-permute-start(f32[64,384]{1,0:T(8,128)S(1)} %add_pieces.5.refs_0_), channel_id=1, source_target_pairs={{8,0},{0,8},{24,16},{16,24},{40,32},{32,40},{56,48},{48,56},{9,1},... | collective-permute-start | bytes 294920 | tf_op jit(solution)/shard_map/ppermute | solution.py:395
  18.7 8.3 %collective-permute-start.6 = (f32[64,384]{1,0:T(8,128)S(1)}, f32[64,384]{1,0:T(8,128)S(1)}, u32[]{:S(2)}, u32[]{:S(2)}) collective-permute-start(f32[64,384]{1,0:T(8,128)S(1)} %add_pieces.6.refs_0_), channel_id=1, source_target_pairs={{16,0},{56,8},{32,16},{8,24},{48,32},{24,40},{0,48},{40,56},{17,1}... | collective-permute-start | bytes 294920 | tf_op jit(solution)/shard_map/ppermute | solution.py:395
  24.6 5.3 %collective-permute-start.5 = (f32[64,384]{1,0:T(8,128)S(1)}, f32[64,384]{1,0:T(8,128)S(1)}, u32[]{:S(2)}, u32[]{:S(2)}) collective-permute-start(f32[64,384]{1,0:T(8,128)S(1)} %add_pieces.6.refs_0_), channel_id=1, source_target_pairs={{56,0},{16,8},{8,16},{32,24},{24,32},{48,40},{40,48},{0,56},{57,1}... | collective-permute-start | bytes 294920 | tf_op jit(solution)/shard_map/ppermute | solution.py:395
  24.6 6.6 %collective-permute-start.4 = (f32[64,384]{1,0:T(8,128)S(1)}, f32[64,384]{1,0:T(8,128)S(1)}, u32[]{:S(2)}, u32[]{:S(2)}) collective-permute-start(f32[64,384]{1,0:T(8,128)S(1)} %add_pieces.6.refs_0_), channel_id=1, source_target_pairs={{40,0},{32,8},{56,16},{48,24},{8,32},{0,40},{24,48},{16,56},{41,1}... | collective-permute-start | bytes 294920 | tf_op jit(solution)/shard_map/ppermute | solution.py:395
  32.4 6.5 %collective-permute-start.7 = (f32[4,88,384]{2,1,0:T(8,128)S(1)}, f32[4,88,384]{2,1,0:T(8,128)S(1)}, u32[]{:S(2)}, u32[]{:S(2)}) collective-permute-start(f32[4,88,384]{2,1,0:T(8,128)S(1)} %product_other_half.1), channel_id=1, source_target_pairs={{0,1},{1,0},{2,3},{3,2},{4,5},{5,4},{6,7},{7,6},{8,9},{9,8},{10,11... | collective-permute-start | bytes 1622024 | tf_op jit(solution)/shard_map/ppermute | solution.py:385
  39.0 6.2 %collective-permute-start.8 = (f32[88,384]{1,0:T(8,128)S(1)}, f32[88,384]{1,0:T(8,128)S(1)}, u32[]{:S(2)}, u32[]{:S(2)}) collective-permute-start(f32[88,384]{1,0:T(8,128)S(1)} %get-tuple-element.17), channel_id=1, source_target_pairs={{0,2},{2,4},{4,6},{6,0},{1,3},{3,5},{5,7},{7,1},{8,10},{10,12},{12... | collective-permute-start | bytes 405512 | tf_op jit(solution)/shard_map/ppermute | solution.py:390
  40.4 8.8 %collective-permute-start.9 = (f32[88,384]{1,0:T(8,128)S(1)}, f32[88,384]{1,0:T(8,128)S(1)}, u32[]{:S(2)}, u32[]{:S(2)}) collective-permute-start(f32[88,384]{1,0:T(8,128)S(1)} %get-tuple-element.18), channel_id=1, source_target_pairs={{0,4},{2,6},{4,0},{6,2},{1,5},{3,7},{5,1},{7,3},{8,12},{10,14},{12... | collective-permute-start | bytes 405512 | tf_op jit(solution)/shard_map/ppermute | solution.py:390
  43.0 6.2 %collective-permute-start.10 = (f32[88,384]{1,0:T(8,128)S(1)}, f32[88,384]{1,0:T(8,128)S(1)}, u32[]{:S(2)}, u32[]{:S(2)}) collective-permute-start(f32[88,384]{1,0:T(8,128)S(1)} %get-tuple-element.19), channel_id=1, source_target_pairs={{0,6},{2,0},{4,2},{6,4},{1,7},{3,1},{5,3},{7,5},{8,14},{10,8},{12,... | collective-permute-start | bytes 405512 | tf_op jit(solution)/shard_map/ppermute | solution.py:390
  49.3 3.8 %collective-permute-start.13 = (f32[80,384]{1,0:T(8,128)S(1)}, f32[80,384]{1,0:T(8,128)S(1)}, u32[]{:S(2)}, u32[]{:S(2)}) collective-permute-start(f32[80,384]{1,0:T(8,128)S(1)} %get-tuple-element.20.own), channel_id=1, source_target_pairs={{0,192},{64,0},{128,64},{192,128},{1,193},{65,1},{129,65},{193,129... | collective-permute-start | bytes 368648 | tf_op jit(solution)/shard_map/ppermute | solution.py:390
  50.8 5.3 %collective-permute-start.12 = (f32[80,384]{1,0:T(8,128)S(1)}, f32[80,384]{1,0:T(8,128)S(1)}, u32[]{:S(2)}, u32[]{:S(2)}) collective-permute-start(f32[80,384]{1,0:T(8,128)S(1)} %get-tuple-element.20.own), channel_id=1, source_target_pairs={{0,128},{64,192},{128,0},{192,64},{1,129},{65,193},{129,1},{193,65... | collective-permute-start | bytes 368648 | tf_op jit(solution)/shard_map/ppermute | solution.py:390
  50.8 8.5 %collective-permute-start.11 = (f32[80,384]{1,0:T(8,128)S(1)}, f32[80,384]{1,0:T(8,128)S(1)}, u32[]{:S(2)}, u32[]{:S(2)}) collective-permute-start(f32[80,384]{1,0:T(8,128)S(1)} %get-tuple-element.20.own), channel_id=1, source_target_pairs={{0,64},{64,128},{128,192},{192,0},{1,65},{65,129},{129,193},{193,1... | collective-permute-start | bytes 368648 | tf_op jit(solution)/shard_map/ppermute | solution.py:390
  59.4 3.9 %collective-permute-start.14 = (f32[64,384]{1,0:T(8,128)S(1)}, f32[64,384]{1,0:T(8,128)S(1)}, u32[]{:S(2)}, u32[]{:S(2)}) collective-permute-start(f32[64,384]{1,0:T(8,128)S(1)} %get-tuple-element.23.refs_0_), channel_id=1, source_target_pairs={{8,0},{0,8},{24,16},{16,24},{40,32},{32,40},{56,48},{48,56},{9,1},... | collective-permute-start | bytes 294920 | tf_op jit(solution)/shard_map/ppermute | solution.py:395
  63.3 9.0 %collective-permute-start.17 = (f32[64,384]{1,0:T(8,128)S(1)}, f32[64,384]{1,0:T(8,128)S(1)}, u32[]{:S(2)}, u32[]{:S(2)}) collective-permute-start(f32[64,384]{1,0:T(8,128)S(1)} %add_pieces.8.refs_0_), channel_id=1, source_target_pairs={{16,0},{56,8},{32,16},{8,24},{48,32},{24,40},{0,48},{40,56},{17,1}... | collective-permute-start | bytes 294920 | tf_op jit(solution)/shard_map/ppermute | solution.py:395
  66.4 5.9 %collective-permute-start.16 = (f32[64,384]{1,0:T(8,128)S(1)}, f32[64,384]{1,0:T(8,128)S(1)}, u32[]{:S(2)}, u32[]{:S(2)}) collective-permute-start(f32[64,384]{1,0:T(8,128)S(1)} %add_pieces.8.refs_0_), channel_id=1, source_target_pairs={{56,0},{16,8},{8,16},{32,24},{24,32},{48,40},{40,48},{0,56},{57,1}... | collective-permute-start | bytes 294920 | tf_op jit(solution)/shard_map/ppermute | solution.py:395
  67.2 8.1 %collective-permute-start.15 = (f32[64,384]{1,0:T(8,128)S(1)}, f32[64,384]{1,0:T(8,128)S(1)}, u32[]{:S(2)}, u32[]{:S(2)}) collective-permute-start(f32[64,384]{1,0:T(8,128)S(1)} %add_pieces.8.refs_0_), channel_id=1, source_target_pairs={{40,0},{32,8},{56,16},{48,24},{8,32},{0,40},{24,48},{16,56},{41,1}... | collective-permute-start | bytes 294920 | tf_op jit(solution)/shard_map/ppermute | solution.py:395
  75.6 6.5 %collective-permute-start.20 = (f32[64,384]{1,0:T(8,128)S(1)}, f32[64,384]{1,0:T(8,128)S(1)}, u32[]{:S(2)}, u32[]{:S(2)}) collective-permute-start(f32[64,384]{1,0:T(8,128)S(1)} %apply_right.1.refs_0_), channel_id=1, source_target_pairs={{0,6},{2,0},{4,2},{6,4},{1,7},{3,1},{5,3},{7,5},{8,14},{10,8},{12,... | collective-permute-start | bytes 294920 | tf_op jit(solution)/shard_map/ppermute | solution.py:390
  77.7 6.5 %collective-permute-start.19 = (f32[64,384]{1,0:T(8,128)S(1)}, f32[64,384]{1,0:T(8,128)S(1)}, u32[]{:S(2)}, u32[]{:S(2)}) collective-permute-start(f32[64,384]{1,0:T(8,128)S(1)} %apply_right.1.refs_0_), channel_id=1, source_target_pairs={{0,4},{2,6},{4,0},{6,2},{1,5},{3,7},{5,1},{7,3},{8,12},{10,14},{12... | collective-permute-start | bytes 294920 | tf_op jit(solution)/shard_map/ppermute | solution.py:390
  78.4 8.8 %collective-permute-start.18 = (f32[64,384]{1,0:T(8,128)S(1)}, f32[64,384]{1,0:T(8,128)S(1)}, u32[]{:S(2)}, u32[]{:S(2)}) collective-permute-start(f32[64,384]{1,0:T(8,128)S(1)} %apply_right.1.refs_0_), channel_id=1, source_target_pairs={{0,2},{2,4},{4,6},{6,0},{1,3},{3,5},{5,7},{7,1},{8,10},{10,12},{12... | collective-permute-start | bytes 294920 | tf_op jit(solution)/shard_map/ppermute | solution.py:390
  78.4 10.7 %collective-permute-start.21 = (f32[64,384]{1,0:T(8,128)S(1)}, f32[64,384]{1,0:T(8,128)S(1)}, u32[]{:S(2)}, u32[]{:S(2)}) collective-permute-start(f32[64,384]{1,0:T(8,128)S(1)} %apply_right.1.refs_0_), channel_id=1, source_target_pairs={{0,1},{1,0},{2,3},{3,2},{4,5},{5,4},{6,7},{7,6},{8,9},{9,8},{10,11... | collective-permute-start | bytes 294920 | tf_op jit(solution)/shard_map/ppermute | solution.py:385
  82.0 7.0 %collective-permute-start.24 = (f32[64,384]{1,0:T(8,128)S(1)}, f32[64,384]{1,0:T(8,128)S(1)}, u32[]{:S(2)}, u32[]{:S(2)}) collective-permute-start(f32[64,384]{1,0:T(8,128)S(1)} %collective-permute-done.20.refs_3_), channel_id=1, source_target_pairs={{0,1},{1,0},{2,3},{3,2},{4,5},{5,4},{6,7},{7,6},{8,9},{9,8},{10,11... | collective-permute-start | bytes 294920 | tf_op jit(solution)/shard_map/ppermute | solution.py:385
  84.2 4.8 %collective-permute-start.23 = (f32[64,384]{1,0:T(8,128)S(1)}, f32[64,384]{1,0:T(8,128)S(1)}, u32[]{:S(2)}, u32[]{:S(2)}) collective-permute-start(f32[64,384]{1,0:T(8,128)S(1)} %collective-permute-done.19.refs_2_), channel_id=1, source_target_pairs={{0,1},{1,0},{2,3},{3,2},{4,5},{5,4},{6,7},{7,6},{8,9},{9,8},{10,11... | collective-permute-start | bytes 294920 | tf_op jit(solution)/shard_map/ppermute | solution.py:385
  87.2 2.0 %collective-permute-start.22 = (f32[64,384]{1,0:T(8,128)S(1)}, f32[64,384]{1,0:T(8,128)S(1)}, u32[]{:S(2)}, u32[]{:S(2)}) collective-permute-start(f32[64,384]{1,0:T(8,128)S(1)} %collective-permute-done.18.refs_1_), channel_id=1, source_target_pairs={{0,1},{1,0},{2,3},{3,2},{4,5},{5,4},{6,7},{7,6},{8,9},{9,8},{10,11... | collective-permute-start | bytes 294920 | tf_op jit(solution)/shard_map/ppermute | solution.py:385

commit v4 on v3

--- a/solution.py
+++ b/solution.py
@@ -21,6 +21,7 @@
 CHUNK = 512
 CHUNKS = COLS // CHUNK
 RUNS = 4
+AHEAD = (0, 1, 3, 2)
 VMEM_LIMIT = 24 * 1024 * 1024
 F32 = jnp.float32
 BF16 = jnp.bfloat16
@@ -250,9 +251,9 @@
 
 def cross_kernel(own, *refs):
     *others, out, left = refs
-    pieces = [own, *others]
-    out[...] = (own[:LEFT] + others[1][:LEFT]) + (others[0][:LEFT] + others[2][:LEFT])
-    for k, piece in enumerate(pieces):
+    near, back, far = others
+    out[...] = (own[:LEFT] + far[:LEFT]) + (near[:LEFT] + back[:LEFT])
+    for k, piece in zip(AHEAD, (own, *others)):
         part = lax.rem(lax.axis_index("x") - k + XS, XS)
         left[pl.ds(pl.multiple_of(part * PART, PART), PART)] = piece[LEFT:REST]
 
@@ -270,9 +271,11 @@
 
 def add_kernel(*refs):
     *pieces, out = refs
-    while len(pieces) > 1:
-        pieces = [a[...] + b[...] for a, b in zip(pieces[::2], pieces[1::2])]
-    out[...] = pieces[0]
+    if len(pieces) == 2:
+        out[...] = pieces[0][...] + pieces[1][...]
+    else:
+        first, second, third, last = pieces
+        out[...] = (first[...] + last[...]) + (second[...] + third[...])
 
 
 def add(*pieces):
@@ -286,7 +289,7 @@
     )(*pieces)
 
 
-def invert_kernel(rest, out):
+def invert_kernel(rest, rows, out, left_out):
     packed = jnp.concatenate([rest[:, :128], rest[:, 128:256]], axis=0)
     turned = pltpu.roll(packed, 64, 1)
     row = lax.broadcasted_iota(jnp.int32, (RANK, 128), 0)
@@ -318,67 +321,73 @@
         axis=0,
     )
     scale = rest[:, 256:]
-    out[0] = jnp.concatenate([left[:RANK] * scale[0:1], left[RANK:] * scale[4:5]], axis=0)
-    out[1] = left * math.sqrt(COLS)
-
-
-def invert(rest):
+    out[...] = jnp.concatenate([left[:RANK] * scale[0:1], left[RANK:] * scale[4:5]], axis=0)
+    left_out[...] = multiply(left * math.sqrt(COLS), rows[...])
+
+
+def multiply(triangle, rows):
+    return jnp.dot(
+        triangle[:, :RANKS], rows, precision=lax.Precision.HIGHEST, preferred_element_type=F32
+    )
+
+
+def invert(rest, rows):
     return pl.pallas_call(
         invert_kernel,
-        in_specs=[whole()],
-        out_specs=whole(),
-        out_shape=jax.ShapeDtypeStruct((2, 64, 128), F32),
+        in_specs=[whole()] * 2,
+        out_specs=[whole()] * 2,
+        out_shape=[
+            jax.ShapeDtypeStruct((RANKS, 128), F32),
+            jax.ShapeDtypeStruct((RANKS, ROWS), F32),
+        ],
         compiler_params=params(),
         cost_estimate=pl.CostEstimate(flops=2_000_000, bytes_accessed=20_000_000, transcendentals=0),
         name="invert_triangle",
-    )(rest)
-
-
-def apply_kernel(which, rows, inverse, out):
-    out[...] = jnp.dot(
-        inverse[which][:, :RANKS],
-        rows[...],
-        precision=lax.Precision.HIGHEST,
-        preferred_element_type=F32,
-    )
-
-
-def apply(which, rows, inverse):
-    return pl.pallas_call(
-        functools.partial(apply_kernel, which),
+    )(rest, rows)
+
+
+def apply_kernel(rows, inverse, out):
+    out[...] = multiply(inverse, rows[...])
+
+
+def apply(rows, inverse):
+    return pl.pallas_call(
+        apply_kernel,
         in_specs=[whole(), whole()],
         out_specs=whole(),
         out_shape=jax.ShapeDtypeStruct((RANKS, ROWS), F32),
         compiler_params=params(),
-        name="apply_left" if which else "apply_right",
+        name="apply_right",
     )(rows, inverse)
 
 
-def assemble_kernel(*refs):
+def assemble_kernel(swapped, *refs):
     *pieces, out, sems = refs
     core, at = lax.axis_index("core"), lax.axis_index("y")
+    half = 1 - core if swapped else core
     copies = []
-    for i, piece in enumerate(pieces):
-        half = core if i < YS else 1 - core
-        block = lax.rem(at - i % YS + YS, YS)
+    for k, piece in enumerate(pieces[-YS:]):
+        block = lax.rem(at - k + YS, YS)
         columns = pl.ds(pl.multiple_of(half * HALF + block * ROWS, 128), ROWS)
-        copies.append(pltpu.make_async_copy(piece, out.at[:, columns], sems.at[i]))
+        copies.append(pltpu.make_async_copy(piece, out.at[:, columns], sems.at[k]))
     for copy in copies:
         copy.start()
     for copy in copies:
         copy.wait()
 
 
-def assemble(pieces):
-    return pl.pallas_call(
-        assemble_kernel,
-        in_specs=[whole()] * (2 * YS),
+def assemble(pieces, out=None):
+    swapped = out is not None
+    return pl.pallas_call(
+        functools.partial(assemble_kernel, swapped),
+        in_specs=[whole(pltpu.HBM)] * swapped + [whole()] * YS,
         out_specs=whole(pltpu.HBM),
         out_shape=jax.ShapeDtypeStruct((RANKS, COLS), F32),
-        scratch_shapes=[pltpu.SemaphoreType.DMA((2 * YS,))],
-        compiler_params=params(),
-        name="assemble_right",
-    )(*pieces)
+        scratch_shapes=[pltpu.SemaphoreType.DMA((YS,))],
+        compiler_params=params(),
+        input_output_aliases={0: 0} if swapped else {},
+        name="assemble_other_half" if swapped else "assemble_own_half",
+    )(*([out] * swapped), *pieces)
 
 
 def swap(value):
@@ -397,24 +406,26 @@
 
 def sum_z(value):
     value = add(value, along_z(value, 1, -1))
-    return add(value, along_z(value, -3, 3), along_z(value, -1, 1), along_z(value, 2, -2))
+    two, near, three = [along_z(value, at, -at) for at in (2, -1, -3)]
+    return add(value, two, near, three)
+
+
+def turns(values, axis, ahead=AHEAD):
+    return [values[0]] + [rotate(value, axis, k) for value, k in zip(values[1:], ahead[1:])]
 
 
 def shards(gradient, error_buffer, previous_q, run_starts, run_owners):
     q = jnp.swapaxes(previous_q, 1, 2)
     merged, partial, dest = merge(gradient, error_buffer, q, run_starts, run_owners)
-    far, near, back = [rotate(partial, "x", step) for step in (2, 1, 3)]
-    factor = sum_z(add(partial, far, near, back))
+    factor = sum_z(add(*turns([partial] * XS, "x")))
     sent = swap(product(False, dest, factor, merged))
     pieces = pair(product(True, dest, factor, merged), sent)
-    pieces = [pieces[0]] + [rotate(pieces[k], "y", k) for k in range(1, YS)]
-    terms, rest = line(pieces)
-    inverse = invert(rest)
-    terms, rows = cross([terms] + [rotate(terms, "x", k) for k in range(1, XS)])
-    right = apply(0, sum_z(terms), inverse)
-    left = apply(1, rows, inverse)
-    right = [right] + [rotate(right, "y", k) for k in range(1, YS)]
-    right = assemble(right + [swap(value) for value in right])
+    terms, rest = line(turns([pieces[k] for k in (0, 2, 1, 3)], "y", (0, 2, 1, 3)))
+    terms, rows = cross(turns([terms] * XS, "x"))
+    inverse, left = invert(rest, rows)
+    right = apply(sum_z(terms), inverse)
+    right = turns([right] * YS, "y", range(YS))
+    right = assemble([swap(value) for value in right], assemble(right))
     shape = (LAYERS, RANK, -1)
     return tuple(jnp.swapaxes(value.reshape(shape), 1, 2) for value in (left, right))
 

time: 90.3 us -> 87.2 us (0.966)
  waiting for transfers between devices: 29 us -> 26.5 us
  starting transfers between devices: 48.3 us -> 47.2 us
    ppermute x8, starting transfers between devices: 18.1 us -> 14.3 us  [along_z(): lax.ppermute(value, 'z', [(source, z) for z, source in enumerate(sources)])]
    ppermute x12, waiting for transfers between devices: 17.3 us -> 14.5 us  [rotate(): lax.ppermute(value, axis, [(i, (i + step) % size) for i in range(size)])]
    ppermute x12, starting transfers between devices: 15.4 us -> 17.8 us  [rotate(): lax.ppermute(value, axis, [(i, (i + step) % size) for i in range(size)])]
  transfers between devices with their start and end apart: 25 -> 25, of which waited for: 13 -> 16; matrix products, arithmetic and copies ran while one was open for 0% -> 0% of each run, Pallas kernels for 5% -> 6%
where the time goes in v4:
time: 87.2 us; the launch traced here: 87.1 us
  starting transfers between devices  47.2 us (54%)
  waiting for transfers between devices  26.5 us (30%)
  Pallas kernels  12.5 us (14%)
  between operations  0.9 us (1%)
    ppermute x12, starting transfers between devices, rotate(): lax.ppermute(value, axis, [(i, (i + step) % size) for i in range(size)])  17.8 us
    ppermute x5, starting transfers between devices, swap(): return lax.ppermute(value, 'core', [(0, 1), (1, 0)])  15 us
    ppermute x12, waiting for transfers between devices, rotate(): lax.ppermute(value, axis, [(i, (i + step) % size) for i in range(size)])  14.5 us
    ppermute x8, starting transfers between devices, along_z(): lax.ppermute(value, 'z', [(source, z) for z, source in enumerate(sources)])  14.3 us
    ppermute x8, waiting for transfers between devices, along_z(): lax.ppermute(value, 'z', [(source, z) for z, source in enumerate(sources)])  11.5 us
    pallas_call x1, Pallas kernels, merge(): pl.pallas_call(merge_kernel, in_specs=[whole(pltpu.HBM)] * 5, out_specs=[...  4.62 us
    pallas_call x1, Pallas kernels, invert(): pl.pallas_call(invert_kernel, in_specs=[whole()] * 2, out_specs=[whole()]...  3.61 us
    pallas_call x2, Pallas kernels, product(): pl.pallas_call(functools.partial(product_kernel, own), in_specs=[whole()]...  2.29 us
  transfers between devices with their start and end apart: 25, of which 16 were waited for; matrix products, arithmetic and copies ran while one was open for 0% of the time, Pallas kernels for 6%

profile of v4, /device:TPU:1, one launch (start us, length us, event | category | flops | bytes accessed | tf_op | source)
XLA Modules:
  0.0 87.1 jit_solution(7785311749528908427)
XLA Ops:
  0.6 4.6 %merge_project.1 = (bf16[2,384,3072]{2,1,0:T(8,128)(2,1)S(1)}, f32[64,384]{1,0:T(8,128)S(1)}, s32[8,384]{1,0:T(8,128)S(1)}) custom-call(bf16[1,2,384,3072]{3,2,1,0:T(8,128)(2,1)} %gradient.1, bf16[1,2,384,3072]{3,2,1,0:T(8,128)(2,1)} %error.1, f32[2,32,3072]{2,1,0:T(8,128)} %bitcast.8, s32[32]{0:T(128)} %starts.1, s32[32]{0:T(128)} %owners.1), custom_call_target="tpu_custom_call" | custom-call | tf_op jit(solution)/shard_map/merge_project/pallas_call | solution.py:119
  5.3 3.7 %collective-permute-start.2 = (f32[64,384]{1,0:T(8,128)S(1)}, f32[64,384]{1,0:T(8,128)S(1)}, u32[]{:S(2)}, u32[]{:S(2)}) collective-permute-start(f32[64,384]{1,0:T(8,128)S(1)} %get-tuple-element.16.refs_0_), channel_id=1, source_target_pairs={{0,128},{64,192},{128,0},{192,64},{1,129},{65,193},{129,1},{193,65... | collective-permute-start | bytes 294920 | tf_op jit(solution)/shard_map/ppermute | solution.py:399
  8.9 0.9 collective-permute-start.1
  9.8 0.6 collective-permute-start
  10.4 0.5 collective-permute-done.2.refs_3_
  10.9 2.8 %collective-permute-done.1.refs_2_ = f32[64,384]{1,0:T(8,128)S(1)} collective-permute-done((f32[64,384]{1,0:T(8,128)S(1)}, f32[64,384]{1,0:T(8,128)S(1)}, u32[]{:S(2)}, u32[]{:S(2)}) %collective-permute-start.1) | collective-permute-done | bytes 98336 | tf_op jit(solution)/shard_map/ppermute | solution.py:399
  13.7 1.4 %collective-permute-done.refs_1_ = f32[64,384]{1,0:T(8,128)S(1)} collective-permute-done((f32[64,384]{1,0:T(8,128)S(1)}, f32[64,384]{1,0:T(8,128)S(1)}, u32[]{:S(2)}, u32[]{:S(2)}) %collective-permute-start) | collective-permute-done | bytes 98336 | tf_op jit(solution)/shard_map/ppermute | solution.py:399
  15.2 1.1 %collective-permute-start.3 = (f32[64,384]{1,0:T(8,128)S(1)}, f32[64,384]{1,0:T(8,128)S(1)}, u32[]{:S(2)}, u32[]{:S(2)}) collective-permute-start(f32[64,384]{1,0:T(8,128)S(1)} %add_pieces.5.refs_0_), channel_id=1, source_target_pairs={{8,0},{0,8},{24,16},{16,24},{40,32},{32,40},{56,48},{48,56},{9,1},... | collective-permute-start | bytes 294920 | tf_op jit(solution)/shard_map/ppermute | solution.py:404
  16.2 2.5 %collective-permute-done.3.refs_1_ = f32[64,384]{1,0:T(8,128)S(1)} collective-permute-done((f32[64,384]{1,0:T(8,128)S(1)}, f32[64,384]{1,0:T(8,128)S(1)}, u32[]{:S(2)}, u32[]{:S(2)}) %collective-permute-start.3) | collective-permute-done | bytes 98336 | tf_op jit(solution)/shard_map/ppermute | solution.py:404
  18.7 5.9 %collective-permute-start.6 = (f32[64,384]{1,0:T(8,128)S(1)}, f32[64,384]{1,0:T(8,128)S(1)}, u32[]{:S(2)}, u32[]{:S(2)}) collective-permute-start(f32[64,384]{1,0:T(8,128)S(1)} %add_pieces.6.refs_0_), channel_id=1, source_target_pairs={{40,0},{32,8},{56,16},{48,24},{8,32},{0,40},{24,48},{16,56},{41,1}... | collective-permute-start | bytes 294920 | tf_op jit(solution)/shard_map/ppermute | solution.py:404
  24.6 0.4 collective-permute-start.4
  25.0 1.7 %collective-permute-done.6.refs_3_ = f32[64,384]{1,0:T(8,128)S(1)} collective-permute-done((f32[64,384]{1,0:T(8,128)S(1)}, f32[64,384]{1,0:T(8,128)S(1)}, u32[]{:S(2)}, u32[]{:S(2)}) %collective-permute-start.6) | collective-permute-done | bytes 98336 | tf_op jit(solution)/shard_map/ppermute | solution.py:404
  26.7 2.9 %collective-permute-done.5.refs_2_ = f32[64,384]{1,0:T(8,128)S(1)} collective-permute-done((f32[64,384]{1,0:T(8,128)S(1)}, f32[64,384]{1,0:T(8,128)S(1)}, u32[]{:S(2)}, u32[]{:S(2)}) %collective-permute-start.5) | collective-permute-done | bytes 98336 | tf_op jit(solution)/shard_map/ppermute | solution.py:404
  29.6 1.4 %collective-permute-done.4.refs_1_ = f32[64,384]{1,0:T(8,128)S(1)} collective-permute-done((f32[64,384]{1,0:T(8,128)S(1)}, f32[64,384]{1,0:T(8,128)S(1)}, u32[]{:S(2)}, u32[]{:S(2)}) %collective-permute-start.4) | collective-permute-done | bytes 98336 | tf_op jit(solution)/shard_map/ppermute | solution.py:404
  31.0 1.1 %product_other_half.1 = f32[4,88,384]{2,1,0:T(8,128)S(1)} custom-call(s32[8,384]{1,0:T(8,128)S(1)} %get-tuple-element.15.dest, f32[64,384]{1,0:T(8,128)S(1)} %add_pieces.7.factor_in, bf16[2,384,3072]{2,1,0:T(8,128)(2,1)S(1)} %get-tuple-element.17.merged), custom_call_target="tpu_custom_call" | custom-call | tf_op jit(solution)/shard_map/product_other_half/pallas_call | solution.py:183
  32.2 4.8 %collective-permute-start.7 = (f32[4,88,384]{2,1,0:T(8,128)S(1)}, f32[4,88,384]{2,1,0:T(8,128)S(1)}, u32[]{:S(2)}, u32[]{:S(2)}) collective-permute-start(f32[4,88,384]{2,1,0:T(8,128)S(1)} %product_other_half.1), channel_id=1, source_target_pairs={{0,1},{1,0},{2,3},{3,2},{4,5},{5,4},{6,7},{7,6},{8,9},{9,8},{10,11... | collective-permute-start | bytes 1622024 | tf_op jit(solution)/shard_map/ppermute | solution.py:394
  36.9 1.1 %product_own_half.1.mine = f32[4,88,384]{2,1,0:T(8,128)S(1)} custom-call(s32[8,384]{1,0:T(8,128)S(1)} %get-tuple-element.15.dest, f32[64,384]{1,0:T(8,128)S(1)} %add_pieces.7.factor_in, bf16[2,384,3072]{2,1,0:T(8,128)(2,1)S(1)} %get-tuple-element.17.merged), custom_call_target="tpu_custom_call" | custom-call | tf_op jit(solution)/shard_map/product_own_half/pallas_call | solution.py:183
  38.1 0.4 collective-permute-done.7.other
  38.5 0.1 add_cores.1
  38.6 3.0 %collective-permute-start.8 = (f32[88,384]{1,0:T(8,128)S(1)}, f32[88,384]{1,0:T(8,128)S(1)}, u32[]{:S(2)}, u32[]{:S(2)}) collective-permute-start(f32[88,384]{1,0:T(8,128)S(1)} %get-tuple-element.19), channel_id=1, source_target_pairs={{0,4},{2,6},{4,0},{6,2},{1,5},{3,7},{5,1},{7,3},{8,12},{10,14},{12... | collective-permute-start | bytes 405512 | tf_op jit(solution)/shard_map/ppermute | solution.py:399
  41.6 0.4 collective-permute-start.9
  42.0 2.3 %collective-permute-start.10 = (f32[88,384]{1,0:T(8,128)S(1)}, f32[88,384]{1,0:T(8,128)S(1)}, u32[]{:S(2)}, u32[]{:S(2)}) collective-permute-start(f32[88,384]{1,0:T(8,128)S(1)} %get-tuple-element.21), channel_id=1, source_target_pairs={{0,6},{2,0},{4,2},{6,4},{1,7},{3,1},{5,3},{7,5},{8,14},{10,8},{12,... | collective-permute-start | bytes 405512 | tf_op jit(solution)/shard_map/ppermute | solution.py:399
  44.3 0.7 collective-permute-done.8.b
  45.0 3.4 %collective-permute-done.9.c = f32[88,384]{1,0:T(8,128)S(1)} collective-permute-done((f32[88,384]{1,0:T(8,128)S(1)}, f32[88,384]{1,0:T(8,128)S(1)}, u32[]{:S(2)}, u32[]{:S(2)}) %collective-permute-start.9) | collective-permute-done | bytes 135200 | tf_op jit(solution)/shard_map/ppermute | solution.py:399
  48.3 0.1 add_line.1
  48.4 1.9 %collective-permute-start.13 = (f32[80,384]{1,0:T(8,128)S(1)}, f32[80,384]{1,0:T(8,128)S(1)}, u32[]{:S(2)}, u32[]{:S(2)}) collective-permute-start(f32[80,384]{1,0:T(8,128)S(1)} %get-tuple-element.23.own), channel_id=1, source_target_pairs={{0,128},{64,192},{128,0},{192,64},{1,129},{65,193},{129,1},{193,65... | collective-permute-start | bytes 368648 | tf_op jit(solution)/shard_map/ppermute | solution.py:399
  50.3 1.0 %collective-permute-start.12 = (f32[80,384]{1,0:T(8,128)S(1)}, f32[80,384]{1,0:T(8,128)S(1)}, u32[]{:S(2)}, u32[]{:S(2)}) collective-permute-start(f32[80,384]{1,0:T(8,128)S(1)} %get-tuple-element.23.own), channel_id=1, source_target_pairs={{0,192},{64,0},{128,64},{192,128},{1,193},{65,1},{129,65},{193,129... | collective-permute-start | bytes 368648 | tf_op jit(solution)/shard_map/ppermute | solution.py:399
  51.2 0.5 collective-permute-start.11
  51.7 2.0 %collective-permute-done.13.refs_2_ = f32[80,384]{1,0:T(8,128)S(1)} collective-permute-done((f32[80,384]{1,0:T(8,128)S(1)}, f32[80,384]{1,0:T(8,128)S(1)}, u32[]{:S(2)}, u32[]{:S(2)}) %collective-permute-start.13) | collective-permute-done | bytes 122912 | tf_op jit(solution)/shard_map/ppermute | solution.py:399
  53.7 1.6 %collective-permute-done.12.refs_1_ = f32[80,384]{1,0:T(8,128)S(1)} collective-permute-done((f32[80,384]{1,0:T(8,128)S(1)}, f32[80,384]{1,0:T(8,128)S(1)}, u32[]{:S(2)}, u32[]{:S(2)}) %collective-permute-start.12) | collective-permute-done | bytes 122912 | tf_op jit(solution)/shard_map/ppermute | solution.py:399
  55.4 2.0 %collective-permute-done.11.refs_0_ = f32[80,384]{1,0:T(8,128)S(1)} collective-permute-done((f32[80,384]{1,0:T(8,128)S(1)}, f32[80,384]{1,0:T(8,128)S(1)}, u32[]{:S(2)}, u32[]{:S(2)}) %collective-permute-start.11) | collective-permute-done | bytes 122912 | tf_op jit(solution)/shard_map/ppermute | solution.py:399
  57.4 2.2 %collective-permute-start.14 = (f32[64,384]{1,0:T(8,128)S(1)}, f32[64,384]{1,0:T(8,128)S(1)}, u32[]{:S(2)}, u32[]{:S(2)}) collective-permute-start(f32[64,384]{1,0:T(8,128)S(1)} %get-tuple-element.26.refs_0_), channel_id=1, source_target_pairs={{8,0},{0,8},{24,16},{16,24},{40,32},{32,40},{56,48},{48,56},{9,1},... | collective-permute-start | bytes 294920 | tf_op jit(solution)/shard_map/ppermute | solution.py:404
  59.6 2.0 %collective-permute-done.14.refs_1_ = f32[64,384]{1,0:T(8,128)S(1)} collective-permute-done((f32[64,384]{1,0:T(8,128)S(1)}, f32[64,384]{1,0:T(8,128)S(1)}, u32[]{:S(2)}, u32[]{:S(2)}) %collective-permute-start.14) | collective-permute-done | bytes 98336 | tf_op jit(solution)/shard_map/ppermute | solution.py:404
  61.6 2.4 %collective-permute-start.17 = (f32[64,384]{1,0:T(8,128)S(1)}, f32[64,384]{1,0:T(8,128)S(1)}, u32[]{:S(2)}, u32[]{:S(2)}) collective-permute-start(f32[64,384]{1,0:T(8,128)S(1)} %add_pieces.8.refs_0_), channel_id=1, source_target_pairs={{40,0},{32,8},{56,16},{48,24},{8,32},{0,40},{24,48},{16,56},{41,1}... | collective-permute-start | bytes 294920 | tf_op jit(solution)/shard_map/ppermute | solution.py:404
  64.0 0.9 %collective-permute-start.16 = (f32[64,384]{1,0:T(8,128)S(1)}, f32[64,384]{1,0:T(8,128)S(1)}, u32[]{:S(2)}, u32[]{:S(2)}) collective-permute-start(f32[64,384]{1,0:T(8,128)S(1)} %add_pieces.8.refs_0_), channel_id=1, source_target_pairs={{56,0},{16,8},{8,16},{32,24},{24,32},{48,40},{40,48},{0,56},{57,1}... | collective-permute-start | bytes 294920 | tf_op jit(solution)/shard_map/ppermute | solution.py:404
  64.9 1.5 %collective-permute-start.15 = (f32[64,384]{1,0:T(8,128)S(1)}, f32[64,384]{1,0:T(8,128)S(1)}, u32[]{:S(2)}, u32[]{:S(2)}) collective-permute-start(f32[64,384]{1,0:T(8,128)S(1)} %add_pieces.8.refs_0_), channel_id=1, source_target_pairs={{16,0},{56,8},{32,16},{8,24},{48,32},{24,40},{0,48},{40,56},{17,1}... | collective-permute-start | bytes 294920 | tf_op jit(solution)/shard_map/ppermute | solution.py:404
  66.4 3.6 %invert_triangle.1 = (f32[64,128]{1,0:T(8,128)S(1)}, f32[64,384]{1,0:T(8,128)}) custom-call(f32[8,384]{1,0:T(8,128)S(1)} %get-tuple-element.22.rest, f32[64,384]{1,0:T(8,128)S(1)} %get-tuple-element.24.rows), custom_call_target="tpu_custom_call" | custom-call | flops 2000000 | bytes 20000000 | tf_op jit(solution)/shard_map/invert_triangle/pallas_call | solution.py:335
  70.1 1.0 %collective-permute-done.15.refs_1_ = f32[64,384]{1,0:T(8,128)S(1)} collective-permute-done((f32[64,384]{1,0:T(8,128)S(1)}, f32[64,384]{1,0:T(8,128)S(1)}, u32[]{:S(2)}, u32[]{:S(2)}) %collective-permute-start.15) | collective-permute-done | bytes 98336 | tf_op jit(solution)/shard_map/ppermute | solution.py:404
  71.1 0.2 apply_right.1.refs_0_
  71.3 1.3 %collective-permute-start.20 = (f32[64,384]{1,0:T(8,128)S(1)}, f32[64,384]{1,0:T(8,128)S(1)}, u32[]{:S(2)}, u32[]{:S(2)}) collective-permute-start(f32[64,384]{1,0:T(8,128)S(1)} %apply_right.1.refs_0_), channel_id=1, source_target_pairs={{0,6},{2,0},{4,2},{6,4},{1,7},{3,1},{5,3},{7,5},{8,14},{10,8},{12,... | collective-permute-start | bytes 294920 | tf_op jit(solution)/shard_map/ppermute | solution.py:399
  72.6 2.4 %collective-permute-start.19 = (f32[64,384]{1,0:T(8,128)S(1)}, f32[64,384]{1,0:T(8,128)S(1)}, u32[]{:S(2)}, u32[]{:S(2)}) collective-permute-start(f32[64,384]{1,0:T(8,128)S(1)} %apply_right.1.refs_0_), channel_id=1, source_target_pairs={{0,4},{2,6},{4,0},{6,2},{1,5},{3,7},{5,1},{7,3},{8,12},{10,14},{12... | collective-permute-start | bytes 294920 | tf_op jit(solution)/shard_map/ppermute | solution.py:399
  75.0 4.4 %collective-permute-start.21 = (f32[64,384]{1,0:T(8,128)S(1)}, f32[64,384]{1,0:T(8,128)S(1)}, u32[]{:S(2)}, u32[]{:S(2)}) collective-permute-start(f32[64,384]{1,0:T(8,128)S(1)} %apply_right.1.refs_0_), channel_id=1, source_target_pairs={{0,1},{1,0},{2,3},{3,2},{4,5},{5,4},{6,7},{7,6},{8,9},{9,8},{10,11... | collective-permute-start | bytes 294920 | tf_op jit(solution)/shard_map/ppermute | solution.py:394
  79.4 1.9 %collective-permute-start.24 = (f32[64,384]{1,0:T(8,128)S(1)}, f32[64,384]{1,0:T(8,128)S(1)}, u32[]{:S(2)}, u32[]{:S(2)}) collective-permute-start(f32[64,384]{1,0:T(8,128)S(1)} %collective-permute-done.20.refs_3_), channel_id=1, source_target_pairs={{0,1},{1,0},{2,3},{3,2},{4,5},{5,4},{6,7},{7,6},{8,9},{9,8},{10,11... | collective-permute-start | bytes 294920 | tf_op jit(solution)/shard_map/ppermute | solution.py:394
  81.3 2.9 %collective-permute-start.23 = (f32[64,384]{1,0:T(8,128)S(1)}, f32[64,384]{1,0:T(8,128)S(1)}, u32[]{:S(2)}, u32[]{:S(2)}) collective-permute-start(f32[64,384]{1,0:T(8,128)S(1)} %collective-permute-done.19.refs_2_), channel_id=1, source_target_pairs={{0,1},{1,0},{2,3},{3,2},{4,5},{5,4},{6,7},{7,6},{8,9},{9,8},{10,11... | collective-permute-start | bytes 294920 | tf_op jit(solution)/shard_map/ppermute | solution.py:394
  84.2 1.1 %collective-permute-start.22 = (f32[64,384]{1,0:T(8,128)S(1)}, f32[64,384]{1,0:T(8,128)S(1)}, u32[]{:S(2)}, u32[]{:S(2)}) collective-permute-start(f32[64,384]{1,0:T(8,128)S(1)} %collective-permute-done.18.refs_1_), channel_id=1, source_target_pairs={{0,1},{1,0},{2,3},{3,2},{4,5},{5,4},{6,7},{7,6},{8,9},{9,8},{10,11... | collective-permute-start | bytes 294920 | tf_op jit(solution)/shard_map/ppermute | solution.py:394
  85.3 0.8 assemble_own_half.1.refs_0_
  86.1 0.1 collective-permute-done.22.refs_2_
  86.2 0.8 assemble_other_half.1
  (17 shorter events, 0.1 us)
Async XLA Ops:
  5.3 5.7 %collective-permute-start.2 = (f32[64,384]{1,0:T(8,128)S(1)}, f32[64,384]{1,0:T(8,128)S(1)}, u32[]{:S(2)}, u32[]{:S(2)}) collective-permute-start(f32[64,384]{1,0:T(8,128)S(1)} %get-tuple-element.16.refs_0_), channel_id=1, source_target_pairs={{0,128},{64,192},{128,0},{192,64},{1,129},{65,193},{129,1},{193,65... | collective-permute-start | bytes 294920 | tf_op jit(solution)/shard_map/ppermute | solution.py:399
  8.9 4.8 %collective-permute-start.1 = (f32[64,384]{1,0:T(8,128)S(1)}, f32[64,384]{1,0:T(8,128)S(1)}, u32[]{:S(2)}, u32[]{:S(2)}) collective-permute-start(f32[64,384]{1,0:T(8,128)S(1)} %get-tuple-element.16.refs_0_), channel_id=1, source_target_pairs={{0,192},{64,0},{128,64},{192,128},{1,193},{65,1},{129,65},{193,129... | collective-permute-start | bytes 294920 | tf_op jit(solution)/shard_map/ppermute | solution.py:399
  9.8 5.4 %collective-permute-start = (f32[64,384]{1,0:T(8,128)S(1)}, f32[64,384]{1,0:T(8,128)S(1)}, u32[]{:S(2)}, u32[]{:S(2)}) collective-permute-start(f32[64,384]{1,0:T(8,128)S(1)} %get-tuple-element.16.refs_0_), channel_id=1, source_target_pairs={{0,64},{64,128},{128,192},{192,0},{1,65},{65,129},{129,193},{193,1... | collective-permute-start | bytes 294920 | tf_op jit(solution)/shard_map/ppermute | solution.py:399
  15.2 3.6 %collective-permute-start.3 = (f32[64,384]{1,0:T(8,128)S(1)}, f32[64,384]{1,0:T(8,128)S(1)}, u32[]{:S(2)}, u32[]{:S(2)}) collective-permute-start(f32[64,384]{1,0:T(8,128)S(1)} %add_pieces.5.refs_0_), channel_id=1, source_target_pairs={{8,0},{0,8},{24,16},{16,24},{40,32},{32,40},{56,48},{48,56},{9,1},... | collective-permute-start | bytes 294920 | tf_op jit(solution)/shard_map/ppermute | solution.py:404
  18.7 8.0 %collective-permute-start.6 = (f32[64,384]{1,0:T(8,128)S(1)}, f32[64,384]{1,0:T(8,128)S(1)}, u32[]{:S(2)}, u32[]{:S(2)}) collective-permute-start(f32[64,384]{1,0:T(8,128)S(1)} %add_pieces.6.refs_0_), channel_id=1, source_target_pairs={{40,0},{32,8},{56,16},{48,24},{8,32},{0,40},{24,48},{16,56},{41,1}... | collective-permute-start | bytes 294920 | tf_op jit(solution)/shard_map/ppermute | solution.py:404
  24.6 5.0 %collective-permute-start.5 = (f32[64,384]{1,0:T(8,128)S(1)}, f32[64,384]{1,0:T(8,128)S(1)}, u32[]{:S(2)}, u32[]{:S(2)}) collective-permute-start(f32[64,384]{1,0:T(8,128)S(1)} %add_pieces.6.refs_0_), channel_id=1, source_target_pairs={{56,0},{16,8},{8,16},{32,24},{24,32},{48,40},{40,48},{0,56},{57,1}... | collective-permute-start | bytes 294920 | tf_op jit(solution)/shard_map/ppermute | solution.py:404
  24.6 6.4 %collective-permute-start.4 = (f32[64,384]{1,0:T(8,128)S(1)}, f32[64,384]{1,0:T(8,128)S(1)}, u32[]{:S(2)}, u32[]{:S(2)}) collective-permute-start(f32[64,384]{1,0:T(8,128)S(1)} %add_pieces.6.refs_0_), channel_id=1, source_target_pairs={{16,0},{56,8},{32,16},{8,24},{48,32},{24,40},{0,48},{40,56},{17,1}... | collective-permute-start | bytes 294920 | tf_op jit(solution)/shard_map/ppermute | solution.py:404
  32.2 6.3 %collective-permute-start.7 = (f32[4,88,384]{2,1,0:T(8,128)S(1)}, f32[4,88,384]{2,1,0:T(8,128)S(1)}, u32[]{:S(2)}, u32[]{:S(2)}) collective-permute-start(f32[4,88,384]{2,1,0:T(8,128)S(1)} %product_other_half.1), channel_id=1, source_target_pairs={{0,1},{1,0},{2,3},{3,2},{4,5},{5,4},{6,7},{7,6},{8,9},{9,8},{10,11... | collective-permute-start | bytes 1622024 | tf_op jit(solution)/shard_map/ppermute | solution.py:394
  38.6 6.4 %collective-permute-start.8 = (f32[88,384]{1,0:T(8,128)S(1)}, f32[88,384]{1,0:T(8,128)S(1)}, u32[]{:S(2)}, u32[]{:S(2)}) collective-permute-start(f32[88,384]{1,0:T(8,128)S(1)} %get-tuple-element.19), channel_id=1, source_target_pairs={{0,4},{2,6},{4,0},{6,2},{1,5},{3,7},{5,1},{7,3},{8,12},{10,14},{12... | collective-permute-start | bytes 405512 | tf_op jit(solution)/shard_map/ppermute | solution.py:399
  41.6 6.8 %collective-permute-start.9 = (f32[88,384]{1,0:T(8,128)S(1)}, f32[88,384]{1,0:T(8,128)S(1)}, u32[]{:S(2)}, u32[]{:S(2)}) collective-permute-start(f32[88,384]{1,0:T(8,128)S(1)} %get-tuple-element.20), channel_id=1, source_target_pairs={{0,2},{2,4},{4,6},{6,0},{1,3},{3,5},{5,7},{7,1},{8,10},{10,12},{12... | collective-permute-start | bytes 405512 | tf_op jit(solution)/shard_map/ppermute | solution.py:399
  42.0 6.4 %collective-permute-start.10 = (f32[88,384]{1,0:T(8,128)S(1)}, f32[88,384]{1,0:T(8,128)S(1)}, u32[]{:S(2)}, u32[]{:S(2)}) collective-permute-start(f32[88,384]{1,0:T(8,128)S(1)} %get-tuple-element.21), channel_id=1, source_target_pairs={{0,6},{2,0},{4,2},{6,4},{1,7},{3,1},{5,3},{7,5},{8,14},{10,8},{12,... | collective-permute-start | bytes 405512 | tf_op jit(solution)/shard_map/ppermute | solution.py:399
  48.4 5.3 %collective-permute-start.13 = (f32[80,384]{1,0:T(8,128)S(1)}, f32[80,384]{1,0:T(8,128)S(1)}, u32[]{:S(2)}, u32[]{:S(2)}) collective-permute-start(f32[80,384]{1,0:T(8,128)S(1)} %get-tuple-element.23.own), channel_id=1, source_target_pairs={{0,128},{64,192},{128,0},{192,64},{1,129},{65,193},{129,1},{193,65... | collective-permute-start | bytes 368648 | tf_op jit(solution)/shard_map/ppermute | solution.py:399
  50.3 5.1 %collective-permute-start.12 = (f32[80,384]{1,0:T(8,128)S(1)}, f32[80,384]{1,0:T(8,128)S(1)}, u32[]{:S(2)}, u32[]{:S(2)}) collective-permute-start(f32[80,384]{1,0:T(8,128)S(1)} %get-tuple-element.23.own), channel_id=1, source_target_pairs={{0,192},{64,0},{128,64},{192,128},{1,193},{65,1},{129,65},{193,129... | collective-permute-start | bytes 368648 | tf_op jit(solution)/shard_map/ppermute | solution.py:399
  51.2 6.1 %collective-permute-start.11 = (f32[80,384]{1,0:T(8,128)S(1)}, f32[80,384]{1,0:T(8,128)S(1)}, u32[]{:S(2)}, u32[]{:S(2)}) collective-permute-start(f32[80,384]{1,0:T(8,128)S(1)} %get-tuple-element.23.own), channel_id=1, source_target_pairs={{0,64},{64,128},{128,192},{192,0},{1,65},{65,129},{129,193},{193,1... | collective-permute-start | bytes 368648 | tf_op jit(solution)/shard_map/ppermute | solution.py:399
  57.4 4.2 %collective-permute-start.14 = (f32[64,384]{1,0:T(8,128)S(1)}, f32[64,384]{1,0:T(8,128)S(1)}, u32[]{:S(2)}, u32[]{:S(2)}) collective-permute-start(f32[64,384]{1,0:T(8,128)S(1)} %get-tuple-element.26.refs_0_), channel_id=1, source_target_pairs={{8,0},{0,8},{24,16},{16,24},{40,32},{32,40},{56,48},{48,56},{9,1},... | collective-permute-start | bytes 294920 | tf_op jit(solution)/shard_map/ppermute | solution.py:404
  61.6 8.5 %collective-permute-start.17 = (f32[64,384]{1,0:T(8,128)S(1)}, f32[64,384]{1,0:T(8,128)S(1)}, u32[]{:S(2)}, u32[]{:S(2)}) collective-permute-start(f32[64,384]{1,0:T(8,128)S(1)} %add_pieces.8.refs_0_), channel_id=1, source_target_pairs={{40,0},{32,8},{56,16},{48,24},{8,32},{0,40},{24,48},{16,56},{41,1}... | collective-permute-start | bytes 294920 | tf_op jit(solution)/shard_map/ppermute | solution.py:404
  64.0 6.0 %collective-permute-start.16 = (f32[64,384]{1,0:T(8,128)S(1)}, f32[64,384]{1,0:T(8,128)S(1)}, u32[]{:S(2)}, u32[]{:S(2)}) collective-permute-start(f32[64,384]{1,0:T(8,128)S(1)} %add_pieces.8.refs_0_), channel_id=1, source_target_pairs={{56,0},{16,8},{8,16},{32,24},{24,32},{48,40},{40,48},{0,56},{57,1}... | collective-permute-start | bytes 294920 | tf_op jit(solution)/shard_map/ppermute | solution.py:404
  64.9 6.1 %collective-permute-start.15 = (f32[64,384]{1,0:T(8,128)S(1)}, f32[64,384]{1,0:T(8,128)S(1)}, u32[]{:S(2)}, u32[]{:S(2)}) collective-permute-start(f32[64,384]{1,0:T(8,128)S(1)} %add_pieces.8.refs_0_), channel_id=1, source_target_pairs={{16,0},{56,8},{32,16},{8,24},{48,32},{24,40},{0,48},{40,56},{17,1}... | collective-permute-start | bytes 294920 | tf_op jit(solution)/shard_map/ppermute | solution.py:404
  71.3 8.1 %collective-permute-start.20 = (f32[64,384]{1,0:T(8,128)S(1)}, f32[64,384]{1,0:T(8,128)S(1)}, u32[]{:S(2)}, u32[]{:S(2)}) collective-permute-start(f32[64,384]{1,0:T(8,128)S(1)} %apply_right.1.refs_0_), channel_id=1, source_target_pairs={{0,6},{2,0},{4,2},{6,4},{1,7},{3,1},{5,3},{7,5},{8,14},{10,8},{12,... | collective-permute-start | bytes 294920 | tf_op jit(solution)/shard_map/ppermute | solution.py:399
  72.6 8.7 %collective-permute-start.19 = (f32[64,384]{1,0:T(8,128)S(1)}, f32[64,384]{1,0:T(8,128)S(1)}, u32[]{:S(2)}, u32[]{:S(2)}) collective-permute-start(f32[64,384]{1,0:T(8,128)S(1)} %apply_right.1.refs_0_), channel_id=1, source_target_pairs={{0,4},{2,6},{4,0},{6,2},{1,5},{3,7},{5,1},{7,3},{8,12},{10,14},{12... | collective-permute-start | bytes 294920 | tf_op jit(solution)/shard_map/ppermute | solution.py:399
  75.0 9.2 %collective-permute-start.18 = (f32[64,384]{1,0:T(8,128)S(1)}, f32[64,384]{1,0:T(8,128)S(1)}, u32[]{:S(2)}, u32[]{:S(2)}) collective-permute-start(f32[64,384]{1,0:T(8,128)S(1)} %apply_right.1.refs_0_), channel_id=1, source_target_pairs={{0,2},{2,4},{4,6},{6,0},{1,3},{3,5},{5,7},{7,1},{8,10},{10,12},{12... | collective-permute-start | bytes 294920 | tf_op jit(solution)/shard_map/ppermute | solution.py:399
  75.0 11.1 %collective-permute-start.21 = (f32[64,384]{1,0:T(8,128)S(1)}, f32[64,384]{1,0:T(8,128)S(1)}, u32[]{:S(2)}, u32[]{:S(2)}) collective-permute-start(f32[64,384]{1,0:T(8,128)S(1)} %apply_right.1.refs_0_), channel_id=1, source_target_pairs={{0,1},{1,0},{2,3},{3,2},{4,5},{5,4},{6,7},{7,6},{8,9},{9,8},{10,11... | collective-permute-start | bytes 294920 | tf_op jit(solution)/shard_map/ppermute | solution.py:394
  79.4 6.6 %collective-permute-start.24 = (f32[64,384]{1,0:T(8,128)S(1)}, f32[64,384]{1,0:T(8,128)S(1)}, u32[]{:S(2)}, u32[]{:S(2)}) collective-permute-start(f32[64,384]{1,0:T(8,128)S(1)} %collective-permute-done.20.refs_3_), channel_id=1, source_target_pairs={{0,1},{1,0},{2,3},{3,2},{4,5},{5,4},{6,7},{7,6},{8,9},{9,8},{10,11... | collective-permute-start | bytes 294920 | tf_op jit(solution)/shard_map/ppermute | solution.py:394
  81.3 4.8 %collective-permute-start.23 = (f32[64,384]{1,0:T(8,128)S(1)}, f32[64,384]{1,0:T(8,128)S(1)}, u32[]{:S(2)}, u32[]{:S(2)}) collective-permute-start(f32[64,384]{1,0:T(8,128)S(1)} %collective-permute-done.19.refs_2_), channel_id=1, source_target_pairs={{0,1},{1,0},{2,3},{3,2},{4,5},{5,4},{6,7},{7,6},{8,9},{9,8},{10,11... | collective-permute-start | bytes 294920 | tf_op jit(solution)/shard_map/ppermute | solution.py:394
  84.2 2.0 %collective-permute-start.22 = (f32[64,384]{1,0:T(8,128)S(1)}, f32[64,384]{1,0:T(8,128)S(1)}, u32[]{:S(2)}, u32[]{:S(2)}) collective-permute-start(f32[64,384]{1,0:T(8,128)S(1)} %collective-permute-done.18.refs_1_), channel_id=1, source_target_pairs={{0,1},{1,0},{2,3},{3,2},{4,5},{5,4},{6,7},{7,6},{8,9},{9,8},{10,11... | collective-permute-start | bytes 294920 | tf_op jit(solution)/shard_map/ppermute | solution.py:394

commit v5 on v4

--- a/solution.py
+++ b/solution.py
@@ -21,7 +21,10 @@
 CHUNK = 512
 CHUNKS = COLS // CHUNK
 RUNS = 4
-AHEAD = (0, 1, 3, 2)
+ORDER_FIRST = (0, 2, 3, 1)
+ORDER_LINE = (0, 1, 2, 3)
+ORDER_CROSS = (0, 2, 3, 1)
+ORDER_LAST = (0, 1, 2, 3)
 VMEM_LIMIT = 24 * 1024 * 1024
 F32 = jnp.float32
 BF16 = jnp.bfloat16
@@ -138,32 +141,16 @@
     )(*operands)
 
 
-def product_kernel(own, dest, factor_in, merged, out):
-    at = lax.axis_index("y")
-    half = lax.axis_index("core") if own else 1 - lax.axis_index("core")
+def prepare_kernel(factor_in, parts, rest):
     factor = factor_in[...]
     biggest = [
         jnp.max(jnp.abs(factor[l * RANK : l * RANK + RANK]), keepdims=True) for l in range(LAYERS)
     ]
-    scales = [jnp.where(b > 0, b * 64.0, 1.0) for b in biggest]
-    columns = pl.ds(pl.multiple_of(half * HALF, 128), HALF)
-    step = [lax.rem(y - at + YS, YS) for y in range(YS)]
+    scales = [jnp.where(b > 0, b * 64.0, 1e-30) for b in biggest]
     for layer in range(LAYERS):
-        ranks = slice(layer * RANK, layer * RANK + RANK)
-        parts = jnp.concatenate(split3(factor[ranks] * (1.0 / scales[layer])), axis=0)
-        product = jnp.dot(parts, merged[layer, :, columns], preferred_element_type=F32)
-        product = product[:RANK] + product[RANK : 2 * RANK] + product[2 * RANK :]
-        for y in range(YS):
-            out[step[y], ranks] = product[:, y * ROWS : y * ROWS + ROWS]
-    first = pl.multiple_of(lax.axis_index("x") * PART, PART)
-    rows = jnp.concatenate(split3(factor_in[pl.ds(first, PART)]), axis=0)
-    wanted = jnp.broadcast_to(dest[0:1], (ROWS, ROWS)) - lax.broadcasted_iota(
-        jnp.int32, (ROWS, ROWS), 0
-    )
-    for y in range(YS):
-        chosen = jnp.where(wanted == (y * 2 + half) * ROWS, 1.0, 0.0).astype(BF16)
-        found = dot_rows(rows, chosen)
-        out[step[y], LEFT:REST] = found[:PART] + found[PART : 2 * PART] + found[2 * PART :]
+        scaled = factor[layer * RANK : layer * RANK + RANK] * (1.0 / scales[layer])
+        for i, part in enumerate(split3(scaled)):
+            parts[layer, i * RANK : i * RANK + RANK] = part
     high, middle, low = split3(factor)
     left = jnp.concatenate([high, middle, low], axis=0)
     right = jnp.concatenate([high, high, middle, middle, low, low], axis=0)
@@ -174,20 +161,55 @@
     gram = jnp.where(lax.rem(lane, 64) < 32, gram[:RANK], gram[RANK:])
     gram = jnp.where(lane[:16] < 64, gram[:16], gram[16:])
     scale = jnp.concatenate([jnp.broadcast_to(s, (4, 128)) for s in scales], axis=0)
-    rest = jnp.concatenate([gram[:8], gram[8:], scale], axis=1)
-    for k in range(YS):
-        out[k, REST:] = rest
-
-
-def product(own, dest, factor, merged):
-    return pl.pallas_call(
-        functools.partial(product_kernel, own),
-        in_specs=[whole()] * 3,
+    rest[...] = jnp.concatenate([gram[:8], gram[8:], scale], axis=1)
+
+
+def prepare(factor):
+    return pl.pallas_call(
+        prepare_kernel,
+        in_specs=[whole()],
+        out_specs=[whole(), whole()],
+        out_shape=[
+            jax.ShapeDtypeStruct((LAYERS, 3 * RANK, ROWS), BF16),
+            jax.ShapeDtypeStruct((8, ROWS), F32),
+        ],
+        compiler_params=params(),
+        name="split_factor",
+    )(factor)
+
+
+def product_kernel(own, steps, dest, factor_in, parts, rest, merged, out):
+    half = lax.axis_index("core") if own else 1 - lax.axis_index("core")
+    first = pl.multiple_of(lax.axis_index("x") * PART, PART)
+    rows = jnp.concatenate(split3(factor_in[pl.ds(first, PART)]), axis=0)
+    wanted = jnp.broadcast_to(dest[0:1], (ROWS, ROWS)) - lax.broadcasted_iota(
+        jnp.int32, (ROWS, ROWS), 0
+    )
+    for i, step in enumerate(steps):
+        y = lax.rem(lax.axis_index("y") + step, YS)
+        columns = pl.ds(pl.multiple_of(half * HALF + y * ROWS, 128), ROWS)
+        for layer in range(LAYERS):
+            product = jnp.dot(
+                parts[layer], merged[layer, :, columns], preferred_element_type=F32
+            )
+            out[i, layer * RANK : layer * RANK + RANK] = (
+                product[:RANK] + product[RANK : 2 * RANK] + product[2 * RANK :]
+            )
+        chosen = jnp.where(wanted == (y * 2 + half) * ROWS, 1.0, 0.0).astype(BF16)
+        found = dot_rows(rows, chosen)
+        out[i, LEFT:REST] = found[:PART] + found[PART : 2 * PART] + found[2 * PART :]
+        out[i, REST:] = rest[...]
+
+
+def product(own, steps, dest, factor, prepared, merged):
+    return pl.pallas_call(
+        functools.partial(product_kernel, own, steps),
+        in_specs=[whole()] * 5,
         out_specs=whole(),
-        out_shape=jax.ShapeDtypeStruct((YS, SENT, ROWS), F32),
+        out_shape=jax.ShapeDtypeStruct((len(steps), SENT, ROWS), F32),
         compiler_params=params(),
         name="product_own_half" if own else "product_other_half",
-    )(dest, factor, pltpu.with_memory_space_constraint(merged, pltpu.VMEM))
+    )(dest, factor, *prepared, pltpu.with_memory_space_constraint(merged, pltpu.VMEM))
 
 
 def add_scaled(pieces):
@@ -224,8 +246,8 @@
     return pl.pallas_call(
         pair_kernel,
         in_specs=[whole(), whole()],
-        out_specs=[whole()] * YS,
-        out_shape=[jax.ShapeDtypeStruct((SENT, ROWS), F32)] * YS,
+        out_specs=[whole()] * len(mine),
+        out_shape=[jax.ShapeDtypeStruct((SENT, ROWS), F32)] * len(mine),
         compiler_params=params(),
         name="add_cores",
     )(mine, other)
@@ -249,18 +271,18 @@
     )(*pieces)
 
 
-def cross_kernel(own, *refs):
-    *others, out, left = refs
-    near, back, far = others
+def cross_kernel(order, *refs):
+    *pieces, out, left = refs
+    own, near, far, back = (pieces[order.index(k)] for k in range(XS))
     out[...] = (own[:LEFT] + far[:LEFT]) + (near[:LEFT] + back[:LEFT])
-    for k, piece in zip(AHEAD, (own, *others)):
+    for k, piece in zip(order, pieces):
         part = lax.rem(lax.axis_index("x") - k + XS, XS)
         left[pl.ds(pl.multiple_of(part * PART, PART), PART)] = piece[LEFT:REST]
 
 
-def cross(pieces):
-    return pl.pallas_call(
-        cross_kernel,
+def cross(order, pieces):
+    return pl.pallas_call(
+        functools.partial(cross_kernel, order),
         in_specs=[whole()] * XS,
         out_specs=[whole(), whole()],
         out_shape=[jax.ShapeDtypeStruct((RANKS, ROWS), F32)] * 2,
@@ -269,18 +291,18 @@
     )(*pieces)
 
 
-def add_kernel(*refs):
-    *pieces, out = refs
-    if len(pieces) == 2:
-        out[...] = pieces[0][...] + pieces[1][...]
-    else:
-        first, second, third, last = pieces
-        out[...] = (first[...] + last[...]) + (second[...] + third[...])
-
-
-def add(*pieces):
-    return pl.pallas_call(
-        add_kernel,
+def add_kernel(mate, *refs):
+    own, *others, out = refs
+    paired = others.pop(mate)
+    total = own[...] + paired[...]
+    if others:
+        total = total + (others[0][...] + others[1][...])
+    out[...] = total
+
+
+def add(mate, *pieces):
+    return pl.pallas_call(
+        functools.partial(add_kernel, mate),
         in_specs=[whole()] * len(pieces),
         out_specs=whole(),
         out_shape=jax.ShapeDtypeStruct((RANKS, ROWS), F32),
@@ -366,7 +388,7 @@
     core, at = lax.axis_index("core"), lax.axis_index("y")
     half = 1 - core if swapped else core
     copies = []
-    for k, piece in enumerate(pieces[-YS:]):
+    for k, piece in zip(ORDER_LAST, pieces[-YS:]):
         block = lax.rem(at - k + YS, YS)
         columns = pl.ds(pl.multiple_of(half * HALF + block * ROWS, 128), ROWS)
         copies.append(pltpu.make_async_copy(piece, out.at[:, columns], sems.at[k]))
@@ -405,26 +427,34 @@
 
 
 def sum_z(value):
-    value = add(value, along_z(value, 1, -1))
-    two, near, three = [along_z(value, at, -at) for at in (2, -1, -3)]
-    return add(value, two, near, three)
-
-
-def turns(values, axis, ahead=AHEAD):
-    return [values[0]] + [rotate(value, axis, k) for value, k in zip(values[1:], ahead[1:])]
+    value = add(0, value, along_z(value, 1, -1))
+    three, near, two = [along_z(value, at, -at) for at in (-3, -1, 2)]
+    return add(0, value, three, near, two)
+
+
+def turns(values, axis, order):
+    return [values[0]] + [rotate(value, axis, k) for value, k in zip(values[1:], order[1:])]
+
+
+def sum_x(value):
+    return add(ORDER_FIRST.index(2) - 1, *turns([value] * XS, "x", ORDER_FIRST))
 
 
 def shards(gradient, error_buffer, previous_q, run_starts, run_owners):
     q = jnp.swapaxes(previous_q, 1, 2)
     merged, partial, dest = merge(gradient, error_buffer, q, run_starts, run_owners)
-    factor = sum_z(add(*turns([partial] * XS, "x")))
-    sent = swap(product(False, dest, factor, merged))
-    pieces = pair(product(True, dest, factor, merged), sent)
-    terms, rest = line(turns([pieces[k] for k in (0, 2, 1, 3)], "y", (0, 2, 1, 3)))
-    terms, rows = cross(turns([terms] * XS, "x"))
+    factor = sum_z(sum_x(partial))
+    prepared = prepare(factor)
+    pieces = {}
+    for steps in ((2, 1), (3, 0)):
+        sent = swap(product(False, steps, dest, factor, prepared, merged))
+        summed = pair(product(True, steps, dest, factor, prepared, merged), sent)
+        pieces.update(zip(steps, summed))
+    terms, rest = line(turns([pieces[k] for k in ORDER_LINE], "y", ORDER_LINE))
+    terms, rows = cross(ORDER_CROSS, turns([terms] * XS, "x", ORDER_CROSS))
     inverse, left = invert(rest, rows)
     right = apply(sum_z(terms), inverse)
-    right = turns([right] * YS, "y", range(YS))
+    right = turns([right] * YS, "y", ORDER_LAST)
     right = assemble([swap(value) for value in right], assemble(right))
     shape = (LAYERS, RANK, -1)
     return tuple(jnp.swapaxes(value.reshape(shape), 1, 2) for value in (left, right))

time: 87.2 us -> 86.1 us (0.987)
    ppermute x5 -> x6, starting transfers between devices: 15 us -> 13.2 us  [swap(): return lax.ppermute(value, 'core', [(0, 1), (1, 0)])]
    ppermute x12, starting transfers between devices: 17.8 us -> 18.8 us  [rotate(): lax.ppermute(value, axis, [(i, (i + step) % size) for i in range(size)])]
    pallas_call x8 -> x11, Pallas kernels: 2.41 us -> 2.59 us  [the longest x4 2.21 us: product(): pl.pallas_call(functools.partial(product_kernel, own, steps), in_specs=[w...]
  transfers between devices with their start and end apart: 25 -> 26, of which waited for: 16 -> 15; matrix products, arithmetic and copies ran while one was open for 0% -> 0% of each run, Pallas kernels for 6% -> 7%
where the time goes in v5:
time: 86.1 us; the launch traced here: 86 us
  starting transfers between devices  46.4 us (54%)
  waiting for transfers between devices  26 us (30%)
  Pallas kernels  12.8 us (15%)
  between operations  0.91 us (1%)
    ppermute x12, starting transfers between devices, rotate(): lax.ppermute(value, axis, [(i, (i + step) % size) for i in range(size)])  18.8 us
    ppermute x8, starting transfers between devices, along_z(): lax.ppermute(value, 'z', [(source, z) for z, source in enumerate(sources)])  14.3 us
    ppermute x12, waiting for transfers between devices, rotate(): lax.ppermute(value, axis, [(i, (i + step) % size) for i in range(size)])  14.3 us
    ppermute x6, starting transfers between devices, swap(): return lax.ppermute(value, 'core', [(0, 1), (1, 0)])  13.2 us
    ppermute x8, waiting for transfers between devices, along_z(): lax.ppermute(value, 'z', [(source, z) for z, source in enumerate(sources)])  11.5 us
    pallas_call x1, Pallas kernels, merge(): pl.pallas_call(merge_kernel, in_specs=[whole(pltpu.HBM)] * 5, out_specs=[...  4.62 us
    pallas_call x1, Pallas kernels, invert(): pl.pallas_call(invert_kernel, in_specs=[whole()] * 2, out_specs=[whole()]...  3.62 us
    pallas_call x4, Pallas kernels, product(): pl.pallas_call(functools.partial(product_kernel, own, steps), in_specs=[w...  2.21 us
  transfers between devices with their start and end apart: 26, of which 15 were waited for; matrix products, arithmetic and copies ran while one was open for 0% of the time, Pallas kernels for 7%

profile of v5, /device:TPU:1, one launch (start us, length us, event | category | flops | bytes accessed | tf_op | source)
XLA Modules:
  0.0 86.0 jit_solution(14265167598406864600)
XLA Ops:
  0.6 4.6 %merge_project.1 = (bf16[2,384,3072]{2,1,0:T(8,128)(2,1)S(1)}, f32[64,384]{1,0:T(8,128)S(1)}, s32[8,384]{1,0:T(8,128)S(1)}) custom-call(bf16[1,2,384,3072]{3,2,1,0:T(8,128)(2,1)} %gradient.1, bf16[1,2,384,3072]{3,2,1,0:T(8,128)(2,1)} %error.1, f32[2,32,3072]{2,1,0:T(8,128)} %bitcast.8, s32[32]{0:T(128)} %starts.1, s32[32]{0:T(128)} %owners.1), custom_call_target="tpu_custom_call" | custom-call | tf_op jit(solution)/shard_map/merge_project/pallas_call | solution.py:122
  5.3 3.7 %collective-permute-start = (f32[64,384]{1,0:T(8,128)S(1)}, f32[64,384]{1,0:T(8,128)S(1)}, u32[]{:S(2)}, u32[]{:S(2)}) collective-permute-start(f32[64,384]{1,0:T(8,128)S(1)} %get-tuple-element.18.refs_0_), channel_id=1, source_target_pairs={{0,128},{64,192},{128,0},{192,64},{1,129},{65,193},{129,1},{193,65... | collective-permute-start | bytes 294920 | tf_op jit(solution)/shard_map/ppermute | solution.py:421
  8.9 0.9 %collective-permute-start.1 = (f32[64,384]{1,0:T(8,128)S(1)}, f32[64,384]{1,0:T(8,128)S(1)}, u32[]{:S(2)}, u32[]{:S(2)}) collective-permute-start(f32[64,384]{1,0:T(8,128)S(1)} %get-tuple-element.18.refs_0_), channel_id=1, source_target_pairs={{0,192},{64,0},{128,64},{192,128},{1,193},{65,1},{129,65},{193,129... | collective-permute-start | bytes 294920 | tf_op jit(solution)/shard_map/ppermute | solution.py:421
  9.8 0.6 collective-permute-start.2
  10.4 0.5 collective-permute-done.refs_1_
  10.9 2.8 %collective-permute-done.1.refs_2_ = f32[64,384]{1,0:T(8,128)S(1)} collective-permute-done((f32[64,384]{1,0:T(8,128)S(1)}, f32[64,384]{1,0:T(8,128)S(1)}, u32[]{:S(2)}, u32[]{:S(2)}) %collective-permute-start.1) | collective-permute-done | bytes 98336 | tf_op jit(solution)/shard_map/ppermute | solution.py:421
  13.7 1.4 %collective-permute-done.2.refs_3_ = f32[64,384]{1,0:T(8,128)S(1)} collective-permute-done((f32[64,384]{1,0:T(8,128)S(1)}, f32[64,384]{1,0:T(8,128)S(1)}, u32[]{:S(2)}, u32[]{:S(2)}) %collective-permute-start.2) | collective-permute-done | bytes 98336 | tf_op jit(solution)/shard_map/ppermute | solution.py:421
  15.2 1.1 %collective-permute-start.3 = (f32[64,384]{1,0:T(8,128)S(1)}, f32[64,384]{1,0:T(8,128)S(1)}, u32[]{:S(2)}, u32[]{:S(2)}) collective-permute-start(f32[64,384]{1,0:T(8,128)S(1)} %add_pieces.5.refs_0_), channel_id=1, source_target_pairs={{8,0},{0,8},{24,16},{16,24},{40,32},{32,40},{56,48},{48,56},{9,1},... | collective-permute-start | bytes 294920 | tf_op jit(solution)/shard_map/ppermute | solution.py:426
  16.2 2.5 %collective-permute-done.3.refs_1_ = f32[64,384]{1,0:T(8,128)S(1)} collective-permute-done((f32[64,384]{1,0:T(8,128)S(1)}, f32[64,384]{1,0:T(8,128)S(1)}, u32[]{:S(2)}, u32[]{:S(2)}) %collective-permute-start.3) | collective-permute-done | bytes 98336 | tf_op jit(solution)/shard_map/ppermute | solution.py:426
  18.7 5.9 %collective-permute-start.4 = (f32[64,384]{1,0:T(8,128)S(1)}, f32[64,384]{1,0:T(8,128)S(1)}, u32[]{:S(2)}, u32[]{:S(2)}) collective-permute-start(f32[64,384]{1,0:T(8,128)S(1)} %add_pieces.6.refs_0_), channel_id=1, source_target_pairs={{40,0},{32,8},{56,16},{48,24},{8,32},{0,40},{24,48},{16,56},{41,1}... | collective-permute-start | bytes 294920 | tf_op jit(solution)/shard_map/ppermute | solution.py:426
  24.6 0.4 collective-permute-start.6
  25.0 1.7 %collective-permute-done.4.refs_1_ = f32[64,384]{1,0:T(8,128)S(1)} collective-permute-done((f32[64,384]{1,0:T(8,128)S(1)}, f32[64,384]{1,0:T(8,128)S(1)}, u32[]{:S(2)}, u32[]{:S(2)}) %collective-permute-start.4) | collective-permute-done | bytes 98336 | tf_op jit(solution)/shard_map/ppermute | solution.py:426
  26.7 2.9 %collective-permute-done.5.refs_2_ = f32[64,384]{1,0:T(8,128)S(1)} collective-permute-done((f32[64,384]{1,0:T(8,128)S(1)}, f32[64,384]{1,0:T(8,128)S(1)}, u32[]{:S(2)}, u32[]{:S(2)}) %collective-permute-start.5) | collective-permute-done | bytes 98336 | tf_op jit(solution)/shard_map/ppermute | solution.py:426
  29.6 1.4 %collective-permute-done.6.refs_3_ = f32[64,384]{1,0:T(8,128)S(1)} collective-permute-done((f32[64,384]{1,0:T(8,128)S(1)}, f32[64,384]{1,0:T(8,128)S(1)}, u32[]{:S(2)}, u32[]{:S(2)}) %collective-permute-start.6) | collective-permute-done | bytes 98336 | tf_op jit(solution)/shard_map/ppermute | solution.py:426
  31.0 0.3 split_factor.1
  31.3 0.6 product_other_half.3
  31.9 4.7 %collective-permute-start.8 = (f32[2,88,384]{2,1,0:T(8,128)S(1)}, f32[2,88,384]{2,1,0:T(8,128)S(1)}, u32[]{:S(2)}, u32[]{:S(2)}) collective-permute-start(f32[2,88,384]{2,1,0:T(8,128)S(1)} %product_other_half.3), channel_id=1, source_target_pairs={{0,1},{1,0},{2,3},{3,2},{4,5},{5,4},{6,7},{7,6},{8,9},{9,8},{10,11... | collective-permute-start | bytes 811016 | tf_op jit(solution)/shard_map/ppermute | solution.py:416
  36.6 0.5 product_other_half.2
  37.2 0.5 product_own_half.3.mine
  37.7 0.6 product_own_half.2.mine
  38.4 3.0 %collective-permute-start.10 = (f32[88,384]{1,0:T(8,128)S(1)}, f32[88,384]{1,0:T(8,128)S(1)}, u32[]{:S(2)}, u32[]{:S(2)}) collective-permute-start(f32[88,384]{1,0:T(8,128)S(1)} %get-tuple-element.24), channel_id=1, source_target_pairs={{0,4},{2,6},{4,0},{6,2},{1,5},{3,7},{5,1},{7,3},{8,12},{10,14},{12... | collective-permute-start | bytes 405512 | tf_op jit(solution)/shard_map/ppermute | solution.py:421
  41.4 0.4 collective-permute-start.9
  41.8 2.3 %collective-permute-start.11 = (f32[88,384]{1,0:T(8,128)S(1)}, f32[88,384]{1,0:T(8,128)S(1)}, u32[]{:S(2)}, u32[]{:S(2)}) collective-permute-start(f32[88,384]{1,0:T(8,128)S(1)} %get-tuple-element.25), channel_id=1, source_target_pairs={{0,6},{2,0},{4,2},{6,4},{1,7},{3,1},{5,3},{7,5},{8,14},{10,8},{12,... | collective-permute-start | bytes 405512 | tf_op jit(solution)/shard_map/ppermute | solution.py:421
  44.2 0.5 collective-permute-done.10.c
  44.6 3.5 %collective-permute-done.9.b = f32[88,384]{1,0:T(8,128)S(1)} collective-permute-done((f32[88,384]{1,0:T(8,128)S(1)}, f32[88,384]{1,0:T(8,128)S(1)}, u32[]{:S(2)}, u32[]{:S(2)}) %collective-permute-start.9) | collective-permute-done | bytes 135200 | tf_op jit(solution)/shard_map/ppermute | solution.py:421
  48.2 2.0 %collective-permute-start.12 = (f32[80,384]{1,0:T(8,128)S(1)}, f32[80,384]{1,0:T(8,128)S(1)}, u32[]{:S(2)}, u32[]{:S(2)}) collective-permute-start(f32[80,384]{1,0:T(8,128)S(1)} %get-tuple-element.27.refs_0_), channel_id=1, source_target_pairs={{0,128},{64,192},{128,0},{192,64},{1,129},{65,193},{129,1},{193,65... | collective-permute-start | bytes 368648 | tf_op jit(solution)/shard_map/ppermute | solution.py:421
  50.2 1.0 %collective-permute-start.13 = (f32[80,384]{1,0:T(8,128)S(1)}, f32[80,384]{1,0:T(8,128)S(1)}, u32[]{:S(2)}, u32[]{:S(2)}) collective-permute-start(f32[80,384]{1,0:T(8,128)S(1)} %get-tuple-element.27.refs_0_), channel_id=1, source_target_pairs={{0,192},{64,0},{128,64},{192,128},{1,193},{65,1},{129,65},{193,129... | collective-permute-start | bytes 368648 | tf_op jit(solution)/shard_map/ppermute | solution.py:421
  51.2 0.5 collective-permute-start.14
  51.7 2.0 %collective-permute-done.12.refs_1_ = f32[80,384]{1,0:T(8,128)S(1)} collective-permute-done((f32[80,384]{1,0:T(8,128)S(1)}, f32[80,384]{1,0:T(8,128)S(1)}, u32[]{:S(2)}, u32[]{:S(2)}) %collective-permute-start.12) | collective-permute-done | bytes 122912 | tf_op jit(solution)/shard_map/ppermute | solution.py:421
  53.7 1.6 %collective-permute-done.13.refs_2_ = f32[80,384]{1,0:T(8,128)S(1)} collective-permute-done((f32[80,384]{1,0:T(8,128)S(1)}, f32[80,384]{1,0:T(8,128)S(1)}, u32[]{:S(2)}, u32[]{:S(2)}) %collective-permute-start.13) | collective-permute-done | bytes 122912 | tf_op jit(solution)/shard_map/ppermute | solution.py:421
  55.3 2.0 %collective-permute-done.14.refs_3_ = f32[80,384]{1,0:T(8,128)S(1)} collective-permute-done((f32[80,384]{1,0:T(8,128)S(1)}, f32[80,384]{1,0:T(8,128)S(1)}, u32[]{:S(2)}, u32[]{:S(2)}) %collective-permute-start.14) | collective-permute-done | bytes 122912 | tf_op jit(solution)/shard_map/ppermute | solution.py:421
  57.3 2.2 %collective-permute-start.15 = (f32[64,384]{1,0:T(8,128)S(1)}, f32[64,384]{1,0:T(8,128)S(1)}, u32[]{:S(2)}, u32[]{:S(2)}) collective-permute-start(f32[64,384]{1,0:T(8,128)S(1)} %get-tuple-element.30.refs_0_), channel_id=1, source_target_pairs={{8,0},{0,8},{24,16},{16,24},{40,32},{32,40},{56,48},{48,56},{9,1},... | collective-permute-start | bytes 294920 | tf_op jit(solution)/shard_map/ppermute | solution.py:426
  59.5 2.0 %collective-permute-done.15.refs_1_ = f32[64,384]{1,0:T(8,128)S(1)} collective-permute-done((f32[64,384]{1,0:T(8,128)S(1)}, f32[64,384]{1,0:T(8,128)S(1)}, u32[]{:S(2)}, u32[]{:S(2)}) %collective-permute-start.15) | collective-permute-done | bytes 98336 | tf_op jit(solution)/shard_map/ppermute | solution.py:426
  61.5 2.4 %collective-permute-start.16 = (f32[64,384]{1,0:T(8,128)S(1)}, f32[64,384]{1,0:T(8,128)S(1)}, u32[]{:S(2)}, u32[]{:S(2)}) collective-permute-start(f32[64,384]{1,0:T(8,128)S(1)} %add_pieces.8.refs_0_), channel_id=1, source_target_pairs={{40,0},{32,8},{56,16},{48,24},{8,32},{0,40},{24,48},{16,56},{41,1}... | collective-permute-start | bytes 294920 | tf_op jit(solution)/shard_map/ppermute | solution.py:426
  64.0 0.9 %collective-permute-start.17 = (f32[64,384]{1,0:T(8,128)S(1)}, f32[64,384]{1,0:T(8,128)S(1)}, u32[]{:S(2)}, u32[]{:S(2)}) collective-permute-start(f32[64,384]{1,0:T(8,128)S(1)} %add_pieces.8.refs_0_), channel_id=1, source_target_pairs={{56,0},{16,8},{8,16},{32,24},{24,32},{48,40},{40,48},{0,56},{57,1}... | collective-permute-start | bytes 294920 | tf_op jit(solution)/shard_map/ppermute | solution.py:426
  64.8 1.5 %collective-permute-start.18 = (f32[64,384]{1,0:T(8,128)S(1)}, f32[64,384]{1,0:T(8,128)S(1)}, u32[]{:S(2)}, u32[]{:S(2)}) collective-permute-start(f32[64,384]{1,0:T(8,128)S(1)} %add_pieces.8.refs_0_), channel_id=1, source_target_pairs={{16,0},{56,8},{32,16},{8,24},{48,32},{24,40},{0,48},{40,56},{17,1}... | collective-permute-start | bytes 294920 | tf_op jit(solution)/shard_map/ppermute | solution.py:426
  66.4 3.6 %invert_triangle.1 = (f32[64,128]{1,0:T(8,128)S(1)}, f32[64,384]{1,0:T(8,128)}) custom-call(f32[8,384]{1,0:T(8,128)S(1)} %get-tuple-element.26.rest, f32[64,384]{1,0:T(8,128)S(1)} %get-tuple-element.28.rows), custom_call_target="tpu_custom_call" | custom-call | flops 2000000 | bytes 20000000 | tf_op jit(solution)/shard_map/invert_triangle/pallas_call | solution.py:357
  70.0 1.0 %collective-permute-done.18.refs_3_ = f32[64,384]{1,0:T(8,128)S(1)} collective-permute-done((f32[64,384]{1,0:T(8,128)S(1)}, f32[64,384]{1,0:T(8,128)S(1)}, u32[]{:S(2)}, u32[]{:S(2)}) %collective-permute-start.18) | collective-permute-done | bytes 98336 | tf_op jit(solution)/shard_map/ppermute | solution.py:426
  71.0 0.2 apply_right.1.refs_0_
  71.2 1.9 %collective-permute-start.19 = (f32[64,384]{1,0:T(8,128)S(1)}, f32[64,384]{1,0:T(8,128)S(1)}, u32[]{:S(2)}, u32[]{:S(2)}) collective-permute-start(f32[64,384]{1,0:T(8,128)S(1)} %apply_right.1.refs_0_), channel_id=1, source_target_pairs={{0,2},{2,4},{4,6},{6,0},{1,3},{3,5},{5,7},{7,1},{8,10},{10,12},{12... | collective-permute-start | bytes 294920 | tf_op jit(solution)/shard_map/ppermute | solution.py:421
  73.2 1.3 %collective-permute-start.20 = (f32[64,384]{1,0:T(8,128)S(1)}, f32[64,384]{1,0:T(8,128)S(1)}, u32[]{:S(2)}, u32[]{:S(2)}) collective-permute-start(f32[64,384]{1,0:T(8,128)S(1)} %apply_right.1.refs_0_), channel_id=1, source_target_pairs={{0,4},{2,6},{4,0},{6,2},{1,5},{3,7},{5,1},{7,3},{8,12},{10,14},{12... | collective-permute-start | bytes 294920 | tf_op jit(solution)/shard_map/ppermute | solution.py:421
  74.5 1.2 %collective-permute-start.21 = (f32[64,384]{1,0:T(8,128)S(1)}, f32[64,384]{1,0:T(8,128)S(1)}, u32[]{:S(2)}, u32[]{:S(2)}) collective-permute-start(f32[64,384]{1,0:T(8,128)S(1)} %apply_right.1.refs_0_), channel_id=1, source_target_pairs={{0,6},{2,0},{4,2},{6,4},{1,7},{3,1},{5,3},{7,5},{8,14},{10,8},{12,... | collective-permute-start | bytes 294920 | tf_op jit(solution)/shard_map/ppermute | solution.py:421
  75.7 4.4 %collective-permute-start.22 = (f32[64,384]{1,0:T(8,128)S(1)}, f32[64,384]{1,0:T(8,128)S(1)}, u32[]{:S(2)}, u32[]{:S(2)}) collective-permute-start(f32[64,384]{1,0:T(8,128)S(1)} %apply_right.1.refs_0_), channel_id=1, source_target_pairs={{0,1},{1,0},{2,3},{3,2},{4,5},{5,4},{6,7},{7,6},{8,9},{9,8},{10,11... | collective-permute-start | bytes 294920 | tf_op jit(solution)/shard_map/ppermute | solution.py:416
  80.1 1.2 %collective-permute-start.23 = (f32[64,384]{1,0:T(8,128)S(1)}, f32[64,384]{1,0:T(8,128)S(1)}, u32[]{:S(2)}, u32[]{:S(2)}) collective-permute-start(f32[64,384]{1,0:T(8,128)S(1)} %collective-permute-done.19.refs_1_), channel_id=1, source_target_pairs={{0,1},{1,0},{2,3},{3,2},{4,5},{5,4},{6,7},{7,6},{8,9},{9,8},{10,11... | collective-permute-start | bytes 294920 | tf_op jit(solution)/shard_map/ppermute | solution.py:416
  81.3 2.1 %collective-permute-start.24 = (f32[64,384]{1,0:T(8,128)S(1)}, f32[64,384]{1,0:T(8,128)S(1)}, u32[]{:S(2)}, u32[]{:S(2)}) collective-permute-start(f32[64,384]{1,0:T(8,128)S(1)} %collective-permute-done.20.refs_2_), channel_id=1, source_target_pairs={{0,1},{1,0},{2,3},{3,2},{4,5},{5,4},{6,7},{7,6},{8,9},{9,8},{10,11... | collective-permute-start | bytes 294920 | tf_op jit(solution)/shard_map/ppermute | solution.py:416
  83.5 0.7 collective-permute-start.25
  84.1 0.8 assemble_own_half.1.refs_0_
  85.1 0.8 assemble_other_half.1
  (23 shorter events, 0.5 us)
Async XLA Ops:
  5.3 5.7 %collective-permute-start = (f32[64,384]{1,0:T(8,128)S(1)}, f32[64,384]{1,0:T(8,128)S(1)}, u32[]{:S(2)}, u32[]{:S(2)}) collective-permute-start(f32[64,384]{1,0:T(8,128)S(1)} %get-tuple-element.18.refs_0_), channel_id=1, source_target_pairs={{0,128},{64,192},{128,0},{192,64},{1,129},{65,193},{129,1},{193,65... | collective-permute-start | bytes 294920 | tf_op jit(solution)/shard_map/ppermute | solution.py:421
  8.9 4.8 %collective-permute-start.1 = (f32[64,384]{1,0:T(8,128)S(1)}, f32[64,384]{1,0:T(8,128)S(1)}, u32[]{:S(2)}, u32[]{:S(2)}) collective-permute-start(f32[64,384]{1,0:T(8,128)S(1)} %get-tuple-element.18.refs_0_), channel_id=1, source_target_pairs={{0,192},{64,0},{128,64},{192,128},{1,193},{65,1},{129,65},{193,129... | collective-permute-start | bytes 294920 | tf_op jit(solution)/shard_map/ppermute | solution.py:421
  9.8 5.3 %collective-permute-start.2 = (f32[64,384]{1,0:T(8,128)S(1)}, f32[64,384]{1,0:T(8,128)S(1)}, u32[]{:S(2)}, u32[]{:S(2)}) collective-permute-start(f32[64,384]{1,0:T(8,128)S(1)} %get-tuple-element.18.refs_0_), channel_id=1, source_target_pairs={{0,64},{64,128},{128,192},{192,0},{1,65},{65,129},{129,193},{193,1... | collective-permute-start | bytes 294920 | tf_op jit(solution)/shard_map/ppermute | solution.py:421
  15.2 3.6 %collective-permute-start.3 = (f32[64,384]{1,0:T(8,128)S(1)}, f32[64,384]{1,0:T(8,128)S(1)}, u32[]{:S(2)}, u32[]{:S(2)}) collective-permute-start(f32[64,384]{1,0:T(8,128)S(1)} %add_pieces.5.refs_0_), channel_id=1, source_target_pairs={{8,0},{0,8},{24,16},{16,24},{40,32},{32,40},{56,48},{48,56},{9,1},... | collective-permute-start | bytes 294920 | tf_op jit(solution)/shard_map/ppermute | solution.py:426
  18.7 8.0 %collective-permute-start.4 = (f32[64,384]{1,0:T(8,128)S(1)}, f32[64,384]{1,0:T(8,128)S(1)}, u32[]{:S(2)}, u32[]{:S(2)}) collective-permute-start(f32[64,384]{1,0:T(8,128)S(1)} %add_pieces.6.refs_0_), channel_id=1, source_target_pairs={{40,0},{32,8},{56,16},{48,24},{8,32},{0,40},{24,48},{16,56},{41,1}... | collective-permute-start | bytes 294920 | tf_op jit(solution)/shard_map/ppermute | solution.py:426
  24.6 5.0 %collective-permute-start.5 = (f32[64,384]{1,0:T(8,128)S(1)}, f32[64,384]{1,0:T(8,128)S(1)}, u32[]{:S(2)}, u32[]{:S(2)}) collective-permute-start(f32[64,384]{1,0:T(8,128)S(1)} %add_pieces.6.refs_0_), channel_id=1, source_target_pairs={{56,0},{16,8},{8,16},{32,24},{24,32},{48,40},{40,48},{0,56},{57,1}... | collective-permute-start | bytes 294920 | tf_op jit(solution)/shard_map/ppermute | solution.py:426
  24.6 6.4 %collective-permute-start.6 = (f32[64,384]{1,0:T(8,128)S(1)}, f32[64,384]{1,0:T(8,128)S(1)}, u32[]{:S(2)}, u32[]{:S(2)}) collective-permute-start(f32[64,384]{1,0:T(8,128)S(1)} %add_pieces.6.refs_0_), channel_id=1, source_target_pairs={{16,0},{56,8},{32,16},{8,24},{48,32},{24,40},{0,48},{40,56},{17,1}... | collective-permute-start | bytes 294920 | tf_op jit(solution)/shard_map/ppermute | solution.py:426
  31.9 6.4 %collective-permute-start.8 = (f32[2,88,384]{2,1,0:T(8,128)S(1)}, f32[2,88,384]{2,1,0:T(8,128)S(1)}, u32[]{:S(2)}, u32[]{:S(2)}) collective-permute-start(f32[2,88,384]{2,1,0:T(8,128)S(1)} %product_other_half.3), channel_id=1, source_target_pairs={{0,1},{1,0},{2,3},{3,2},{4,5},{5,4},{6,7},{7,6},{8,9},{9,8},{10,11... | collective-permute-start | bytes 811016 | tf_op jit(solution)/shard_map/ppermute | solution.py:416
  37.1 4.6 %collective-permute-start.7 = (f32[2,88,384]{2,1,0:T(8,128)S(1)}, f32[2,88,384]{2,1,0:T(8,128)S(1)}, u32[]{:S(2)}, u32[]{:S(2)}) collective-permute-start(f32[2,88,384]{2,1,0:T(8,128)S(1)} %product_other_half.2), channel_id=1, source_target_pairs={{0,1},{1,0},{2,3},{3,2},{4,5},{5,4},{6,7},{7,6},{8,9},{9,8},{10,11... | collective-permute-start | bytes 811016 | tf_op jit(solution)/shard_map/ppermute | solution.py:416
  38.4 6.3 %collective-permute-start.10 = (f32[88,384]{1,0:T(8,128)S(1)}, f32[88,384]{1,0:T(8,128)S(1)}, u32[]{:S(2)}, u32[]{:S(2)}) collective-permute-start(f32[88,384]{1,0:T(8,128)S(1)} %get-tuple-element.24), channel_id=1, source_target_pairs={{0,4},{2,6},{4,0},{6,2},{1,5},{3,7},{5,1},{7,3},{8,12},{10,14},{12... | collective-permute-start | bytes 405512 | tf_op jit(solution)/shard_map/ppermute | solution.py:421
  41.4 6.8 %collective-permute-start.9 = (f32[88,384]{1,0:T(8,128)S(1)}, f32[88,384]{1,0:T(8,128)S(1)}, u32[]{:S(2)}, u32[]{:S(2)}) collective-permute-start(f32[88,384]{1,0:T(8,128)S(1)} %get-tuple-element.23), channel_id=1, source_target_pairs={{0,2},{2,4},{4,6},{6,0},{1,3},{3,5},{5,7},{7,1},{8,10},{10,12},{12... | collective-permute-start | bytes 405512 | tf_op jit(solution)/shard_map/ppermute | solution.py:421
  41.8 6.3 %collective-permute-start.11 = (f32[88,384]{1,0:T(8,128)S(1)}, f32[88,384]{1,0:T(8,128)S(1)}, u32[]{:S(2)}, u32[]{:S(2)}) collective-permute-start(f32[88,384]{1,0:T(8,128)S(1)} %get-tuple-element.25), channel_id=1, source_target_pairs={{0,6},{2,0},{4,2},{6,4},{1,7},{3,1},{5,3},{7,5},{8,14},{10,8},{12,... | collective-permute-start | bytes 405512 | tf_op jit(solution)/shard_map/ppermute | solution.py:421
  48.2 5.5 %collective-permute-start.12 = (f32[80,384]{1,0:T(8,128)S(1)}, f32[80,384]{1,0:T(8,128)S(1)}, u32[]{:S(2)}, u32[]{:S(2)}) collective-permute-start(f32[80,384]{1,0:T(8,128)S(1)} %get-tuple-element.27.refs_0_), channel_id=1, source_target_pairs={{0,128},{64,192},{128,0},{192,64},{1,129},{65,193},{129,1},{193,65... | collective-permute-start | bytes 368648 | tf_op jit(solution)/shard_map/ppermute | solution.py:421
  50.2 5.1 %collective-permute-start.13 = (f32[80,384]{1,0:T(8,128)S(1)}, f32[80,384]{1,0:T(8,128)S(1)}, u32[]{:S(2)}, u32[]{:S(2)}) collective-permute-start(f32[80,384]{1,0:T(8,128)S(1)} %get-tuple-element.27.refs_0_), channel_id=1, source_target_pairs={{0,192},{64,0},{128,64},{192,128},{1,193},{65,1},{129,65},{193,129... | collective-permute-start | bytes 368648 | tf_op jit(solution)/shard_map/ppermute | solution.py:421
  51.2 6.1 %collective-permute-start.14 = (f32[80,384]{1,0:T(8,128)S(1)}, f32[80,384]{1,0:T(8,128)S(1)}, u32[]{:S(2)}, u32[]{:S(2)}) collective-permute-start(f32[80,384]{1,0:T(8,128)S(1)} %get-tuple-element.27.refs_0_), channel_id=1, source_target_pairs={{0,64},{64,128},{128,192},{192,0},{1,65},{65,129},{129,193},{193,1... | collective-permute-start | bytes 368648 | tf_op jit(solution)/shard_map/ppermute | solution.py:421
  57.3 4.2 %collective-permute-start.15 = (f32[64,384]{1,0:T(8,128)S(1)}, f32[64,384]{1,0:T(8,128)S(1)}, u32[]{:S(2)}, u32[]{:S(2)}) collective-permute-start(f32[64,384]{1,0:T(8,128)S(1)} %get-tuple-element.30.refs_0_), channel_id=1, source_target_pairs={{8,0},{0,8},{24,16},{16,24},{40,32},{32,40},{56,48},{48,56},{9,1},... | collective-permute-start | bytes 294920 | tf_op jit(solution)/shard_map/ppermute | solution.py:426
  61.5 8.5 %collective-permute-start.16 = (f32[64,384]{1,0:T(8,128)S(1)}, f32[64,384]{1,0:T(8,128)S(1)}, u32[]{:S(2)}, u32[]{:S(2)}) collective-permute-start(f32[64,384]{1,0:T(8,128)S(1)} %add_pieces.8.refs_0_), channel_id=1, source_target_pairs={{40,0},{32,8},{56,16},{48,24},{8,32},{0,40},{24,48},{16,56},{41,1}... | collective-permute-start | bytes 294920 | tf_op jit(solution)/shard_map/ppermute | solution.py:426
  64.0 6.0 %collective-permute-start.17 = (f32[64,384]{1,0:T(8,128)S(1)}, f32[64,384]{1,0:T(8,128)S(1)}, u32[]{:S(2)}, u32[]{:S(2)}) collective-permute-start(f32[64,384]{1,0:T(8,128)S(1)} %add_pieces.8.refs_0_), channel_id=1, source_target_pairs={{56,0},{16,8},{8,16},{32,24},{24,32},{48,40},{40,48},{0,56},{57,1}... | collective-permute-start | bytes 294920 | tf_op jit(solution)/shard_map/ppermute | solution.py:426
  64.8 6.1 %collective-permute-start.18 = (f32[64,384]{1,0:T(8,128)S(1)}, f32[64,384]{1,0:T(8,128)S(1)}, u32[]{:S(2)}, u32[]{:S(2)}) collective-permute-start(f32[64,384]{1,0:T(8,128)S(1)} %add_pieces.8.refs_0_), channel_id=1, source_target_pairs={{16,0},{56,8},{32,16},{8,24},{48,32},{24,40},{0,48},{40,56},{17,1}... | collective-permute-start | bytes 294920 | tf_op jit(solution)/shard_map/ppermute | solution.py:426
  71.2 8.9 %collective-permute-start.19 = (f32[64,384]{1,0:T(8,128)S(1)}, f32[64,384]{1,0:T(8,128)S(1)}, u32[]{:S(2)}, u32[]{:S(2)}) collective-permute-start(f32[64,384]{1,0:T(8,128)S(1)} %apply_right.1.refs_0_), channel_id=1, source_target_pairs={{0,2},{2,4},{4,6},{6,0},{1,3},{3,5},{5,7},{7,1},{8,10},{10,12},{12... | collective-permute-start | bytes 294920 | tf_op jit(solution)/shard_map/ppermute | solution.py:421
  73.2 8.2 %collective-permute-start.20 = (f32[64,384]{1,0:T(8,128)S(1)}, f32[64,384]{1,0:T(8,128)S(1)}, u32[]{:S(2)}, u32[]{:S(2)}) collective-permute-start(f32[64,384]{1,0:T(8,128)S(1)} %apply_right.1.refs_0_), channel_id=1, source_target_pairs={{0,4},{2,6},{4,0},{6,2},{1,5},{3,7},{5,1},{7,3},{8,12},{10,14},{12... | collective-permute-start | bytes 294920 | tf_op jit(solution)/shard_map/ppermute | solution.py:421
  74.5 9.0 %collective-permute-start.21 = (f32[64,384]{1,0:T(8,128)S(1)}, f32[64,384]{1,0:T(8,128)S(1)}, u32[]{:S(2)}, u32[]{:S(2)}) collective-permute-start(f32[64,384]{1,0:T(8,128)S(1)} %apply_right.1.refs_0_), channel_id=1, source_target_pairs={{0,6},{2,0},{4,2},{6,4},{1,7},{3,1},{5,3},{7,5},{8,14},{10,8},{12,... | collective-permute-start | bytes 294920 | tf_op jit(solution)/shard_map/ppermute | solution.py:421
  75.7 9.2 %collective-permute-start.22 = (f32[64,384]{1,0:T(8,128)S(1)}, f32[64,384]{1,0:T(8,128)S(1)}, u32[]{:S(2)}, u32[]{:S(2)}) collective-permute-start(f32[64,384]{1,0:T(8,128)S(1)} %apply_right.1.refs_0_), channel_id=1, source_target_pairs={{0,1},{1,0},{2,3},{3,2},{4,5},{5,4},{6,7},{7,6},{8,9},{9,8},{10,11... | collective-permute-start | bytes 294920 | tf_op jit(solution)/shard_map/ppermute | solution.py:416
  80.1 4.8 %collective-permute-start.23 = (f32[64,384]{1,0:T(8,128)S(1)}, f32[64,384]{1,0:T(8,128)S(1)}, u32[]{:S(2)}, u32[]{:S(2)}) collective-permute-start(f32[64,384]{1,0:T(8,128)S(1)} %collective-permute-done.19.refs_1_), channel_id=1, source_target_pairs={{0,1},{1,0},{2,3},{3,2},{4,5},{5,4},{6,7},{7,6},{8,9},{9,8},{10,11... | collective-permute-start | bytes 294920 | tf_op jit(solution)/shard_map/ppermute | solution.py:416
  81.3 3.6 %collective-permute-start.24 = (f32[64,384]{1,0:T(8,128)S(1)}, f32[64,384]{1,0:T(8,128)S(1)}, u32[]{:S(2)}, u32[]{:S(2)}) collective-permute-start(f32[64,384]{1,0:T(8,128)S(1)} %collective-permute-done.20.refs_2_), channel_id=1, source_target_pairs={{0,1},{1,0},{2,3},{3,2},{4,5},{5,4},{6,7},{7,6},{8,9},{9,8},{10,11... | collective-permute-start | bytes 294920 | tf_op jit(solution)/shard_map/ppermute | solution.py:416
  83.5 1.6 %collective-permute-start.25 = (f32[64,384]{1,0:T(8,128)S(1)}, f32[64,384]{1,0:T(8,128)S(1)}, u32[]{:S(2)}, u32[]{:S(2)}) collective-permute-start(f32[64,384]{1,0:T(8,128)S(1)} %collective-permute-done.21.refs_3_), channel_id=1, source_target_pairs={{0,1},{1,0},{2,3},{3,2},{4,5},{5,4},{6,7},{7,6},{8,9},{9,8},{10,11... | collective-permute-start | bytes 294920 | tf_op jit(solution)/shard_map/ppermute | solution.py:416

commit v6 on v5

--- a/solution.py
+++ b/solution.py
@@ -24,7 +24,7 @@
 ORDER_FIRST = (0, 2, 3, 1)
 ORDER_LINE = (0, 1, 2, 3)
 ORDER_CROSS = (0, 2, 3, 1)
-ORDER_LAST = (0, 1, 2, 3)
+ORDER_LAST = (0, 2, 1, 3)
 VMEM_LIMIT = 24 * 1024 * 1024
 F32 = jnp.float32
 BF16 = jnp.bfloat16

time: 86.1 us -> 85.5 us (level)
  no operation moved by 1% of the time
where the time goes in v6:
time: 85.5 us; the launch traced here: 85.4 us
  starting transfers between devices  45.8 us (54%)
  waiting for transfers between devices  26 us (30%)
  Pallas kernels  12.8 us (15%)
  between operations  0.91 us (1%)
    ppermute x12, starting transfers between devices, rotate(): lax.ppermute(value, axis, [(i, (i + step) % size) for i in range(size)])  18.7 us
    ppermute x8, starting transfers between devices, along_z(): lax.ppermute(value, 'z', [(source, z) for z, source in enumerate(sources)])  14.3 us
    ppermute x12, waiting for transfers between devices, rotate(): lax.ppermute(value, axis, [(i, (i + step) % size) for i in range(size)])  14.3 us
    ppermute x6, starting transfers between devices, swap(): return lax.ppermute(value, 'core', [(0, 1), (1, 0)])  12.7 us
    ppermute x8, waiting for transfers between devices, along_z(): lax.ppermute(value, 'z', [(source, z) for z, source in enumerate(sources)])  11.5 us
    pallas_call x1, Pallas kernels, merge(): pl.pallas_call(merge_kernel, in_specs=[whole(pltpu.HBM)] * 5, out_specs=[...  4.62 us
    pallas_call x1, Pallas kernels, invert(): pl.pallas_call(invert_kernel, in_specs=[whole()] * 2, out_specs=[whole()]...  3.62 us
    pallas_call x4, Pallas kernels, product(): pl.pallas_call(functools.partial(product_kernel, own, steps), in_specs=[w...  2.21 us
  transfers between devices with their start and end apart: 26, of which 15 were waited for; matrix products, arithmetic and copies ran while one was open for 0% of the time, Pallas kernels for 7%

profile of v6, /device:TPU:1, one launch (start us, length us, event | category | flops | bytes accessed | tf_op | source)
XLA Modules:
  0.0 85.4 jit_solution(10068483907358064666)
XLA Ops:
  0.6 4.6 %merge_project.1 = (bf16[2,384,3072]{2,1,0:T(8,128)(2,1)S(1)}, f32[64,384]{1,0:T(8,128)S(1)}, s32[8,384]{1,0:T(8,128)S(1)}) custom-call(bf16[1,2,384,3072]{3,2,1,0:T(8,128)(2,1)} %gradient.1, bf16[1,2,384,3072]{3,2,1,0:T(8,128)(2,1)} %error.1, f32[2,32,3072]{2,1,0:T(8,128)} %bitcast.8, s32[32]{0:T(128)} %starts.1, s32[32]{0:T(128)} %owners.1), custom_call_target="tpu_custom_call" | custom-call | tf_op jit(solution)/shard_map/merge_project/pallas_call | solution.py:122
  5.3 3.7 %collective-permute-start = (f32[64,384]{1,0:T(8,128)S(1)}, f32[64,384]{1,0:T(8,128)S(1)}, u32[]{:S(2)}, u32[]{:S(2)}) collective-permute-start(f32[64,384]{1,0:T(8,128)S(1)} %get-tuple-element.18.refs_0_), channel_id=1, source_target_pairs={{0,128},{64,192},{128,0},{192,64},{1,129},{65,193},{129,1},{193,65... | collective-permute-start | bytes 294920 | tf_op jit(solution)/shard_map/ppermute | solution.py:421
  8.9 0.9 %collective-permute-start.1 = (f32[64,384]{1,0:T(8,128)S(1)}, f32[64,384]{1,0:T(8,128)S(1)}, u32[]{:S(2)}, u32[]{:S(2)}) collective-permute-start(f32[64,384]{1,0:T(8,128)S(1)} %get-tuple-element.18.refs_0_), channel_id=1, source_target_pairs={{0,192},{64,0},{128,64},{192,128},{1,193},{65,1},{129,65},{193,129... | collective-permute-start | bytes 294920 | tf_op jit(solution)/shard_map/ppermute | solution.py:421
  9.8 0.6 collective-permute-start.2
  10.4 0.5 collective-permute-done.refs_1_
  10.9 2.8 %collective-permute-done.1.refs_2_ = f32[64,384]{1,0:T(8,128)S(1)} collective-permute-done((f32[64,384]{1,0:T(8,128)S(1)}, f32[64,384]{1,0:T(8,128)S(1)}, u32[]{:S(2)}, u32[]{:S(2)}) %collective-permute-start.1) | collective-permute-done | bytes 98336 | tf_op jit(solution)/shard_map/ppermute | solution.py:421
  13.7 1.4 %collective-permute-done.2.refs_3_ = f32[64,384]{1,0:T(8,128)S(1)} collective-permute-done((f32[64,384]{1,0:T(8,128)S(1)}, f32[64,384]{1,0:T(8,128)S(1)}, u32[]{:S(2)}, u32[]{:S(2)}) %collective-permute-start.2) | collective-permute-done | bytes 98336 | tf_op jit(solution)/shard_map/ppermute | solution.py:421
  15.2 1.1 %collective-permute-start.3 = (f32[64,384]{1,0:T(8,128)S(1)}, f32[64,384]{1,0:T(8,128)S(1)}, u32[]{:S(2)}, u32[]{:S(2)}) collective-permute-start(f32[64,384]{1,0:T(8,128)S(1)} %add_pieces.5.refs_0_), channel_id=1, source_target_pairs={{8,0},{0,8},{24,16},{16,24},{40,32},{32,40},{56,48},{48,56},{9,1},... | collective-permute-start | bytes 294920 | tf_op jit(solution)/shard_map/ppermute | solution.py:426
  16.2 2.5 %collective-permute-done.3.refs_1_ = f32[64,384]{1,0:T(8,128)S(1)} collective-permute-done((f32[64,384]{1,0:T(8,128)S(1)}, f32[64,384]{1,0:T(8,128)S(1)}, u32[]{:S(2)}, u32[]{:S(2)}) %collective-permute-start.3) | collective-permute-done | bytes 98336 | tf_op jit(solution)/shard_map/ppermute | solution.py:426
  18.7 5.9 %collective-permute-start.4 = (f32[64,384]{1,0:T(8,128)S(1)}, f32[64,384]{1,0:T(8,128)S(1)}, u32[]{:S(2)}, u32[]{:S(2)}) collective-permute-start(f32[64,384]{1,0:T(8,128)S(1)} %add_pieces.6.refs_0_), channel_id=1, source_target_pairs={{40,0},{32,8},{56,16},{48,24},{8,32},{0,40},{24,48},{16,56},{41,1}... | collective-permute-start | bytes 294920 | tf_op jit(solution)/shard_map/ppermute | solution.py:426
  24.6 0.4 collective-permute-start.6
  25.0 1.7 %collective-permute-done.4.refs_1_ = f32[64,384]{1,0:T(8,128)S(1)} collective-permute-done((f32[64,384]{1,0:T(8,128)S(1)}, f32[64,384]{1,0:T(8,128)S(1)}, u32[]{:S(2)}, u32[]{:S(2)}) %collective-permute-start.4) | collective-permute-done | bytes 98336 | tf_op jit(solution)/shard_map/ppermute | solution.py:426
  26.7 2.9 %collective-permute-done.5.refs_2_ = f32[64,384]{1,0:T(8,128)S(1)} collective-permute-done((f32[64,384]{1,0:T(8,128)S(1)}, f32[64,384]{1,0:T(8,128)S(1)}, u32[]{:S(2)}, u32[]{:S(2)}) %collective-permute-start.5) | collective-permute-done | bytes 98336 | tf_op jit(solution)/shard_map/ppermute | solution.py:426
  29.6 1.4 %collective-permute-done.6.refs_3_ = f32[64,384]{1,0:T(8,128)S(1)} collective-permute-done((f32[64,384]{1,0:T(8,128)S(1)}, f32[64,384]{1,0:T(8,128)S(1)}, u32[]{:S(2)}, u32[]{:S(2)}) %collective-permute-start.6) | collective-permute-done | bytes 98336 | tf_op jit(solution)/shard_map/ppermute | solution.py:426
  31.0 0.3 split_factor.1
  31.3 0.6 product_other_half.3
  31.9 4.7 %collective-permute-start.8 = (f32[2,88,384]{2,1,0:T(8,128)S(1)}, f32[2,88,384]{2,1,0:T(8,128)S(1)}, u32[]{:S(2)}, u32[]{:S(2)}) collective-permute-start(f32[2,88,384]{2,1,0:T(8,128)S(1)} %product_other_half.3), channel_id=1, source_target_pairs={{0,1},{1,0},{2,3},{3,2},{4,5},{5,4},{6,7},{7,6},{8,9},{9,8},{10,11... | collective-permute-start | bytes 811016 | tf_op jit(solution)/shard_map/ppermute | solution.py:416
  36.6 0.5 product_other_half.2
  37.2 0.5 product_own_half.3.mine
  37.7 0.6 product_own_half.2.mine
  38.4 3.0 %collective-permute-start.10 = (f32[88,384]{1,0:T(8,128)S(1)}, f32[88,384]{1,0:T(8,128)S(1)}, u32[]{:S(2)}, u32[]{:S(2)}) collective-permute-start(f32[88,384]{1,0:T(8,128)S(1)} %get-tuple-element.24), channel_id=1, source_target_pairs={{0,4},{2,6},{4,0},{6,2},{1,5},{3,7},{5,1},{7,3},{8,12},{10,14},{12... | collective-permute-start | bytes 405512 | tf_op jit(solution)/shard_map/ppermute | solution.py:421
  41.4 0.4 collective-permute-start.9
  41.8 2.3 %collective-permute-start.11 = (f32[88,384]{1,0:T(8,128)S(1)}, f32[88,384]{1,0:T(8,128)S(1)}, u32[]{:S(2)}, u32[]{:S(2)}) collective-permute-start(f32[88,384]{1,0:T(8,128)S(1)} %get-tuple-element.25), channel_id=1, source_target_pairs={{0,6},{2,0},{4,2},{6,4},{1,7},{3,1},{5,3},{7,5},{8,14},{10,8},{12,... | collective-permute-start | bytes 405512 | tf_op jit(solution)/shard_map/ppermute | solution.py:421
  44.2 0.5 collective-permute-done.10.c
  44.6 3.5 %collective-permute-done.9.b = f32[88,384]{1,0:T(8,128)S(1)} collective-permute-done((f32[88,384]{1,0:T(8,128)S(1)}, f32[88,384]{1,0:T(8,128)S(1)}, u32[]{:S(2)}, u32[]{:S(2)}) %collective-permute-start.9) | collective-permute-done | bytes 135200 | tf_op jit(solution)/shard_map/ppermute | solution.py:421
  48.2 2.0 %collective-permute-start.12 = (f32[80,384]{1,0:T(8,128)S(1)}, f32[80,384]{1,0:T(8,128)S(1)}, u32[]{:S(2)}, u32[]{:S(2)}) collective-permute-start(f32[80,384]{1,0:T(8,128)S(1)} %get-tuple-element.27.refs_0_), channel_id=1, source_target_pairs={{0,128},{64,192},{128,0},{192,64},{1,129},{65,193},{129,1},{193,65... | collective-permute-start | bytes 368648 | tf_op jit(solution)/shard_map/ppermute | solution.py:421
  50.2 1.0 %collective-permute-start.13 = (f32[80,384]{1,0:T(8,128)S(1)}, f32[80,384]{1,0:T(8,128)S(1)}, u32[]{:S(2)}, u32[]{:S(2)}) collective-permute-start(f32[80,384]{1,0:T(8,128)S(1)} %get-tuple-element.27.refs_0_), channel_id=1, source_target_pairs={{0,192},{64,0},{128,64},{192,128},{1,193},{65,1},{129,65},{193,129... | collective-permute-start | bytes 368648 | tf_op jit(solution)/shard_map/ppermute | solution.py:421
  51.2 0.5 collective-permute-start.14
  51.7 2.0 %collective-permute-done.12.refs_1_ = f32[80,384]{1,0:T(8,128)S(1)} collective-permute-done((f32[80,384]{1,0:T(8,128)S(1)}, f32[80,384]{1,0:T(8,128)S(1)}, u32[]{:S(2)}, u32[]{:S(2)}) %collective-permute-start.12) | collective-permute-done | bytes 122912 | tf_op jit(solution)/shard_map/ppermute | solution.py:421
  53.7 1.6 %collective-permute-done.13.refs_2_ = f32[80,384]{1,0:T(8,128)S(1)} collective-permute-done((f32[80,384]{1,0:T(8,128)S(1)}, f32[80,384]{1,0:T(8,128)S(1)}, u32[]{:S(2)}, u32[]{:S(2)}) %collective-permute-start.13) | collective-permute-done | bytes 122912 | tf_op jit(solution)/shard_map/ppermute | solution.py:421
  55.3 2.0 %collective-permute-done.14.refs_3_ = f32[80,384]{1,0:T(8,128)S(1)} collective-permute-done((f32[80,384]{1,0:T(8,128)S(1)}, f32[80,384]{1,0:T(8,128)S(1)}, u32[]{:S(2)}, u32[]{:S(2)}) %collective-permute-start.14) | collective-permute-done | bytes 122912 | tf_op jit(solution)/shard_map/ppermute | solution.py:421
  57.3 2.2 %collective-permute-start.15 = (f32[64,384]{1,0:T(8,128)S(1)}, f32[64,384]{1,0:T(8,128)S(1)}, u32[]{:S(2)}, u32[]{:S(2)}) collective-permute-start(f32[64,384]{1,0:T(8,128)S(1)} %get-tuple-element.30.refs_0_), channel_id=1, source_target_pairs={{8,0},{0,8},{24,16},{16,24},{40,32},{32,40},{56,48},{48,56},{9,1},... | collective-permute-start | bytes 294920 | tf_op jit(solution)/shard_map/ppermute | solution.py:426
  59.5 2.0 %collective-permute-done.15.refs_1_ = f32[64,384]{1,0:T(8,128)S(1)} collective-permute-done((f32[64,384]{1,0:T(8,128)S(1)}, f32[64,384]{1,0:T(8,128)S(1)}, u32[]{:S(2)}, u32[]{:S(2)}) %collective-permute-start.15) | collective-permute-done | bytes 98336 | tf_op jit(solution)/shard_map/ppermute | solution.py:426
  61.5 2.4 %collective-permute-start.16 = (f32[64,384]{1,0:T(8,128)S(1)}, f32[64,384]{1,0:T(8,128)S(1)}, u32[]{:S(2)}, u32[]{:S(2)}) collective-permute-start(f32[64,384]{1,0:T(8,128)S(1)} %add_pieces.8.refs_0_), channel_id=1, source_target_pairs={{40,0},{32,8},{56,16},{48,24},{8,32},{0,40},{24,48},{16,56},{41,1}... | collective-permute-start | bytes 294920 | tf_op jit(solution)/shard_map/ppermute | solution.py:426
  64.0 0.9 %collective-permute-start.17 = (f32[64,384]{1,0:T(8,128)S(1)}, f32[64,384]{1,0:T(8,128)S(1)}, u32[]{:S(2)}, u32[]{:S(2)}) collective-permute-start(f32[64,384]{1,0:T(8,128)S(1)} %add_pieces.8.refs_0_), channel_id=1, source_target_pairs={{56,0},{16,8},{8,16},{32,24},{24,32},{48,40},{40,48},{0,56},{57,1}... | collective-permute-start | bytes 294920 | tf_op jit(solution)/shard_map/ppermute | solution.py:426
  64.8 1.5 %collective-permute-start.18 = (f32[64,384]{1,0:T(8,128)S(1)}, f32[64,384]{1,0:T(8,128)S(1)}, u32[]{:S(2)}, u32[]{:S(2)}) collective-permute-start(f32[64,384]{1,0:T(8,128)S(1)} %add_pieces.8.refs_0_), channel_id=1, source_target_pairs={{16,0},{56,8},{32,16},{8,24},{48,32},{24,40},{0,48},{40,56},{17,1}... | collective-permute-start | bytes 294920 | tf_op jit(solution)/shard_map/ppermute | solution.py:426
  66.4 3.6 %invert_triangle.1 = (f32[64,128]{1,0:T(8,128)S(1)}, f32[64,384]{1,0:T(8,128)}) custom-call(f32[8,384]{1,0:T(8,128)S(1)} %get-tuple-element.26.rest, f32[64,384]{1,0:T(8,128)S(1)} %get-tuple-element.28.rows), custom_call_target="tpu_custom_call" | custom-call | flops 2000000 | bytes 20000000 | tf_op jit(solution)/shard_map/invert_triangle/pallas_call | solution.py:357
  70.0 1.0 %collective-permute-done.18.refs_3_ = f32[64,384]{1,0:T(8,128)S(1)} collective-permute-done((f32[64,384]{1,0:T(8,128)S(1)}, f32[64,384]{1,0:T(8,128)S(1)}, u32[]{:S(2)}, u32[]{:S(2)}) %collective-permute-start.18) | collective-permute-done | bytes 98336 | tf_op jit(solution)/shard_map/ppermute | solution.py:426
  71.0 0.2 apply_right.1.refs_0_
  71.2 1.2 %collective-permute-start.19 = (f32[64,384]{1,0:T(8,128)S(1)}, f32[64,384]{1,0:T(8,128)S(1)}, u32[]{:S(2)}, u32[]{:S(2)}) collective-permute-start(f32[64,384]{1,0:T(8,128)S(1)} %apply_right.1.refs_0_), channel_id=1, source_target_pairs={{0,4},{2,6},{4,0},{6,2},{1,5},{3,7},{5,1},{7,3},{8,12},{10,14},{12... | collective-permute-start | bytes 294920 | tf_op jit(solution)/shard_map/ppermute | solution.py:421
  72.5 1.4 %collective-permute-start.20 = (f32[64,384]{1,0:T(8,128)S(1)}, f32[64,384]{1,0:T(8,128)S(1)}, u32[]{:S(2)}, u32[]{:S(2)}) collective-permute-start(f32[64,384]{1,0:T(8,128)S(1)} %apply_right.1.refs_0_), channel_id=1, source_target_pairs={{0,2},{2,4},{4,6},{6,0},{1,3},{3,5},{5,7},{7,1},{8,10},{10,12},{12... | collective-permute-start | bytes 294920 | tf_op jit(solution)/shard_map/ppermute | solution.py:421
  73.9 1.7 %collective-permute-start.21 = (f32[64,384]{1,0:T(8,128)S(1)}, f32[64,384]{1,0:T(8,128)S(1)}, u32[]{:S(2)}, u32[]{:S(2)}) collective-permute-start(f32[64,384]{1,0:T(8,128)S(1)} %apply_right.1.refs_0_), channel_id=1, source_target_pairs={{0,6},{2,0},{4,2},{6,4},{1,7},{3,1},{5,3},{7,5},{8,14},{10,8},{12,... | collective-permute-start | bytes 294920 | tf_op jit(solution)/shard_map/ppermute | solution.py:421
  75.6 4.9 %collective-permute-start.22 = (f32[64,384]{1,0:T(8,128)S(1)}, f32[64,384]{1,0:T(8,128)S(1)}, u32[]{:S(2)}, u32[]{:S(2)}) collective-permute-start(f32[64,384]{1,0:T(8,128)S(1)} %apply_right.1.refs_0_), channel_id=1, source_target_pairs={{0,1},{1,0},{2,3},{3,2},{4,5},{5,4},{6,7},{7,6},{8,9},{9,8},{10,11... | collective-permute-start | bytes 294920 | tf_op jit(solution)/shard_map/ppermute | solution.py:416
  80.5 1.1 %collective-permute-start.23 = (f32[64,384]{1,0:T(8,128)S(1)}, f32[64,384]{1,0:T(8,128)S(1)}, u32[]{:S(2)}, u32[]{:S(2)}) collective-permute-start(f32[64,384]{1,0:T(8,128)S(1)} %collective-permute-done.19.refs_1_), channel_id=1, source_target_pairs={{0,1},{1,0},{2,3},{3,2},{4,5},{5,4},{6,7},{7,6},{8,9},{9,8},{10,11... | collective-permute-start | bytes 294920 | tf_op jit(solution)/shard_map/ppermute | solution.py:416
  81.6 1.5 %collective-permute-start.24 = (f32[64,384]{1,0:T(8,128)S(1)}, f32[64,384]{1,0:T(8,128)S(1)}, u32[]{:S(2)}, u32[]{:S(2)}) collective-permute-start(f32[64,384]{1,0:T(8,128)S(1)} %collective-permute-done.20.refs_2_), channel_id=1, source_target_pairs={{0,1},{1,0},{2,3},{3,2},{4,5},{5,4},{6,7},{7,6},{8,9},{9,8},{10,11... | collective-permute-start | bytes 294920 | tf_op jit(solution)/shard_map/ppermute | solution.py:416
  83.1 0.4 collective-permute-start.25
  83.5 0.8 assemble_own_half.1.refs_0_
  84.5 0.8 assemble_other_half.1
  (23 shorter events, 0.5 us)
Async XLA Ops:
  5.3 5.7 %collective-permute-start = (f32[64,384]{1,0:T(8,128)S(1)}, f32[64,384]{1,0:T(8,128)S(1)}, u32[]{:S(2)}, u32[]{:S(2)}) collective-permute-start(f32[64,384]{1,0:T(8,128)S(1)} %get-tuple-element.18.refs_0_), channel_id=1, source_target_pairs={{0,128},{64,192},{128,0},{192,64},{1,129},{65,193},{129,1},{193,65... | collective-permute-start | bytes 294920 | tf_op jit(solution)/shard_map/ppermute | solution.py:421
  8.9 4.8 %collective-permute-start.1 = (f32[64,384]{1,0:T(8,128)S(1)}, f32[64,384]{1,0:T(8,128)S(1)}, u32[]{:S(2)}, u32[]{:S(2)}) collective-permute-start(f32[64,384]{1,0:T(8,128)S(1)} %get-tuple-element.18.refs_0_), channel_id=1, source_target_pairs={{0,192},{64,0},{128,64},{192,128},{1,193},{65,1},{129,65},{193,129... | collective-permute-start | bytes 294920 | tf_op jit(solution)/shard_map/ppermute | solution.py:421
  9.8 5.3 %collective-permute-start.2 = (f32[64,384]{1,0:T(8,128)S(1)}, f32[64,384]{1,0:T(8,128)S(1)}, u32[]{:S(2)}, u32[]{:S(2)}) collective-permute-start(f32[64,384]{1,0:T(8,128)S(1)} %get-tuple-element.18.refs_0_), channel_id=1, source_target_pairs={{0,64},{64,128},{128,192},{192,0},{1,65},{65,129},{129,193},{193,1... | collective-permute-start | bytes 294920 | tf_op jit(solution)/shard_map/ppermute | solution.py:421
  15.2 3.6 %collective-permute-start.3 = (f32[64,384]{1,0:T(8,128)S(1)}, f32[64,384]{1,0:T(8,128)S(1)}, u32[]{:S(2)}, u32[]{:S(2)}) collective-permute-start(f32[64,384]{1,0:T(8,128)S(1)} %add_pieces.5.refs_0_), channel_id=1, source_target_pairs={{8,0},{0,8},{24,16},{16,24},{40,32},{32,40},{56,48},{48,56},{9,1},... | collective-permute-start | bytes 294920 | tf_op jit(solution)/shard_map/ppermute | solution.py:426
  18.7 8.0 %collective-permute-start.4 = (f32[64,384]{1,0:T(8,128)S(1)}, f32[64,384]{1,0:T(8,128)S(1)}, u32[]{:S(2)}, u32[]{:S(2)}) collective-permute-start(f32[64,384]{1,0:T(8,128)S(1)} %add_pieces.6.refs_0_), channel_id=1, source_target_pairs={{40,0},{32,8},{56,16},{48,24},{8,32},{0,40},{24,48},{16,56},{41,1}... | collective-permute-start | bytes 294920 | tf_op jit(solution)/shard_map/ppermute | solution.py:426
  24.6 5.0 %collective-permute-start.5 = (f32[64,384]{1,0:T(8,128)S(1)}, f32[64,384]{1,0:T(8,128)S(1)}, u32[]{:S(2)}, u32[]{:S(2)}) collective-permute-start(f32[64,384]{1,0:T(8,128)S(1)} %add_pieces.6.refs_0_), channel_id=1, source_target_pairs={{56,0},{16,8},{8,16},{32,24},{24,32},{48,40},{40,48},{0,56},{57,1}... | collective-permute-start | bytes 294920 | tf_op jit(solution)/shard_map/ppermute | solution.py:426
  24.6 6.4 %collective-permute-start.6 = (f32[64,384]{1,0:T(8,128)S(1)}, f32[64,384]{1,0:T(8,128)S(1)}, u32[]{:S(2)}, u32[]{:S(2)}) collective-permute-start(f32[64,384]{1,0:T(8,128)S(1)} %add_pieces.6.refs_0_), channel_id=1, source_target_pairs={{16,0},{56,8},{32,16},{8,24},{48,32},{24,40},{0,48},{40,56},{17,1}... | collective-permute-start | bytes 294920 | tf_op jit(solution)/shard_map/ppermute | solution.py:426
  31.9 6.4 %collective-permute-start.8 = (f32[2,88,384]{2,1,0:T(8,128)S(1)}, f32[2,88,384]{2,1,0:T(8,128)S(1)}, u32[]{:S(2)}, u32[]{:S(2)}) collective-permute-start(f32[2,88,384]{2,1,0:T(8,128)S(1)} %product_other_half.3), channel_id=1, source_target_pairs={{0,1},{1,0},{2,3},{3,2},{4,5},{5,4},{6,7},{7,6},{8,9},{9,8},{10,11... | collective-permute-start | bytes 811016 | tf_op jit(solution)/shard_map/ppermute | solution.py:416
  37.1 4.6 %collective-permute-start.7 = (f32[2,88,384]{2,1,0:T(8,128)S(1)}, f32[2,88,384]{2,1,0:T(8,128)S(1)}, u32[]{:S(2)}, u32[]{:S(2)}) collective-permute-start(f32[2,88,384]{2,1,0:T(8,128)S(1)} %product_other_half.2), channel_id=1, source_target_pairs={{0,1},{1,0},{2,3},{3,2},{4,5},{5,4},{6,7},{7,6},{8,9},{9,8},{10,11... | collective-permute-start | bytes 811016 | tf_op jit(solution)/shard_map/ppermute | solution.py:416
  38.4 6.3 %collective-permute-start.10 = (f32[88,384]{1,0:T(8,128)S(1)}, f32[88,384]{1,0:T(8,128)S(1)}, u32[]{:S(2)}, u32[]{:S(2)}) collective-permute-start(f32[88,384]{1,0:T(8,128)S(1)} %get-tuple-element.24), channel_id=1, source_target_pairs={{0,4},{2,6},{4,0},{6,2},{1,5},{3,7},{5,1},{7,3},{8,12},{10,14},{12... | collective-permute-start | bytes 405512 | tf_op jit(solution)/shard_map/ppermute | solution.py:421
  41.4 6.8 %collective-permute-start.9 = (f32[88,384]{1,0:T(8,128)S(1)}, f32[88,384]{1,0:T(8,128)S(1)}, u32[]{:S(2)}, u32[]{:S(2)}) collective-permute-start(f32[88,384]{1,0:T(8,128)S(1)} %get-tuple-element.23), channel_id=1, source_target_pairs={{0,2},{2,4},{4,6},{6,0},{1,3},{3,5},{5,7},{7,1},{8,10},{10,12},{12... | collective-permute-start | bytes 405512 | tf_op jit(solution)/shard_map/ppermute | solution.py:421
  41.8 6.3 %collective-permute-start.11 = (f32[88,384]{1,0:T(8,128)S(1)}, f32[88,384]{1,0:T(8,128)S(1)}, u32[]{:S(2)}, u32[]{:S(2)}) collective-permute-start(f32[88,384]{1,0:T(8,128)S(1)} %get-tuple-element.25), channel_id=1, source_target_pairs={{0,6},{2,0},{4,2},{6,4},{1,7},{3,1},{5,3},{7,5},{8,14},{10,8},{12,... | collective-permute-start | bytes 405512 | tf_op jit(solution)/shard_map/ppermute | solution.py:421
  48.2 5.5 %collective-permute-start.12 = (f32[80,384]{1,0:T(8,128)S(1)}, f32[80,384]{1,0:T(8,128)S(1)}, u32[]{:S(2)}, u32[]{:S(2)}) collective-permute-start(f32[80,384]{1,0:T(8,128)S(1)} %get-tuple-element.27.refs_0_), channel_id=1, source_target_pairs={{0,128},{64,192},{128,0},{192,64},{1,129},{65,193},{129,1},{193,65... | collective-permute-start | bytes 368648 | tf_op jit(solution)/shard_map/ppermute | solution.py:421
  50.2 5.1 %collective-permute-start.13 = (f32[80,384]{1,0:T(8,128)S(1)}, f32[80,384]{1,0:T(8,128)S(1)}, u32[]{:S(2)}, u32[]{:S(2)}) collective-permute-start(f32[80,384]{1,0:T(8,128)S(1)} %get-tuple-element.27.refs_0_), channel_id=1, source_target_pairs={{0,192},{64,0},{128,64},{192,128},{1,193},{65,1},{129,65},{193,129... | collective-permute-start | bytes 368648 | tf_op jit(solution)/shard_map/ppermute | solution.py:421
  51.2 6.1 %collective-permute-start.14 = (f32[80,384]{1,0:T(8,128)S(1)}, f32[80,384]{1,0:T(8,128)S(1)}, u32[]{:S(2)}, u32[]{:S(2)}) collective-permute-start(f32[80,384]{1,0:T(8,128)S(1)} %get-tuple-element.27.refs_0_), channel_id=1, source_target_pairs={{0,64},{64,128},{128,192},{192,0},{1,65},{65,129},{129,193},{193,1... | collective-permute-start | bytes 368648 | tf_op jit(solution)/shard_map/ppermute | solution.py:421
  57.3 4.2 %collective-permute-start.15 = (f32[64,384]{1,0:T(8,128)S(1)}, f32[64,384]{1,0:T(8,128)S(1)}, u32[]{:S(2)}, u32[]{:S(2)}) collective-permute-start(f32[64,384]{1,0:T(8,128)S(1)} %get-tuple-element.30.refs_0_), channel_id=1, source_target_pairs={{8,0},{0,8},{24,16},{16,24},{40,32},{32,40},{56,48},{48,56},{9,1},... | collective-permute-start | bytes 294920 | tf_op jit(solution)/shard_map/ppermute | solution.py:426
  61.5 8.5 %collective-permute-start.16 = (f32[64,384]{1,0:T(8,128)S(1)}, f32[64,384]{1,0:T(8,128)S(1)}, u32[]{:S(2)}, u32[]{:S(2)}) collective-permute-start(f32[64,384]{1,0:T(8,128)S(1)} %add_pieces.8.refs_0_), channel_id=1, source_target_pairs={{40,0},{32,8},{56,16},{48,24},{8,32},{0,40},{24,48},{16,56},{41,1}... | collective-permute-start | bytes 294920 | tf_op jit(solution)/shard_map/ppermute | solution.py:426
  64.0 6.0 %collective-permute-start.17 = (f32[64,384]{1,0:T(8,128)S(1)}, f32[64,384]{1,0:T(8,128)S(1)}, u32[]{:S(2)}, u32[]{:S(2)}) collective-permute-start(f32[64,384]{1,0:T(8,128)S(1)} %add_pieces.8.refs_0_), channel_id=1, source_target_pairs={{56,0},{16,8},{8,16},{32,24},{24,32},{48,40},{40,48},{0,56},{57,1}... | collective-permute-start | bytes 294920 | tf_op jit(solution)/shard_map/ppermute | solution.py:426
  64.8 6.1 %collective-permute-start.18 = (f32[64,384]{1,0:T(8,128)S(1)}, f32[64,384]{1,0:T(8,128)S(1)}, u32[]{:S(2)}, u32[]{:S(2)}) collective-permute-start(f32[64,384]{1,0:T(8,128)S(1)} %add_pieces.8.refs_0_), channel_id=1, source_target_pairs={{16,0},{56,8},{32,16},{8,24},{48,32},{24,40},{0,48},{40,56},{17,1}... | collective-permute-start | bytes 294920 | tf_op jit(solution)/shard_map/ppermute | solution.py:426
  71.2 9.3 %collective-permute-start.19 = (f32[64,384]{1,0:T(8,128)S(1)}, f32[64,384]{1,0:T(8,128)S(1)}, u32[]{:S(2)}, u32[]{:S(2)}) collective-permute-start(f32[64,384]{1,0:T(8,128)S(1)} %apply_right.1.refs_0_), channel_id=1, source_target_pairs={{0,4},{2,6},{4,0},{6,2},{1,5},{3,7},{5,1},{7,3},{8,12},{10,14},{12... | collective-permute-start | bytes 294920 | tf_op jit(solution)/shard_map/ppermute | solution.py:421
  72.5 9.2 %collective-permute-start.20 = (f32[64,384]{1,0:T(8,128)S(1)}, f32[64,384]{1,0:T(8,128)S(1)}, u32[]{:S(2)}, u32[]{:S(2)}) collective-permute-start(f32[64,384]{1,0:T(8,128)S(1)} %apply_right.1.refs_0_), channel_id=1, source_target_pairs={{0,2},{2,4},{4,6},{6,0},{1,3},{3,5},{5,7},{7,1},{8,10},{10,12},{12... | collective-permute-start | bytes 294920 | tf_op jit(solution)/shard_map/ppermute | solution.py:421
  73.9 9.2 %collective-permute-start.21 = (f32[64,384]{1,0:T(8,128)S(1)}, f32[64,384]{1,0:T(8,128)S(1)}, u32[]{:S(2)}, u32[]{:S(2)}) collective-permute-start(f32[64,384]{1,0:T(8,128)S(1)} %apply_right.1.refs_0_), channel_id=1, source_target_pairs={{0,6},{2,0},{4,2},{6,4},{1,7},{3,1},{5,3},{7,5},{8,14},{10,8},{12,... | collective-permute-start | bytes 294920 | tf_op jit(solution)/shard_map/ppermute | solution.py:421
  75.6 8.7 %collective-permute-start.22 = (f32[64,384]{1,0:T(8,128)S(1)}, f32[64,384]{1,0:T(8,128)S(1)}, u32[]{:S(2)}, u32[]{:S(2)}) collective-permute-start(f32[64,384]{1,0:T(8,128)S(1)} %apply_right.1.refs_0_), channel_id=1, source_target_pairs={{0,1},{1,0},{2,3},{3,2},{4,5},{5,4},{6,7},{7,6},{8,9},{9,8},{10,11... | collective-permute-start | bytes 294920 | tf_op jit(solution)/shard_map/ppermute | solution.py:416
  80.5 3.8 %collective-permute-start.23 = (f32[64,384]{1,0:T(8,128)S(1)}, f32[64,384]{1,0:T(8,128)S(1)}, u32[]{:S(2)}, u32[]{:S(2)}) collective-permute-start(f32[64,384]{1,0:T(8,128)S(1)} %collective-permute-done.19.refs_1_), channel_id=1, source_target_pairs={{0,1},{1,0},{2,3},{3,2},{4,5},{5,4},{6,7},{7,6},{8,9},{9,8},{10,11... | collective-permute-start | bytes 294920 | tf_op jit(solution)/shard_map/ppermute | solution.py:416
  81.6 2.7 %collective-permute-start.24 = (f32[64,384]{1,0:T(8,128)S(1)}, f32[64,384]{1,0:T(8,128)S(1)}, u32[]{:S(2)}, u32[]{:S(2)}) collective-permute-start(f32[64,384]{1,0:T(8,128)S(1)} %collective-permute-done.20.refs_2_), channel_id=1, source_target_pairs={{0,1},{1,0},{2,3},{3,2},{4,5},{5,4},{6,7},{7,6},{8,9},{9,8},{10,11... | collective-permute-start | bytes 294920 | tf_op jit(solution)/shard_map/ppermute | solution.py:416
  83.1 1.4 %collective-permute-start.25 = (f32[64,384]{1,0:T(8,128)S(1)}, f32[64,384]{1,0:T(8,128)S(1)}, u32[]{:S(2)}, u32[]{:S(2)}) collective-permute-start(f32[64,384]{1,0:T(8,128)S(1)} %collective-permute-done.21.refs_3_), channel_id=1, source_target_pairs={{0,1},{1,0},{2,3},{3,2},{4,5},{5,4},{6,7},{7,6},{8,9},{9,8},{10,11... | collective-permute-start | bytes 294920 | tf_op jit(solution)/shard_map/ppermute | solution.py:416
